TPU v7x, 32 devices: a whole 2x2x4 slice. The times are simulated.
32 devices in a mesh: mol: 2 (over x), tile: 8 (over z, y), rep: 2 (over core).
Axes of the slice: x: 2, y: 2, z: 4, core: 2. Of those that a mesh axis runs over, the one named last changes fastest.
Arguments:
- tasks: int32 [2, 8192], P(None, ('mol', 'tile')), parts along dimension 1, may hold values from 0 to 7, as said below
- task_count: int32 [16], P(('mol', 'tile')), parts along dimension 0, may hold values from 64 to 512, as said below
- integrals: float32 [8192, 4096], P(('mol', 'tile')), parts along dimension 0, may hold values from -0.1875 to 0.1875
- amplitudes: float32 [400, 64, 768], P(('mol', 'tile'), None, 'rep'), parts along dimension 0, may hold values from -6 to 6
- amp_slot: int32 [400], P('mol'), parts along dimension 0, may hold values from 0 to 199, as said below
- need_amp: int32 [128], P(('mol', 'tile')), parts along dimension 0, may hold values from 0 to 199, as said below
- res_slot: int32 [400], P('mol'), parts along dimension 0, may hold values from 0 to 199, as said below
- needed_residual_tiles: int32 [128], P(('mol', 'tile')), parts along dimension 0, may hold values from 0 to 199, as said below
- pair_energy: float32 [1536], P(('mol', 'rep')), parts along dimension 0, may hold values from -3 to -1
- virt_energy: float32 [3200], P('mol'), parts along dimension 0, may hold values from 0.2 to 3
- window_energy: float32 [16], P('mol'), parts along dimension 0, may hold values from 0.2 to 3
Outputs:
- new_amplitudes: float32 [400, 64, 768], P(('mol', 'tile'), None, 'rep'), parts along dimension 0
There are 2 independent parts, one for each index of `mol`. A program takes and returns all parts, laid end to end along the dimension named above; each array names one. Nothing has to cross between parts.
Inputs may be any that keep to these rules, and one draw needn't show every extreme that they name: `tasks`: column k describes slot k % 512 of tile device k // 512; positions index that device's lists. `task_count`: some devices have all 512 slots live and some only 64. `amp_slot`: A permutation; slot s is stored on tile device s // 25 at position s % 25. `need_amp`: entries 8 t to 8 (t + 1) - 1 are tile device t's list: exactly 2 distinct tiles stored on each of 4 distinct owners, none on the others. `res_slot`: A permutation; slot s is owned by tile device s // 25 at position s % 25. `needed_residual_tiles`: entries 8 t to 8 (t + 1) - 1 are tile device t's list: exactly 2 distinct tiles owned by each of 4 distinct owners, none by the others.
All inputs are finite; a program needn't handle non-finite values.
Results may differ from a plain program's by a relative error of at most 0.0003.
Values sent between devices are 32-bit elements; how exact they have to be, the bound alone decides.
No kernel may reach another device: no remote copies, remote signals or barrier semaphores. Data moves between devices by JAX's collectives and lax.ppermute only.
A program may use at most 128 MiB of HBM per device.

v0:
```python
import jax
import jax.numpy as jnp
from jax import lax
from jax.sharding import PartitionSpec as P

TW = 64
CAP = 2
TBLK = 64


def lookup(table_values, wanted_ids):
    matches = wanted_ids[:, None] == jnp.arange(table_values.shape[0], dtype=jnp.int32)[None, :]
    return jnp.sum(jnp.where(matches, table_values[None, :], 0), axis=1)


def routing(tile_ids, slot_map, per_owner, owners, capacity):
    slot_ids = lookup(slot_map, tile_ids)
    owner_of = slot_ids // per_owner
    local_slot = slot_ids % per_owner
    sequence = jnp.arange(tile_ids.shape[0], dtype=jnp.int32)
    earlier = (owner_of[:, None] == owner_of[None, :]) & (sequence[:, None] > sequence[None, :])
    position = jnp.sum(earlier, axis=1)
    flat_slot = owner_of * capacity + position
    placed = flat_slot[:, None] == jnp.arange(owners * capacity, dtype=jnp.int32)[None, :]
    wanted = jnp.sum(jnp.where(placed, local_slot[:, None] + 1, 0), axis=0) - 1
    return (flat_slot, placed, wanted.reshape(owners, capacity))


def accumulate(task_rows, integral_rows, lower, upper, amp_table, list_slots, usable, start_totals):
    tile_width = amp_table.shape[1]

    def contract(block_index, totals):
        offset = block_index * TBLK
        picked = lax.dynamic_slice_in_dim(task_rows, offset, TBLK, 1)
        operator_matrices = lax.dynamic_slice_in_dim(integral_rows, offset, TBLK, 0).reshape(
            TBLK, tile_width, tile_width
        )
        input_factor = amp_table[picked[1]]
        contracted_output = jnp.einsum(
            "fzo,fou->fzu", operator_matrices, input_factor, precision=lax.Precision.HIGHEST
        )
        spots = offset + jnp.arange(TBLK, dtype=jnp.int32)
        is_live = (spots >= lower) & (spots < upper) & usable[picked[1]]
        selection_mask = (
            (picked[0][:, None] == jnp.arange(list_slots, dtype=jnp.int32)[None, :])
            & is_live[:, None]
        ).astype(jnp.float32)
        return totals + jnp.einsum(
            "tg,tar->gar", selection_mask, contracted_output, precision=lax.Precision.HIGHEST
        )

    return lax.fori_loop(lower // TBLK, (upper + TBLK - 1) // TBLK, contract, start_totals)


def serve_from(amplitudes, asked_for):
    clipped = jnp.maximum(asked_for, 0)
    tile_data = amplitudes[clipped]
    return jnp.where((asked_for >= 0)[:, :, None, None], tile_data, jnp.zeros_like(tile_data))


def local(
    tasks,
    task_count,
    integrals,
    amplitudes,
    amp_slot,
    need_amp,
    res_slot,
    needed_residual_tiles,
    pair_energy,
    virt_energy,
    window_energy,
):
    owners = lax.axis_size("tile")
    own_index = lax.axis_index("tile")
    amp_dev = amplitudes.shape[0]
    row_count = amplitudes.shape[2]
    res_dev = res_slot.shape[0] // owners
    list_slots = needed_residual_tiles.shape[0]
    live_count = task_count[0]
    start_totals = jnp.zeros((list_slots, TW, row_count), jnp.float32)
    flat_amp, placed_amp, wanted = routing(need_amp, amp_slot, amp_dev, owners, CAP)
    fetched = lax.all_to_all(
        serve_from(
            amplitudes, lax.all_to_all(wanted, "tile", split_axis=0, concat_axis=0, tiled=True)
        ),
        "tile",
        split_axis=0,
        concat_axis=0,
        tiled=True,
    )
    amp_table = fetched.reshape(owners * CAP, TW, row_count)[flat_amp]
    every_tile = jnp.ones((flat_amp.shape[0],), dtype=bool)
    totals = accumulate(
        tasks, integrals, 0, live_count, amp_table, list_slots, every_tile, start_totals
    )
    flat_res, placed_res, target = routing(needed_residual_tiles, res_slot, res_dev, owners, CAP)
    outgoing = jnp.einsum(
        "gs,gar->sar", placed_res.astype(jnp.float32), totals, precision=lax.Precision.HIGHEST
    )
    outgoing = outgoing.reshape(owners, CAP, TW, row_count)
    arrived, arrived_ids = (
        lax.all_to_all(outgoing, "tile", split_axis=0, concat_axis=0, tiled=True),
        lax.all_to_all(target.astype(jnp.float32), "tile", split_axis=0, concat_axis=0, tiled=True),
    )
    incoming = (
        arrived_ids.reshape(-1)[:, None] == jnp.arange(res_dev, dtype=jnp.float32)[None, :]
    ).astype(jnp.float32)
    residual = jnp.einsum(
        "sj,sar->jar",
        incoming,
        arrived.reshape(owners * CAP, TW, row_count),
        precision=lax.Precision.HIGHEST,
    )
    slot_ids = own_index * res_dev + jnp.arange(res_dev, dtype=jnp.int32)
    matches = res_slot[None, :] == slot_ids[:, None]
    tile_ids = jnp.sum(
        jnp.where(matches, jnp.arange(res_slot.shape[0], dtype=jnp.int32)[None, :], 0), axis=1
    )
    tile_count = virt_energy.shape[0] // TW
    column = tile_ids % tile_count
    window = tile_ids // tile_count
    column_hits = (column[:, None] == jnp.arange(tile_count, dtype=jnp.int32)[None, :]).astype(
        jnp.float32
    )
    virt_part = jnp.dot(
        column_hits, virt_energy.reshape(tile_count, TW), precision=lax.Precision.HIGHEST
    )
    window_hits = window[:, None] == jnp.arange(window_energy.shape[0], dtype=jnp.int32)[None, :]
    window_part = jnp.sum(jnp.where(window_hits, window_energy[None, :], 0.0), axis=1)
    denominator = pair_energy[None, None, :] - virt_part[:, :, None] - window_part[:, None, None]
    return residual / denominator


def solution(mesh):
    in_specs = (
        P(None, ("mol", "tile")),
        P(("mol", "tile")),
        P(("mol", "tile"), None),
        P(("mol", "tile"), None, "rep"),
        P("mol"),
        P(("mol", "tile")),
        P("mol"),
        P(("mol", "tile")),
        P(("mol", "rep")),
        P("mol"),
        P("mol"),
    )
    out_specs = P(("mol", "tile"), None, "rep")
    return jax.shard_map(local, mesh=mesh, in_specs=in_specs, out_specs=out_specs, check_vma=False)
```

profile of v0, /device:TPU:12, one launch (start us, length us, event | category | flops | bytes accessed | tf_op | source)
XLA Modules:
  0.0 338.4 jit_solution(10479491258811692893)
XLA Ops:
  0.0 1.0 select_reduce_fusion.1
  1.0 0.2 convert_reduce_fusion
  1.2 0.1 select_reduce_fusion.4
  1.3 0.1 sub.55
  1.4 10.1 %all_to_all.22 = s32[8,1,2]{2,1,0:T(1,128)S(1)} all-to-all(s32[8,1,2]{2,1,0:T(1,128)S(1)} %bitcast.62), channel_id=1, replica_groups=mesh['mol'=2,'tile'=8,'rep'=2] {'tile'}, dimensions={0} | all-to-all | bytes 128 | tf_op jit(solution)/shard_map/all_to_all | solution.py:85
  11.6 0.1 reshape.283
  11.7 0.1 copy.32
  11.8 0.1 copy.33
  11.9 1.8 gather_fusion.1
  13.7 2.8 broadcast_select_fusion
  16.4 6.5 %all-to-all-start.2 = ((f32[8,2,64,384]{3,2,1,0:T(8,128)}), f32[8,2,64,384]{3,2,1,0:T(8,128)}, u32[]{:S(2)}, u32[]{:S(2)}) async-start(f32[8,2,64,384]{3,2,1,0:T(8,128)} %broadcast_select_fusion), calls=%async_computation.2 | async-start | bytes 3145728 | tf_op jit(solution)/shard_map/all_to_all | solution.py:83
  23.7 0.2 select_reduce_fusion.2
  23.9 0.2 convert_reduce_fusion.1
  24.1 0.1 select_reduce_fusion.5
  24.2 0.7 convert_element_type.25
  24.9 30.6 %all-to-all-done.2 = f32[8,2,64,384]{3,2,1,0:T(8,128)} async-done(((f32[8,2,64,384]{3,2,1,0:T(8,128)}), f32[8,2,64,384]{3,2,1,0:T(8,128)}, u32[]{:S(2)}, u32[]{:S(2)}) %all-to-all-start.2) | async-done | bytes 1572896 | tf_op jit(solution)/shard_map/all_to_all | solution.py:83
  55.5 7.0 %all-to-all-start = ((f32[8,1,2]{2,1,0:T(1,128)}), f32[8,1,2]{2,1,0:T(1,128)S(1)}, u32[]{:S(2)}, u32[]{:S(2)}) async-start(f32[8,1,2]{2,1,0:T(1,128)} %bitcast.4), calls=%async_computation | async-start | bytes 8192 | tf_op jit(solution)/shard_map/all_to_all | solution.py:104
  62.5 2.0 gather_fusion.2
  64.5 0.9 broadcast_in_dim.80
  65.5 105.9 %while.10 = (s32[]{:T(128)}, f32[8,64,384]{2,0,1:T(8,128)}, s32[]{:T(128)}, s32[2,512]{1,0:T(2,128)}, s32[]{:T(128)}, /*index=5*/f32[512,4096]{1,0:T(8,128)}, f3...) while((s32[]{:T(128)}, f32[8,64,384]{2,0,1:T(8,128)}, s32[]{:T(128)}, ...), condition=%wide.region_7.8_spmd, body=%wide.region_6.7_spmd.sunk | while | flops 1359153664 | bytes 38280232 | solution.py:52
  65.5 0.7 constant_dynamic-slice_fusion.5
  66.2 3.6 %gather_fusion = f32[64,64,384]{2,1,0:T(8,128)} fusion(f32[8,64,384]{2,1,0:T(8,128)S(1)} %get-tuple-element.137, s32[1024]{0:T(1024)S(1)} %pad_clamp_fusion.4), kind=kCustom, calls=%fused_computation.clone.1 | custom fusion | bytes 12583168 | tf_op jit(solution)/shard_map/while/body/gather | solution.py:38
  69.8 2.3 constant_dynamic-slice_fusion.4
  72.1 3.1 reshape.324
  75.2 8.4 %fusion.45 = f32[64,64,384]{2,1,0:T(8,128)S(1)} fusion(f32[64,64,64]{2,1,0:T(8,128)} %reshape.324, f32[64,64,384]{2,1,0:T(8,128)} %gather_fusion), kind=kOutput, calls=%fused_computation.69.clone.1 | convolution fusion | flops 1207959552 | bytes 13631488 | tf_op jit(solution)/shard_map/while/body/fzo,fou->fzu/dot_general | solution.py:39
  83.6 0.7 compare_and_fusion.3
  84.3 7.7 %fusion.46 = f32[8,64,384]{2,0,1:T(8,128)} fusion(f32[8,64,384]{2,0,1:T(8,128)} %get-tuple-element.121, f32[64,64,384]{2,1,0:T(8,128)S(1)} %fusion.45, s32[64]{0:T(128)S(1)} %slice_bitcast_fusion.2, pred[64]{0:T(512)(128)(4,1)S(1)} %compare_and_fusion.3), kind=kOutput, calls=%fused_computation.5.clone.1 | convolution fusion | flops 151192576 | bytes 7864640 | tf_op jit(solution)/shard_map/while/body/tg,tar->gar/dot_general | solution.py:48
  91.9 0.7 constant_dynamic-slice_fusion.5
  92.7 3.6 %gather_fusion = f32[64,64,384]{2,1,0:T(8,128)} fusion(f32[8,64,384]{2,1,0:T(8,128)S(1)} %get-tuple-element.137, s32[1024]{0:T(1024)S(1)} %pad_clamp_fusion.4), kind=kCustom, calls=%fused_computation.clone.1 | custom fusion | bytes 12583168 | tf_op jit(solution)/shard_map/while/body/gather | solution.py:38
  96.3 2.3 constant_dynamic-slice_fusion.4
  98.6 3.1 reshape.324
  101.7 8.4 %fusion.45 = f32[64,64,384]{2,1,0:T(8,128)S(1)} fusion(f32[64,64,64]{2,1,0:T(8,128)} %reshape.324, f32[64,64,384]{2,1,0:T(8,128)} %gather_fusion), kind=kOutput, calls=%fused_computation.69.clone.1 | convolution fusion | flops 1207959552 | bytes 13631488 | tf_op jit(solution)/shard_map/while/body/fzo,fou->fzu/dot_general | solution.py:39
  110.1 0.7 compare_and_fusion.3
  110.7 7.7 %fusion.46 = f32[8,64,384]{2,0,1:T(8,128)} fusion(f32[8,64,384]{2,0,1:T(8,128)} %get-tuple-element.121, f32[64,64,384]{2,1,0:T(8,128)S(1)} %fusion.45, s32[64]{0:T(128)S(1)} %slice_bitcast_fusion.2, pred[64]{0:T(512)(128)(4,1)S(1)} %compare_and_fusion.3), kind=kOutput, calls=%fused_computation.5.clone.1 | convolution fusion | flops 151192576 | bytes 7864640 | tf_op jit(solution)/shard_map/while/body/tg,tar->gar/dot_general | solution.py:48
  118.4 0.7 constant_dynamic-slice_fusion.5
  119.2 3.6 %gather_fusion = f32[64,64,384]{2,1,0:T(8,128)} fusion(f32[8,64,384]{2,1,0:T(8,128)S(1)} %get-tuple-element.137, s32[1024]{0:T(1024)S(1)} %pad_clamp_fusion.4), kind=kCustom, calls=%fused_computation.clone.1 | custom fusion | bytes 12583168 | tf_op jit(solution)/shard_map/while/body/gather | solution.py:38
  122.8 2.3 constant_dynamic-slice_fusion.4
  125.1 3.1 reshape.324
  128.2 8.4 %fusion.45 = f32[64,64,384]{2,1,0:T(8,128)S(1)} fusion(f32[64,64,64]{2,1,0:T(8,128)} %reshape.324, f32[64,64,384]{2,1,0:T(8,128)} %gather_fusion), kind=kOutput, calls=%fused_computation.69.clone.1 | convolution fusion | flops 1207959552 | bytes 13631488 | tf_op jit(solution)/shard_map/while/body/fzo,fou->fzu/dot_general | solution.py:39
  136.5 0.7 compare_and_fusion.3
  137.2 7.7 %fusion.46 = f32[8,64,384]{2,0,1:T(8,128)} fusion(f32[8,64,384]{2,0,1:T(8,128)} %get-tuple-element.121, f32[64,64,384]{2,1,0:T(8,128)S(1)} %fusion.45, s32[64]{0:T(128)S(1)} %slice_bitcast_fusion.2, pred[64]{0:T(512)(128)(4,1)S(1)} %compare_and_fusion.3), kind=kOutput, calls=%fused_computation.5.clone.1 | convolution fusion | flops 151192576 | bytes 7864640 | tf_op jit(solution)/shard_map/while/body/tg,tar->gar/dot_general | solution.py:48
  144.9 0.7 constant_dynamic-slice_fusion.5
  145.6 3.6 %gather_fusion = f32[64,64,384]{2,1,0:T(8,128)} fusion(f32[8,64,384]{2,1,0:T(8,128)S(1)} %get-tuple-element.137, s32[1024]{0:T(1024)S(1)} %pad_clamp_fusion.4), kind=kCustom, calls=%fused_computation.clone.1 | custom fusion | bytes 12583168 | tf_op jit(solution)/shard_map/while/body/gather | solution.py:38
  149.3 2.3 constant_dynamic-slice_fusion.4
  151.6 3.1 reshape.324
  154.6 8.4 %fusion.45 = f32[64,64,384]{2,1,0:T(8,128)S(1)} fusion(f32[64,64,64]{2,1,0:T(8,128)} %reshape.324, f32[64,64,384]{2,1,0:T(8,128)} %gather_fusion), kind=kOutput, calls=%fused_computation.69.clone.1 | convolution fusion | flops 1207959552 | bytes 13631488 | tf_op jit(solution)/shard_map/while/body/fzo,fou->fzu/dot_general | solution.py:39
  163.0 0.7 compare_and_fusion.3
  163.7 7.7 %fusion.46 = f32[8,64,384]{2,0,1:T(8,128)} fusion(f32[8,64,384]{2,0,1:T(8,128)} %get-tuple-element.121, f32[64,64,384]{2,1,0:T(8,128)S(1)} %fusion.45, s32[64]{0:T(128)S(1)} %slice_bitcast_fusion.2, pred[64]{0:T(512)(128)(4,1)S(1)} %compare_and_fusion.3), kind=kOutput, calls=%fused_computation.5.clone.1 | convolution fusion | flops 151192576 | bytes 7864640 | tf_op jit(solution)/shard_map/while/body/tg,tar->gar/dot_general | solution.py:48
  171.4 3.2 fusion.19
  174.5 3.0 reshape.255
  177.6 3.1 copy.34
  180.7 111.9 %all-to-all-start.3 = ((f32[8,2,64,384]{3,1,2,0:T(2,128)}), f32[8,2,64,384]{3,1,2,0:T(2,128)}, u32[]{:S(2)}, u32[]{:S(2)}) async-start(f32[8,2,64,384]{3,1,2,0:T(2,128)} %copy.34), calls=%async_computation.3 | async-start | bytes 3145728 | tf_op jit(solution)/shard_map/all_to_all | solution.py:103
  292.6 0.1 reshape.257
  292.7 0.2 select_reduce_fusion
  292.9 0.1 select_reduce_fusion.3
  293.0 0.2 fusion.11
  293.2 0.5 broadcast.461
  293.8 0.6 reduce.7
  294.4 0.1 eq.161
  294.5 31.5 %all-to-all-done.3 = f32[8,2,64,384]{3,1,2,0:T(2,128)} async-done(((f32[8,2,64,384]{3,1,2,0:T(2,128)}), f32[8,2,64,384]{3,1,2,0:T(2,128)}, u32[]{:S(2)}, u32[]{:S(2)}) %all-to-all-start.3) | async-done | bytes 1572896 | tf_op jit(solution)/shard_map/all_to_all | solution.py:103
  326.0 3.1 copy.35
  329.0 3.2 reshape.256
  332.2 3.3 subtract_divide_fusion
  335.5 2.9 copy.37
  (38 shorter events, 0.2 us)
Async XLA Ops:
  0.0 11.9 %copy-start = (f32[25,64,384]{2,1,0:T(8,128)S(1)}, f32[25,64,384]{2,1,0:T(8,128)}, u32[]{:S(2)}) copy-start(f32[25,64,384]{2,1,0:T(8,128)} %param.16) | copy-start | bytes 7372804
  13.7 10.0 %copy-start.2 = (s32[200]{0:T(256)S(1)}, s32[200]{0:T(256)}, u32[]{:S(2)}) copy-start(s32[200]{0:T(256)} %param.19) | copy-start | bytes 2404
  13.7 10.0 %copy-start.3 = (s32[8]{0:T(128)S(1)}, s32[8]{0:T(128)}, u32[]{:S(2)}) copy-start(s32[8]{0:T(128)} %param.20) | copy-start | bytes 100
  16.4 39.1 %all-to-all-start.2 = ((f32[8,2,64,384]{3,2,1,0:T(8,128)}), f32[8,2,64,384]{3,2,1,0:T(8,128)}, u32[]{:S(2)}, u32[]{:S(2)}) async-start(f32[8,2,64,384]{3,2,1,0:T(8,128)} %broadcast_select_fusion), calls=%async_computation.2 | async-start | bytes 3145728 | tf_op jit(solution)/shard_map/all_to_all | solution.py:83
  55.5 125.2 %all-to-all-start = ((f32[8,1,2]{2,1,0:T(1,128)}), f32[8,1,2]{2,1,0:T(1,128)S(1)}, u32[]{:S(2)}, u32[]{:S(2)}) async-start(f32[8,1,2]{2,1,0:T(1,128)} %bitcast.4), calls=%async_computation | async-start | bytes 8192 | tf_op jit(solution)/shard_map/all_to_all | solution.py:104
  177.6 115.0 %copy-start.1 = (f32[1600]{0:T(1024)S(1)}, f32[1600]{0:T(1024)}, u32[]{:S(2)}) copy-start(f32[1600]{0:T(1024)} %param.22) | copy-start | bytes 19204
  177.6 115.3 %copy-start.5 = (f32[8]{0:T(128)S(1)}, f32[8]{0:T(128)}, u32[]{:S(2)}) copy-start(f32[8]{0:T(128)} %param.23) | copy-start | bytes 100
  180.7 145.2 %all-to-all-start.3 = ((f32[8,2,64,384]{3,1,2,0:T(2,128)}), f32[8,2,64,384]{3,1,2,0:T(2,128)}, u32[]{:S(2)}, u32[]{:S(2)}) async-start(f32[8,2,64,384]{3,1,2,0:T(2,128)} %copy.34), calls=%async_computation.3 | async-start | bytes 3145728 | tf_op jit(solution)/shard_map/all_to_all | solution.py:103
  294.5 37.8 %copy-start.4 = (f32[384]{0:T(512)S(1)}, f32[384]{0:T(512)}, u32[]{:S(2)}) copy-start(f32[384]{0:T(512)} %param.21) | copy-start | bytes 4612
where the time goes:
time: 344 us; the launch traced here: 338 us
  starting transfers between devices  125 us (36%)
  matrix products  70.8 us (21%)
  waiting for transfers between devices  62.1 us (18%)
  local copies, waits for them, and re-layouts  60.8 us (18%)
  blocking collectives  10.1 us (3%)
  other arithmetic  8.23 us (2%)
    all_to_all x1, starting transfers between devices, local(): lax.all_to_all(outgoing, 'tile', split_axis=0, concat_axis=0, tiled=True)  112 us
    dot_general x4, matrix products, contract(): jnp.einsum('fzo,fou->fzu', operator_matrices, input_factor, precision=lax...  33.4 us
    all_to_all x1, waiting for transfers between devices, local(): lax.all_to_all(outgoing, 'tile', split_axis=0, concat_axis=0, tiled=True)  31.5 us
    dot_general x4, matrix products, contract(): jnp.einsum('tg,tar->gar', selection_mask, contracted_output, precision=la...  30.7 us
    all_to_all x1, waiting for transfers between devices, local(): lax.all_to_all(serve_from(amplitudes, lax.all_to_all(wanted, 'tile', spli...  30.6 us
    gather x4, local copies, waits for them, and re-layouts, contract(): input_factor = amp_table[picked[1]]  14.4 us
    reshape x4, local copies, waits for them, and re-layouts, contract(): lax.dynamic_slice_in_dim(integral_rows, offset, TBLK, 0)  12.3 us
    all_to_all x1, blocking collectives, local(): lax.all_to_all(wanted, 'tile', split_axis=0, concat_axis=0, tiled=True)  10.1 us
  transfers between devices with their start and end apart: 3, of which 2 were waited for; matrix products, arithmetic and copies ran while one was open for 36% of the time, Pallas kernels for 0%

commit v1 on v0

v1 whole, which is shorter than its diff:
```python
import functools

import jax
import jax.numpy as jnp
from jax import lax
from jax.experimental import pallas as pl
from jax.experimental.pallas import tpu as pltpu
from jax.sharding import PartitionSpec as P

TW = 64
CAP = 2
VMEM_LIMIT = 56 * 1024 * 1024
F32 = jnp.float32
BF16 = jnp.bfloat16

HBM_SPEC = pl.BlockSpec(memory_space=pl.ANY)
SMEM_SPEC = pl.BlockSpec(memory_space=pltpu.SMEM)
VMEM_SPEC = pl.BlockSpec(memory_space=pltpu.VMEM)


def params(limit=VMEM_LIMIT):
    return pltpu.CompilerParams(vmem_limit_bytes=limit)


def cost(flops, touched):
    return pl.CostEstimate(flops=flops, bytes_accessed=touched, transcendentals=0)


def clear(ref, count, value):
    @pl.loop(0, count)
    def _(i):
        ref[i] = value


def pack_kernel(owners, per_owner, width, me_ref, lists_ref, amp_slot_ref, amplitudes, *rest):
    outs, picked, seen, sems = rest[: owners - 1], rest[-3], rest[-2], rest[-1]
    list_length = lists_ref.shape[0] // owners // 2
    start = width[0]
    me = me_ref[0]
    low = me * per_owner
    clear(picked, owners * CAP, -1)
    clear(seen, owners, 0)

    @pl.loop(0, owners * list_length)
    def _(i):
        partner = i // list_length
        tile = lists_ref[partner * 2 * list_length + i % list_length]
        local = amp_slot_ref[tile] - low
        mine = (local >= 0) & (local < per_owner)

        @pl.when(mine)
        def _():
            count = seen[partner]
            picked[partner * CAP + count] = local
            seen[partner] = count + 1

    def copy(d, k):
        partner = jnp.bitwise_xor(me, d)
        local = picked[partner * CAP + k]
        return local, pltpu.make_async_copy(
            amplitudes.at[jnp.maximum(local, 0), :, pl.ds(start, width[1])],
            outs[d - 1].at[k],
            sems.at[d * CAP + k],
        )

    for step in ("start", "wait"):
        for d in range(owners - 1, 0, -1):
            for k in range(CAP):
                local, moved = copy(d, k)
                pl.when(local >= 0)(getattr(moved, step))


def maps_kernel(
    owners, per_amp, per_res, me_ref, lists_ref, amp_slot_ref, res_slot_ref,
    amp_from, amp_self, res_to, res_from, res_tile, seen,
):
    list_length = lists_ref.shape[0] // owners // 2
    me = me_ref[0]
    for ref in (amp_from, res_to, res_from):
        clear(ref, owners * CAP, -1)
    clear(amp_self, CAP, 0)
    clear(res_tile, owners * CAP, 0)

    def own_list(offset, slot_map, per_owner, place):
        clear(seen, owners, 0)

        @pl.loop(0, list_length)
        def _(g):
            slot = slot_map[lists_ref[me * 2 * list_length + offset + g]]
            owner = slot // per_owner
            d = jnp.bitwise_xor(owner, me)
            count = seen[d]
            place(d * CAP + count, g, slot - owner * per_owner, d, count)
            seen[d] = count + 1

    def place_amp(at, g, local, d, count):
        amp_from[at] = g

        @pl.when(d == 0)
        def _():
            amp_self[count] = local

    def place_res(at, g, local, d, count):
        res_to[at] = g

    own_list(0, amp_slot_ref, per_amp, place_amp)
    own_list(list_length, res_slot_ref, per_res, place_res)
    clear(seen, owners, 0)
    low = me * per_res

    @pl.loop(0, owners * list_length)
    def _(i):
        partner = i // list_length
        tile = lists_ref[partner * 2 * list_length + list_length + i % list_length]
        local = res_slot_ref[tile] - low

        @pl.when((local >= 0) & (local < per_res))
        def _():
            d = jnp.bitwise_xor(partner, me)
            count = seen[d]
            res_from[d * CAP + count] = local
            res_tile[d * CAP + count] = tile
            seen[d] = count + 1


def sum_kernel(count_ref, tasks_ref, integrals_ref, sums_ref, hits):
    slots = sums_ref.shape[0]
    tasks_here = integrals_ref.shape[0]
    list_length = int(round(slots**0.5))

    @pl.when(pl.program_id(0) == 0)
    def _():
        pair = tasks_ref[0:1, :] * list_length + tasks_ref[1:2, :]
        spot = lax.broadcasted_iota(jnp.int32, (1, tasks_here), 1)
        pair = jnp.where(spot < count_ref[0], pair, -1)
        row = lax.broadcasted_iota(jnp.int32, (slots, tasks_here), 0)
        hits[...] = jnp.where(row == pair, 1.0, 0.0).astype(BF16)

    rows = integrals_ref[...]
    high = rows.astype(BF16)
    low = (rows - high.astype(F32)).astype(BF16)
    sums_ref[...] = jnp.dot(hits[...], high, preferred_element_type=F32) + jnp.dot(
        hits[...], low, preferred_element_type=F32
    )


def product_kernel(owners, width, amp_from, amp_self, res_to, operator, amplitudes, *rest):
    arrived, outs = rest[: owners - 1], rest[owners - 1 : 2 * owners - 1]
    table, high, low, totals, in_sems, out_sems = rest[2 * owners - 1 :]
    start, columns = width
    rows = operator.shape[0]

    def fetch(d, k):
        g = amp_from[d * CAP + k]
        if d == 0:
            source = amplitudes.at[amp_self[k], :, pl.ds(start, columns)]
        else:
            source = arrived[d - 1].at[k]
        return g, pltpu.make_async_copy(source, table.at[jnp.maximum(g, 0)], in_sems.at[d * CAP + k])

    def deliver(d, k):
        g = res_to[d * CAP + k]
        return g, pltpu.make_async_copy(totals.at[jnp.maximum(g, 0)], outs[d].at[k], out_sems.at[d * CAP + k])

    def each(move, step):
        for d in range(owners):
            for k in range(CAP):
                g, moved = move(d, k)
                pl.when(g >= 0)(getattr(moved, step))

    each(fetch, "start")
    each(fetch, "wait")
    values = table[...].reshape(rows, columns)
    top = values.astype(BF16)
    high[...] = top
    low[...] = (values - top.astype(F32)).astype(BF16)
    step = 2 * TW

    @pl.loop(0, rows // step)
    def _(i):
        left = operator[pl.ds(pl.multiple_of(i * step, step), step), :]
        left_high = left.astype(BF16)
        left_low = (left - left_high.astype(F32)).astype(BF16)
        total = jnp.dot(left_high, low[...], preferred_element_type=F32)
        total += jnp.dot(left_low, high[...], preferred_element_type=F32)
        total += jnp.dot(left_high, high[...], preferred_element_type=F32)
        totals[pl.ds(i * 2, 2)] = total.reshape(2, TW, columns)

    each(deliver, "start")
    each(deliver, "wait")


def final_kernel(owners, width, tiles, chained, res_from, res_tile, window, pair, virt, *rest):
    arrived, (out, table, sums, in_sems, out_sem) = rest[:owners], rest[-5:]
    start, columns = width
    per_res = sums.shape[0]

    def fetch(d, k):
        local = res_from[d * CAP + k]
        return local, pltpu.make_async_copy(arrived[d].at[k], table.at[d * CAP + k], in_sems.at[d * CAP + k])

    for d in range(owners):
        for k in range(CAP):
            local, moved = fetch(d, k)
            pl.when(local >= 0)(moved.start)

    sums[...] = jnp.zeros_like(sums)
    for d in range(owners):
        for k in range(CAP):
            local, moved = fetch(d, k)

            @pl.when(local >= 0)
            def _():
                moved.wait()
                tile = res_tile[d * CAP + k]
                column = tile % tiles
                base = pair[...] - window[tile // tiles]
                below = base - jnp.concatenate([virt[column]] * (columns // 128), axis=1)
                sums[local] = sums[local] + table[d * CAP + k] / below

    written = pltpu.make_async_copy(sums, out.at[:, :, pl.ds(start, columns)], out_sem)
    written.start()
    written.wait()


def local(
    tasks,
    task_count,
    integrals,
    amplitudes,
    amp_slot,
    need_amp,
    res_slot,
    needed_residual_tiles,
    pair_energy,
    virt_energy,
    window_energy,
):
    owners = lax.axis_size("tile")
    me = lax.axis_index("tile").astype(jnp.int32)
    per_amp, _, row_count = amplitudes.shape
    per_res = res_slot.shape[0] // owners
    list_length = need_amp.shape[0]
    tile_count = virt_energy.shape[0] // TW
    slots = list_length * list_length
    task_slots = tasks.shape[1]
    chunks = [(0, row_count)]

    own_lists = jnp.concatenate([need_amp, needed_residual_tiles])
    spots = jnp.arange(owners, dtype=jnp.int32)[:, None] == me
    lists = lax.psum(jnp.where(spots, own_lists[None, :], 0), "tile").reshape(-1)
    me_ref = me.reshape(1)

    def exchange(buffers):
        return [
            lax.ppermute(buffers[d - 1], "tile", [(i, i ^ d) for i in range(owners)])
            for d in range(1, owners)
        ]

    def pack(chunk):
        piece = jax.ShapeDtypeStruct((CAP, TW, chunk[1]), F32)
        return pl.pallas_call(
            functools.partial(pack_kernel, owners, per_amp, chunk),
            out_shape=[piece] * (owners - 1),
            in_specs=[SMEM_SPEC] * 3 + [HBM_SPEC],
            out_specs=[HBM_SPEC] * (owners - 1),
            scratch_shapes=[
                pltpu.SMEM((owners * CAP,), jnp.int32),
                pltpu.SMEM((owners,), jnp.int32),
                pltpu.SemaphoreType.DMA((owners * CAP,)),
            ],
            compiler_params=params(),
            cost_estimate=cost(0, 2 * list_length * TW * chunk[1] * 4),
            name="pack_tiles",
        )(me_ref, lists, amp_slot, amplitudes)

    fetched = [exchange(pack(chunk)) for chunk in chunks]

    small = jax.ShapeDtypeStruct((owners * CAP,), jnp.int32)
    amp_from, amp_self, res_to, res_from, res_tile = pl.pallas_call(
        functools.partial(maps_kernel, owners, per_amp, per_res),
        out_shape=[small, jax.ShapeDtypeStruct((CAP,), jnp.int32), small, small, small],
        in_specs=[SMEM_SPEC] * 4,
        out_specs=[SMEM_SPEC] * 5,
        scratch_shapes=[pltpu.SMEM((owners,), jnp.int32)],
        compiler_params=params(),
        name="list_maps",
    )(me_ref, lists, amp_slot, res_slot)

    block = 512
    sums = pl.pallas_call(
        sum_kernel,
        grid=(TW * TW // block,),
        out_shape=jax.ShapeDtypeStruct((slots, TW * TW), F32),
        in_specs=[
            SMEM_SPEC,
            pl.BlockSpec((2, task_slots), lambda i: (0, 0)),
            pl.BlockSpec((task_slots, block), lambda i: (0, i)),
        ],
        out_specs=pl.BlockSpec((slots, block), lambda i: (0, i)),
        scratch_shapes=[pltpu.VMEM((slots, task_slots), BF16)],
        compiler_params=params(),
        cost_estimate=cost(4 * slots * task_slots * TW * TW, (task_slots + slots) * TW * TW * 4),
        name="sum_integrals",
    )(task_count, tasks, integrals)
    operator = (
        sums.reshape(list_length, list_length, TW, TW)
        .transpose(0, 2, 1, 3)
        .reshape(list_length * TW, list_length * TW)
    )

    def multiply(chunk, pieces):
        depth = list_length * TW
        piece = jax.ShapeDtypeStruct((CAP, TW, chunk[1]), F32)
        return pl.pallas_call(
            functools.partial(product_kernel, owners, chunk),
            out_shape=[piece] * owners,
            in_specs=[SMEM_SPEC] * 3 + [VMEM_SPEC] + [HBM_SPEC] * owners,
            out_specs=[HBM_SPEC] * owners,
            scratch_shapes=[
                pltpu.VMEM((list_length, TW, chunk[1]), F32),
                pltpu.VMEM((depth, chunk[1]), BF16),
                pltpu.VMEM((depth, chunk[1]), BF16),
                pltpu.VMEM((list_length, TW, chunk[1]), F32),
                pltpu.SemaphoreType.DMA((owners * CAP,)),
                pltpu.SemaphoreType.DMA((owners * CAP,)),
            ],
            compiler_params=params(),
            cost_estimate=cost(6 * depth * depth * chunk[1], 4 * depth * (depth + 2 * chunk[1])),
            name="multiply_tiles",
        )(amp_from, amp_self, res_to, operator, amplitudes, *pieces)

    virt = jnp.broadcast_to(virt_energy.reshape(tile_count, TW, 1), (tile_count, TW, 128))
    pair = pair_energy.reshape(1, row_count)

    def finish(chunk, pieces):
        return pl.pallas_call(
            functools.partial(final_kernel, owners, chunk, tile_count, False),
            out_shape=jax.ShapeDtypeStruct((per_res, TW, row_count), F32),
            in_specs=[SMEM_SPEC] * 3 + [VMEM_SPEC] * 2 + [HBM_SPEC] * owners,
            out_specs=HBM_SPEC,
            scratch_shapes=[
                pltpu.VMEM((owners * CAP, TW, chunk[1]), F32),
                pltpu.VMEM((per_res, TW, chunk[1]), F32),
                pltpu.SemaphoreType.DMA((owners * CAP,)),
                pltpu.SemaphoreType.DMA,
            ],
            compiler_params=params(),
            cost_estimate=cost(0, per_res * TW * chunk[1] * 4),
            name="finish_tiles",
        )(res_from, res_tile, window_energy, pair, virt, *pieces)

    for chunk, pieces in zip(chunks, fetched):
        products = multiply(chunk, pieces)
        result = finish(chunk, [products[0]] + exchange(products[1:]))
    return result


def solution(mesh):
    in_specs = (
        P(None, ("mol", "tile")),
        P(("mol", "tile")),
        P(("mol", "tile"), None),
        P(("mol", "tile"), None, "rep"),
        P("mol"),
        P(("mol", "tile")),
        P("mol"),
        P(("mol", "tile")),
        P(("mol", "rep")),
        P("mol"),
        P("mol"),
    )
    out_specs = P(("mol", "tile"), None, "rep")
    return jax.shard_map(local, mesh=mesh, in_specs=in_specs, out_specs=out_specs, check_vma=False)
```

time: 344 us -> 135 us (0.39); the launches traced: 338 us -> 137 us
  starting transfers between devices: 125 us -> 18.7 us
  matrix products: 70.8 us -> 0 us
  Pallas kernels: 0 us -> 60.1 us
  local copies, waits for them, and re-layouts: 60.8 us -> 9.84 us
  waiting for transfers between devices: 62.1 us -> 35.8 us
  other arithmetic: 8.23 us -> 0.82 us
    all_to_all x3 -> x0, starting transfers between devices: 125 us -> none  [the longest x1 112 us: local(): lax.all_to_all(outgoing, 'tile', split_axis=0, concat_axis=0, tiled=True)]
    dot_general x11 -> x0, matrix products: 70.8 us -> none  [the longest x4 33.4 us: contract(): jnp.einsum('fzo,fou->fzu', operator_matrices, input_factor, precision=lax...]
    all_to_all x3 -> x0, waiting for transfers between devices: 62.1 us -> none  [the longest x1 31.5 us: local(): lax.all_to_all(outgoing, 'tile', split_axis=0, concat_axis=0, tiled=True)]
    pallas_call x0 -> x5, Pallas kernels: none -> 60.1 us  [the longest x1 39.2 us: pack(): pl.pallas_call(functools.partial(pack_kernel, owners, per_amp, chunk), ou...]
    ppermute x0 -> x14, waiting for transfers between devices: none -> 35.8 us  [exchange(): lax.ppermute(buffers[d - 1], 'tile', [(i, i ^ d) for i in range(owners)])]
    ppermute x0 -> x14, starting transfers between devices: none -> 18.7 us  [exchange(): lax.ppermute(buffers[d - 1], 'tile', [(i, i ^ d) for i in range(owners)])]
    gather x6 -> x0, local copies, waits for them, and re-layouts: 18.2 us -> none  [the longest x4 14.4 us: contract(): input_factor = amp_table[picked[1]]]
    reshape x8 -> x5, local copies, waits for them, and re-layouts: 21.7 us -> 7.85 us  [the longest x2 4.51 us: local(): sums.reshape(list_length, list_length, TW, TW).transpose(0, 2, 1, 3)]
  transfers between devices with their start and end apart: 3 -> 14, of which waited for: 2 -> 9; matrix products, arithmetic and copies ran while one was open for 36% -> 6% of each run, Pallas kernels for 0% -> 9%
where the time goes in v1:
time: 135 us; the launch traced here: 137 us
  Pallas kernels  60.1 us (45%)
  waiting for transfers between devices  35.8 us (27%)
  starting transfers between devices  18.7 us (14%)
  blocking collectives  11.1 us (8%)
  local copies, waits for them, and re-layouts  9.84 us (7%)
    pallas_call x1, Pallas kernels, pack(): pl.pallas_call(functools.partial(pack_kernel, owners, per_amp, chunk), ou...  39.2 us
    ppermute x14, waiting for transfers between devices, exchange(): lax.ppermute(buffers[d - 1], 'tile', [(i, i ^ d) for i in range(owners)])  35.8 us
    ppermute x14, starting transfers between devices, exchange(): lax.ppermute(buffers[d - 1], 'tile', [(i, i ^ d) for i in range(owners)])  18.7 us
    psum x1, blocking collectives, local(): lax.psum(jnp.where(spots, own_lists[None, :], 0), 'tile').reshape(-1)  11.1 us
    pallas_call x1, Pallas kernels, local(): pl.pallas_call(sum_kernel, grid=(TW * TW // block,), out_shape=jax.ShapeD...  7.95 us
    pallas_call x1, Pallas kernels, multiply(): pl.pallas_call(functools.partial(product_kernel, owners, chunk), out_shap...  5.23 us
    reshape x2, local copies, waits for them, and re-layouts, local(): sums.reshape(list_length, list_length, TW, TW).transpose(0, 2, 1, 3)  4.51 us
    pallas_call x1, Pallas kernels, finish(): pl.pallas_call(functools.partial(final_kernel, owners, chunk, tile_count,...  3.9 us
  transfers between devices with their start and end apart: 14, of which 9 were waited for; matrix products, arithmetic and copies ran while one was open for 6% of the time, Pallas kernels for 9%

profile of v1, /device:TPU:12, one launch (start us, length us, event | category | flops | bytes accessed | tf_op | source)
XLA Modules:
  0.0 137.1 jit_solution(179024903625025281)
XLA Ops:
  0.0 0.7 pad_add_fusion
  0.8 0.1 broadcast_select_fusion
  0.8 0.1 reshape.24
  0.9 11.1 %psum.7.lists_ref = s32[128]{0:T(128)} all-reduce(s32[128]{0:T(128)S(1)} %reshape.24), channel_id=1, replica_groups=mesh['mol'=2,'tile'=8,'rep'=2] {'tile'}, use_global_device_ids=true, to_apply=%region_0.1 | all-reduce | flops 128 | bytes 1024 | tf_op jit(solution)/shard_map/psum | solution.py:251
  12.0 39.2 %pack_tiles.1 = (f32[2,64,384]{2,1,0:T(8,128)}, f32[2,64,384]{2,1,0:T(8,128)}, f32[2,64,384]{2,1,0:T(8,128)}, f32[2,64,384]{2,1,0:T(8,128)}, f32[2,64,384]{2,1,0...) custom-call(s32[1]{0:T(128)} %bitcast.me_ref, s32[128]{0:T(128)} %psum.7.lists_ref, s32[200]{0:T(256)} %amp_slot_ref.3, ...), custom_call_target="tpu_custom_call" | custom-call | bytes 1572864 | tf_op jit(solution)/shard_map/pack_tiles/pallas_call | solution.py:262
  51.2 0.1 collective-permute-start
  51.3 0.1 collective-permute-start.1
  51.3 3.4 %collective-permute-start.2 = (f32[2,64,384]{2,1,0:T(8,128)}, f32[2,64,384]{2,1,0:T(8,128)S(1)}, u32[]{:S(2)}, u32[]{:S(2)}) collective-permute-start(f32[2,64,384]{2,1,0:T(8,128)} %get-tuple-element.32), channel_id=1, source_target_pairs={{0,6},{2,4},{4,2},{6,0},{8,14},{10,12},{12,10},{14,8},{1,7},{3,5},... | collective-permute-start | bytes 589832 | tf_op jit(solution)/shard_map/ppermute | solution.py:256
  54.7 0.0 collective-permute-start.3
  54.7 2.4 %collective-permute-start.4 = (f32[2,64,384]{2,1,0:T(8,128)}, f32[2,64,384]{2,1,0:T(8,128)S(1)}, u32[]{:S(2)}, u32[]{:S(2)}) collective-permute-start(f32[2,64,384]{2,1,0:T(8,128)} %get-tuple-element.34), channel_id=1, source_target_pairs={{0,10},{2,8},{4,14},{6,12},{8,2},{10,0},{12,6},{14,4},{1,11},{3,9}... | collective-permute-start | bytes 589832 | tf_op jit(solution)/shard_map/ppermute | solution.py:256
  57.2 3.8 %collective-permute-done.rest_0_ = f32[2,64,384]{2,1,0:T(8,128)S(1)} collective-permute-done((f32[2,64,384]{2,1,0:T(8,128)}, f32[2,64,384]{2,1,0:T(8,128)S(1)}, u32[]{:S(2)}, u32[]{:S(2)}) %collective-permute-start) | collective-permute-done | bytes 196640 | tf_op jit(solution)/shard_map/ppermute | solution.py:256
  61.0 0.0 copy-start
  61.0 0.0 collective-permute-start.5
  61.0 0.0 collective-permute-done.1.rest_1_
  61.0 0.0 copy-start.1
  61.0 2.1 %collective-permute-start.6 = (f32[2,64,384]{2,1,0:T(8,128)}, f32[2,64,384]{2,1,0:T(8,128)S(1)}, u32[]{:S(2)}, u32[]{:S(2)}) collective-permute-start(f32[2,64,384]{2,1,0:T(8,128)} %get-tuple-element.36), channel_id=1, source_target_pairs={{0,14},{2,12},{4,10},{6,8},{8,6},{10,4},{12,2},{14,0},{1,15},{3,13... | collective-permute-start | bytes 589832 | tf_op jit(solution)/shard_map/ppermute | solution.py:256
  63.7 3.8 %list_maps.1 = (s32[16]{0:T(128)}, s32[2]{0:T(128)}, s32[16]{0:T(128)}, s32[16]{0:T(128)}, s32[16]{0:T(128)}) custom-call(s32[1]{0:T(128)} %bitcast.me_ref, s32[128]{0:T(128)} %psum.7.lists_ref, s32[200]{0:T(256)} %amp_slot_ref.3, s32[200]{0:T(256)} %res_slot_ref.1), custom_call_target="tpu_custom_call" | custom-call | tf_op jit(solution)/shard_map/list_maps/pallas_call | solution.py:280
  67.5 8.0 %sum_integrals.1 = f32[64,4096]{1,0:T(8,128)} custom-call(s32[1]{0:T(128)S(6)} %copy.15.count_ref, s32[2,512]{1,0:T(2,128)} %tasks_ref.1, f32[512,4096]{1,0:T(8,128)} %integrals_ref.1), custom_call_target="tpu_custom_call" | custom-call | flops 536870912 | bytes 9437184 | tf_op jit(solution)/shard_map/sum_integrals/pallas_call | solution.py:291
  75.4 0.0 copy-done
  75.4 0.0 copy-done.1
  75.4 2.0 %reshape.26 = f32[8,8,64,64]{3,2,1,0:T(8,128)S(1)} reshape(f32[64,4096]{1,0:T(8,128)} %sum_integrals.1) | data formatting | bytes 2097152 | tf_op jit(solution)/shard_map/reshape | solution.py:307
  77.5 2.5 %copy.14 = f32[8,8,64,64]{3,1,2,0:T(8,128)} copy(f32[8,8,64,64]{3,2,1,0:T(8,128)S(1)} %reshape.26) | data formatting | bytes 2097152 | tf_op jit(solution)/shard_map/reshape | solution.py:307
  80.0 2.7 %reshape.27.operator = f32[512,512]{1,0:T(8,128)} reshape(f32[8,64,8,64]{3,2,1,0:T(8,128)} %bitcast.6) | data formatting | bytes 2097152 | tf_op jit(solution)/shard_map/reshape | solution.py:309
  82.7 0.0 collective-permute-done.2.rest_2_
  82.7 0.0 copy-start.2
  82.7 0.0 collective-permute-done.3.rest_3_
  82.7 0.0 copy-start.3
  82.7 0.0 collective-permute-done.4.rest_4_
  82.7 0.0 copy-start.4
  82.7 1.7 %collective-permute-done.5.rest_5_ = f32[2,64,384]{2,1,0:T(8,128)S(1)} collective-permute-done((f32[2,64,384]{2,1,0:T(8,128)}, f32[2,64,384]{2,1,0:T(8,128)S(1)}, u32[]{:S(2)}, u32[]{:S(2)}) %collective-permute-start.5) | collective-permute-done | bytes 196640 | tf_op jit(solution)/shard_map/ppermute | solution.py:256
  84.5 2.9 %collective-permute-done.6.rest_6_ = f32[2,64,384]{2,1,0:T(8,128)S(1)} collective-permute-done((f32[2,64,384]{2,1,0:T(8,128)}, f32[2,64,384]{2,1,0:T(8,128)S(1)}, u32[]{:S(2)}, u32[]{:S(2)}) %collective-permute-start.6) | collective-permute-done | bytes 196640 | tf_op jit(solution)/shard_map/ppermute | solution.py:256
  87.3 0.0 copy-done.2
  87.3 0.0 copy-done.3
  87.4 0.0 copy-done.4
  87.4 0.0 copy-done.6
  87.4 0.7 copy-done.10
  88.0 5.2 %multiply_tiles.1 = (f32[2,64,384]{2,1,0:T(8,128)}, f32[2,64,384]{2,1,0:T(8,128)}, f32[2,64,384]{2,1,0:T(8,128)}, f32[2,64,384]{2,1,0:T(8,128)}, f32[2,64,384]{2...) custom-call(s32[16]{0:T(128)} %get-tuple-element.27.amp_from, ...), custom_call_target="tpu_custom_call" | custom-call | flops 603979776 | bytes 2621440 | tf_op jit(solution)/shard_map/multiply_tiles/pallas_call | solution.py:315
  93.3 1.5 %collective-permute-start.7 = (f32[2,64,384]{2,1,0:T(8,128)}, f32[2,64,384]{2,1,0:T(8,128)S(1)}, u32[]{:S(2)}, u32[]{:S(2)}) collective-permute-start(f32[2,64,384]{2,1,0:T(8,128)} %get-tuple-element.38), channel_id=1, source_target_pairs={{0,2},{2,0},{4,6},{6,4},{8,10},{10,8},{12,14},{14,12},{1,3},{3,1},... | collective-permute-start | bytes 589832 | tf_op jit(solution)/shard_map/ppermute | solution.py:256
  94.8 0.0 collective-permute-start.8
  94.8 2.0 %collective-permute-start.9 = (f32[2,64,384]{2,1,0:T(8,128)}, f32[2,64,384]{2,1,0:T(8,128)S(1)}, u32[]{:S(2)}, u32[]{:S(2)}) collective-permute-start(f32[2,64,384]{2,1,0:T(8,128)} %get-tuple-element.40), channel_id=1, source_target_pairs={{0,6},{2,4},{4,2},{6,0},{8,14},{10,12},{12,10},{14,8},{1,7},{3,5},... | collective-permute-start | bytes 589832 | tf_op jit(solution)/shard_map/ppermute | solution.py:256
  96.8 1.1 collective-permute-start.10
  98.0 2.7 %collective-permute-start.11 = (f32[2,64,384]{2,1,0:T(8,128)}, f32[2,64,384]{2,1,0:T(8,128)S(1)}, u32[]{:S(2)}, u32[]{:S(2)}) collective-permute-start(f32[2,64,384]{2,1,0:T(8,128)} %get-tuple-element.42), channel_id=1, source_target_pairs={{0,10},{2,8},{4,14},{6,12},{8,2},{10,0},{12,6},{14,4},{1,11},{3,9}... | collective-permute-start | bytes 589832 | tf_op jit(solution)/shard_map/ppermute | solution.py:256
  100.7 0.0 collective-permute-done.7.rest_1_
  100.7 1.9 %collective-permute-start.12 = (f32[2,64,384]{2,1,0:T(8,128)}, f32[2,64,384]{2,1,0:T(8,128)S(1)}, u32[]{:S(2)}, u32[]{:S(2)}) collective-permute-start(f32[2,64,384]{2,1,0:T(8,128)} %get-tuple-element.43), channel_id=1, source_target_pairs={{0,12},{2,14},{4,8},{6,10},{8,4},{10,6},{12,0},{14,2},{1,13},{3,15... | collective-permute-start | bytes 589832 | tf_op jit(solution)/shard_map/ppermute | solution.py:256
  102.5 2.7 %collective-permute-done.8.rest_2_ = f32[2,64,384]{2,1,0:T(8,128)S(1)} collective-permute-done((f32[2,64,384]{2,1,0:T(8,128)}, f32[2,64,384]{2,1,0:T(8,128)S(1)}, u32[]{:S(2)}, u32[]{:S(2)}) %collective-permute-start.8) | collective-permute-done | bytes 196640 | tf_op jit(solution)/shard_map/ppermute | solution.py:256
  105.3 1.4 %collective-permute-start.13 = (f32[2,64,384]{2,1,0:T(8,128)}, f32[2,64,384]{2,1,0:T(8,128)S(1)}, u32[]{:S(2)}, u32[]{:S(2)}) collective-permute-start(f32[2,64,384]{2,1,0:T(8,128)} %get-tuple-element.44), channel_id=1, source_target_pairs={{0,14},{2,12},{4,10},{6,8},{8,6},{10,4},{12,2},{14,0},{1,15},{3,13... | collective-permute-start | bytes 589832 | tf_op jit(solution)/shard_map/ppermute | solution.py:256
  106.7 0.0 copy-done.15
  106.7 0.6 reshape.25.pair
  107.2 0.0 copy-done.14
  107.3 0.1 broadcast_in_dim.32
  107.3 2.1 %collective-permute-done.9.rest_3_ = f32[2,64,384]{2,1,0:T(8,128)S(1)} collective-permute-done((f32[2,64,384]{2,1,0:T(8,128)}, f32[2,64,384]{2,1,0:T(8,128)S(1)}, u32[]{:S(2)}, u32[]{:S(2)}) %collective-permute-start.9) | collective-permute-done | bytes 196640 | tf_op jit(solution)/shard_map/ppermute | solution.py:256
  109.4 2.0 %collective-permute-done.10.rest_4_ = f32[2,64,384]{2,1,0:T(8,128)S(1)} collective-permute-done((f32[2,64,384]{2,1,0:T(8,128)}, f32[2,64,384]{2,1,0:T(8,128)S(1)}, u32[]{:S(2)}, u32[]{:S(2)}) %collective-permute-start.10) | collective-permute-done | bytes 196640 | tf_op jit(solution)/shard_map/ppermute | solution.py:256
  111.4 13.2 %collective-permute-done.11.rest_5_ = f32[2,64,384]{2,1,0:T(8,128)S(1)} collective-permute-done((f32[2,64,384]{2,1,0:T(8,128)}, f32[2,64,384]{2,1,0:T(8,128)S(1)}, u32[]{:S(2)}, u32[]{:S(2)}) %collective-permute-start.11) | collective-permute-done | bytes 196640 | tf_op jit(solution)/shard_map/ppermute | solution.py:256
  124.6 4.5 %collective-permute-done.12.rest_6_ = f32[2,64,384]{2,1,0:T(8,128)S(1)} collective-permute-done((f32[2,64,384]{2,1,0:T(8,128)}, f32[2,64,384]{2,1,0:T(8,128)S(1)}, u32[]{:S(2)}, u32[]{:S(2)}) %collective-permute-start.12) | collective-permute-done | bytes 196640 | tf_op jit(solution)/shard_map/ppermute | solution.py:256
  129.1 2.9 %collective-permute-done.13.rest_7_ = f32[2,64,384]{2,1,0:T(8,128)S(1)} collective-permute-done((f32[2,64,384]{2,1,0:T(8,128)}, f32[2,64,384]{2,1,0:T(8,128)S(1)}, u32[]{:S(2)}, u32[]{:S(2)}) %collective-permute-start.13) | collective-permute-done | bytes 196640 | tf_op jit(solution)/shard_map/ppermute | solution.py:256
  132.0 1.2 broadcast_in_dim.33.virt
  133.2 0.0 copy-done.5
  133.2 0.0 copy-done.7
  133.2 0.0 copy-done.8
  133.2 0.0 copy-done.9
  133.2 0.0 copy-done.11
  133.2 0.0 copy-done.12
  133.2 0.0 copy-done.13
  133.2 3.9 %finish_tiles.1 = f32[25,64,384]{2,1,0:T(8,128)} custom-call(s32[16]{0:T(128)} %get-tuple-element.25.res_from, s32[16]{0:T(128)} %get-tuple-element.26.res_tile, f32[8]{0:T(128)} %window.1, f32[1,384]{1,0:T(1,128)} %reshape.25.pair, f32[25,64,128]{2,1,0:T(8,128)} %broadcast_in_dim.33.virt, f32[2,64,384]{2,1,0:T(8,128)} %get-tuple-element.37.rest_0_, ...), custom_call_target="tpu_custom_call" | custom-call | bytes 2457600 | tf_op jit(solution)/shard_map/finish_tiles/pallas_call | solution.py:337
  (12 shorter events, 0.0 us)
Async XLA Ops:
  51.2 9.8 %collective-permute-start = (f32[2,64,384]{2,1,0:T(8,128)}, f32[2,64,384]{2,1,0:T(8,128)S(1)}, u32[]{:S(2)}, u32[]{:S(2)}) collective-permute-start(f32[2,64,384]{2,1,0:T(8,128)} %get-tuple-element.30), channel_id=1, source_target_pairs={{0,2},{2,0},{4,6},{6,4},{8,10},{10,8},{12,14},{14,12},{1,3},{3,1},... | collective-permute-start | bytes 589832 | tf_op jit(solution)/shard_map/ppermute | solution.py:256
  51.3 9.7 %collective-permute-start.1 = (f32[2,64,384]{2,1,0:T(8,128)}, f32[2,64,384]{2,1,0:T(8,128)S(1)}, u32[]{:S(2)}, u32[]{:S(2)}) collective-permute-start(f32[2,64,384]{2,1,0:T(8,128)} %get-tuple-element.31), channel_id=1, source_target_pairs={{0,4},{2,6},{4,0},{6,2},{8,12},{10,14},{12,8},{14,10},{1,5},{3,7},... | collective-permute-start | bytes 589832 | tf_op jit(solution)/shard_map/ppermute | solution.py:256
  51.3 31.3 %collective-permute-start.2 = (f32[2,64,384]{2,1,0:T(8,128)}, f32[2,64,384]{2,1,0:T(8,128)S(1)}, u32[]{:S(2)}, u32[]{:S(2)}) collective-permute-start(f32[2,64,384]{2,1,0:T(8,128)} %get-tuple-element.32), channel_id=1, source_target_pairs={{0,6},{2,4},{4,2},{6,0},{8,14},{10,12},{12,10},{14,8},{1,7},{3,5},... | collective-permute-start | bytes 589832 | tf_op jit(solution)/shard_map/ppermute | solution.py:256
  54.7 28.0 %collective-permute-start.3 = (f32[2,64,384]{2,1,0:T(8,128)}, f32[2,64,384]{2,1,0:T(8,128)S(1)}, u32[]{:S(2)}, u32[]{:S(2)}) collective-permute-start(f32[2,64,384]{2,1,0:T(8,128)} %get-tuple-element.33), channel_id=1, source_target_pairs={{0,8},{2,10},{4,12},{6,14},{8,0},{10,2},{12,4},{14,6},{1,9},{3,11}... | collective-permute-start | bytes 589832 | tf_op jit(solution)/shard_map/ppermute | solution.py:256
  54.7 28.0 %collective-permute-start.4 = (f32[2,64,384]{2,1,0:T(8,128)}, f32[2,64,384]{2,1,0:T(8,128)S(1)}, u32[]{:S(2)}, u32[]{:S(2)}) collective-permute-start(f32[2,64,384]{2,1,0:T(8,128)} %get-tuple-element.34), channel_id=1, source_target_pairs={{0,10},{2,8},{4,14},{6,12},{8,2},{10,0},{12,6},{14,4},{1,11},{3,9}... | collective-permute-start | bytes 589832 | tf_op jit(solution)/shard_map/ppermute | solution.py:256
  61.0 14.5 %copy-start = (f32[2,64,384]{2,1,0:T(8,128)}, f32[2,64,384]{2,1,0:T(8,128)S(1)}, u32[]{:S(2)}) copy-start(f32[2,64,384]{2,1,0:T(8,128)S(1)} %collective-permute-done.rest_0_) | copy-start | bytes 589828
  61.0 23.5 %collective-permute-start.5 = (f32[2,64,384]{2,1,0:T(8,128)}, f32[2,64,384]{2,1,0:T(8,128)S(1)}, u32[]{:S(2)}, u32[]{:S(2)}) collective-permute-start(f32[2,64,384]{2,1,0:T(8,128)} %get-tuple-element.35), channel_id=1, source_target_pairs={{0,12},{2,14},{4,8},{6,10},{8,4},{10,6},{12,0},{14,2},{1,13},{3,15... | collective-permute-start | bytes 589832 | tf_op jit(solution)/shard_map/ppermute | solution.py:256
  61.0 14.5 %copy-start.1 = (f32[2,64,384]{2,1,0:T(8,128)}, f32[2,64,384]{2,1,0:T(8,128)S(1)}, u32[]{:S(2)}) copy-start(f32[2,64,384]{2,1,0:T(8,128)S(1)} %collective-permute-done.1.rest_1_) | copy-start | bytes 589828
  61.0 26.4 %collective-permute-start.6 = (f32[2,64,384]{2,1,0:T(8,128)}, f32[2,64,384]{2,1,0:T(8,128)S(1)}, u32[]{:S(2)}, u32[]{:S(2)}) collective-permute-start(f32[2,64,384]{2,1,0:T(8,128)} %get-tuple-element.36), channel_id=1, source_target_pairs={{0,14},{2,12},{4,10},{6,8},{8,6},{10,4},{12,2},{14,0},{1,15},{3,13... | collective-permute-start | bytes 589832 | tf_op jit(solution)/shard_map/ppermute | solution.py:256
  82.7 24.0 %copy-start.15 = (f32[384]{0:T(512)S(1)}, f32[384]{0:T(512)}, u32[]{:S(2)}) copy-start(f32[384]{0:T(512)} %param.19) | copy-start | bytes 4612
  82.7 24.6 %copy-start.14 = (f32[1600]{0:T(1024)S(1)}, f32[1600]{0:T(1024)}, u32[]{:S(2)}) copy-start(f32[1600]{0:T(1024)} %param.20) | copy-start | bytes 19204
  82.7 4.7 %copy-start.2 = (f32[2,64,384]{2,1,0:T(8,128)}, f32[2,64,384]{2,1,0:T(8,128)S(1)}, u32[]{:S(2)}) copy-start(f32[2,64,384]{2,1,0:T(8,128)S(1)} %collective-permute-done.2.rest_2_) | copy-start | bytes 589828
  82.7 4.7 %copy-start.3 = (f32[2,64,384]{2,1,0:T(8,128)}, f32[2,64,384]{2,1,0:T(8,128)S(1)}, u32[]{:S(2)}) copy-start(f32[2,64,384]{2,1,0:T(8,128)S(1)} %collective-permute-done.3.rest_3_) | copy-start | bytes 589828
  82.7 4.6 %copy-start.4 = (f32[2,64,384]{2,1,0:T(8,128)}, f32[2,64,384]{2,1,0:T(8,128)S(1)}, u32[]{:S(2)}) copy-start(f32[2,64,384]{2,1,0:T(8,128)S(1)} %collective-permute-done.4.rest_4_) | copy-start | bytes 589828
  84.5 2.9 %copy-start.6 = (f32[2,64,384]{2,1,0:T(8,128)}, f32[2,64,384]{2,1,0:T(8,128)S(1)}, u32[]{:S(2)}) copy-start(f32[2,64,384]{2,1,0:T(8,128)S(1)} %collective-permute-done.5.rest_5_) | copy-start | bytes 589828
  87.3 0.7 copy-start.10
  93.3 7.4 %collective-permute-start.7 = (f32[2,64,384]{2,1,0:T(8,128)}, f32[2,64,384]{2,1,0:T(8,128)S(1)}, u32[]{:S(2)}, u32[]{:S(2)}) collective-permute-start(f32[2,64,384]{2,1,0:T(8,128)} %get-tuple-element.38), channel_id=1, source_target_pairs={{0,2},{2,0},{4,6},{6,4},{8,10},{10,8},{12,14},{14,12},{1,3},{3,1},... | collective-permute-start | bytes 589832 | tf_op jit(solution)/shard_map/ppermute | solution.py:256
  94.8 10.4 %collective-permute-start.8 = (f32[2,64,384]{2,1,0:T(8,128)}, f32[2,64,384]{2,1,0:T(8,128)S(1)}, u32[]{:S(2)}, u32[]{:S(2)}) collective-permute-start(f32[2,64,384]{2,1,0:T(8,128)} %get-tuple-element.39), channel_id=1, source_target_pairs={{0,4},{2,6},{4,0},{6,2},{8,12},{10,14},{12,8},{14,10},{1,5},{3,7},... | collective-permute-start | bytes 589832 | tf_op jit(solution)/shard_map/ppermute | solution.py:256
  94.8 14.6 %collective-permute-start.9 = (f32[2,64,384]{2,1,0:T(8,128)}, f32[2,64,384]{2,1,0:T(8,128)S(1)}, u32[]{:S(2)}, u32[]{:S(2)}) collective-permute-start(f32[2,64,384]{2,1,0:T(8,128)} %get-tuple-element.40), channel_id=1, source_target_pairs={{0,6},{2,4},{4,2},{6,0},{8,14},{10,12},{12,10},{14,8},{1,7},{3,5},... | collective-permute-start | bytes 589832 | tf_op jit(solution)/shard_map/ppermute | solution.py:256
  96.8 14.6 %collective-permute-start.10 = (f32[2,64,384]{2,1,0:T(8,128)}, f32[2,64,384]{2,1,0:T(8,128)S(1)}, u32[]{:S(2)}, u32[]{:S(2)}) collective-permute-start(f32[2,64,384]{2,1,0:T(8,128)} %get-tuple-element.41), channel_id=1, source_target_pairs={{0,8},{2,10},{4,12},{6,14},{8,0},{10,2},{12,4},{14,6},{1,9},{3,11}... | collective-permute-start | bytes 589832 | tf_op jit(solution)/shard_map/ppermute | solution.py:256
  98.0 26.7 %collective-permute-start.11 = (f32[2,64,384]{2,1,0:T(8,128)}, f32[2,64,384]{2,1,0:T(8,128)S(1)}, u32[]{:S(2)}, u32[]{:S(2)}) collective-permute-start(f32[2,64,384]{2,1,0:T(8,128)} %get-tuple-element.42), channel_id=1, source_target_pairs={{0,10},{2,8},{4,14},{6,12},{8,2},{10,0},{12,6},{14,4},{1,11},{3,9}... | collective-permute-start | bytes 589832 | tf_op jit(solution)/shard_map/ppermute | solution.py:256
  100.7 32.5 %copy-start.5 = (f32[2,64,384]{2,1,0:T(8,128)}, f32[2,64,384]{2,1,0:T(8,128)S(1)}, u32[]{:S(2)}) copy-start(f32[2,64,384]{2,1,0:T(8,128)S(1)} %collective-permute-done.7.rest_1_) | copy-start | bytes 589828
  100.7 28.4 %collective-permute-start.12 = (f32[2,64,384]{2,1,0:T(8,128)}, f32[2,64,384]{2,1,0:T(8,128)S(1)}, u32[]{:S(2)}, u32[]{:S(2)}) collective-permute-start(f32[2,64,384]{2,1,0:T(8,128)} %get-tuple-element.43), channel_id=1, source_target_pairs={{0,12},{2,14},{4,8},{6,10},{8,4},{10,6},{12,0},{14,2},{1,13},{3,15... | collective-permute-start | bytes 589832 | tf_op jit(solution)/shard_map/ppermute | solution.py:256
  105.3 27.9 %copy-start.7 = (f32[2,64,384]{2,1,0:T(8,128)}, f32[2,64,384]{2,1,0:T(8,128)S(1)}, u32[]{:S(2)}) copy-start(f32[2,64,384]{2,1,0:T(8,128)S(1)} %collective-permute-done.8.rest_2_) | copy-start | bytes 589828
  105.3 26.7 %collective-permute-start.13 = (f32[2,64,384]{2,1,0:T(8,128)}, f32[2,64,384]{2,1,0:T(8,128)S(1)}, u32[]{:S(2)}, u32[]{:S(2)}) collective-permute-start(f32[2,64,384]{2,1,0:T(8,128)} %get-tuple-element.44), channel_id=1, source_target_pairs={{0,14},{2,12},{4,10},{6,8},{8,6},{10,4},{12,2},{14,0},{1,15},{3,13... | collective-permute-start | bytes 589832 | tf_op jit(solution)/shard_map/ppermute | solution.py:256
  109.4 23.7 %copy-start.8 = (f32[2,64,384]{2,1,0:T(8,128)}, f32[2,64,384]{2,1,0:T(8,128)S(1)}, u32[]{:S(2)}) copy-start(f32[2,64,384]{2,1,0:T(8,128)S(1)} %collective-permute-done.9.rest_3_) | copy-start | bytes 589828
  111.4 21.7 %copy-start.9 = (f32[2,64,384]{2,1,0:T(8,128)}, f32[2,64,384]{2,1,0:T(8,128)S(1)}, u32[]{:S(2)}) copy-start(f32[2,64,384]{2,1,0:T(8,128)S(1)} %collective-permute-done.10.rest_4_) | copy-start | bytes 589828
  124.6 8.6 %copy-start.11 = (f32[2,64,384]{2,1,0:T(8,128)}, f32[2,64,384]{2,1,0:T(8,128)S(1)}, u32[]{:S(2)}) copy-start(f32[2,64,384]{2,1,0:T(8,128)S(1)} %collective-permute-done.11.rest_5_) | copy-start | bytes 589828
  129.1 4.1 %copy-start.12 = (f32[2,64,384]{2,1,0:T(8,128)}, f32[2,64,384]{2,1,0:T(8,128)S(1)}, u32[]{:S(2)}) copy-start(f32[2,64,384]{2,1,0:T(8,128)S(1)} %collective-permute-done.12.rest_6_) | copy-start | bytes 589828
  132.0 1.2 copy-start.13

commit v2 on v1

--- a/solution.py
+++ b/solution.py
@@ -33,7 +33,7 @@
 
 
 def pack_kernel(owners, per_owner, width, me_ref, lists_ref, amp_slot_ref, amplitudes, *rest):
-    outs, picked, seen, sems = rest[: owners - 1], rest[-3], rest[-2], rest[-1]
+    outs, (staged, picked, seen, in_sems, out_sems) = rest[: owners - 1], rest[-5:]
     list_length = lists_ref.shape[0] // owners // 2
     start = width[0]
     me = me_ref[0]
@@ -54,20 +54,33 @@
             picked[partner * CAP + count] = local
             seen[partner] = count + 1
 
-    def copy(d, k):
-        partner = jnp.bitwise_xor(me, d)
-        local = picked[partner * CAP + k]
-        return local, pltpu.make_async_copy(
-            amplitudes.at[jnp.maximum(local, 0), :, pl.ds(start, width[1])],
-            outs[d - 1].at[k],
-            sems.at[d * CAP + k],
-        )
-
-    for step in ("start", "wait"):
-        for d in range(owners - 1, 0, -1):
-            for k in range(CAP):
-                local, moved = copy(d, k)
-                pl.when(local >= 0)(getattr(moved, step))
+    def load(d, k):
+        spot = d * CAP + k
+        local = picked[jnp.bitwise_xor(me, d) * CAP + k]
+        source = amplitudes.at[jnp.maximum(local, 0), :, pl.ds(start, width[1])]
+        return local, pltpu.make_async_copy(source, staged.at[spot], in_sems.at[spot])
+
+    def store(d, k):
+        spot = d * CAP + k
+        local = picked[jnp.bitwise_xor(me, d) * CAP + k]
+        return local, pltpu.make_async_copy(staged.at[spot], outs[d - 1].at[k], out_sems.at[spot])
+
+    spots = [(d, k) for d in range(owners - 1, 0, -1) for k in range(CAP)]
+    for d, k in spots:
+        local, loaded = load(d, k)
+        pl.when(local >= 0)(loaded.start)
+    for d, k in spots:
+        local, loaded = load(d, k)
+        _, stored = store(d, k)
+
+        @pl.when(local >= 0)
+        def _():
+            loaded.wait()
+            stored.start()
+
+    for d, k in spots:
+        local, stored = store(d, k)
+        pl.when(local >= 0)(stored.wait)
 
 
 def maps_kernel(
@@ -265,8 +278,10 @@
             in_specs=[SMEM_SPEC] * 3 + [HBM_SPEC],
             out_specs=[HBM_SPEC] * (owners - 1),
             scratch_shapes=[
+                pltpu.VMEM((owners * CAP, TW, chunk[1]), F32),
                 pltpu.SMEM((owners * CAP,), jnp.int32),
                 pltpu.SMEM((owners,), jnp.int32),
+                pltpu.SemaphoreType.DMA((owners * CAP,)),
                 pltpu.SemaphoreType.DMA((owners * CAP,)),
             ],
             compiler_params=params(),

time: 135 us -> 103 us (0.76); the launches traced: 137 us -> 102 us
  Pallas kernels: 60.1 us -> 25.2 us
    pallas_call x1, Pallas kernels: 39.2 us -> 4.35 us  [pack(): pl.pallas_call(functools.partial(pack_kernel, owners, per_amp, chunk), ou...]
  transfers between devices with their start and end apart: 14 -> 14, of which waited for: 9 -> 10; matrix products, arithmetic and copies ran while one was open for 6% -> 8% of each run, Pallas kernels for 9% -> 12%
where the time goes in v2:
time: 103 us; the launch traced here: 102 us
  waiting for transfers between devices  36.5 us (35%)
  Pallas kernels  25.2 us (24%)
  starting transfers between devices  17.5 us (17%)
  blocking collectives  11.1 us (11%)
  local copies, waits for them, and re-layouts  9.84 us (10%)
    ppermute x14, waiting for transfers between devices, exchange(): lax.ppermute(buffers[d - 1], 'tile', [(i, i ^ d) for i in range(owners)])  36.5 us
    ppermute x14, starting transfers between devices, exchange(): lax.ppermute(buffers[d - 1], 'tile', [(i, i ^ d) for i in range(owners)])  17.5 us
    psum x1, blocking collectives, local(): lax.psum(jnp.where(spots, own_lists[None, :], 0), 'tile').reshape(-1)  11.1 us
    pallas_call x1, Pallas kernels, local(): pl.pallas_call(sum_kernel, grid=(TW * TW // block,), out_shape=jax.ShapeD...  7.95 us
    pallas_call x1, Pallas kernels, multiply(): pl.pallas_call(functools.partial(product_kernel, owners, chunk), out_shap...  5.19 us
    reshape x2, local copies, waits for them, and re-layouts, local(): sums.reshape(list_length, list_length, TW, TW).transpose(0, 2, 1, 3)  4.51 us
    pallas_call x1, Pallas kernels, pack(): pl.pallas_call(functools.partial(pack_kernel, owners, per_amp, chunk), ou...  4.35 us
    pallas_call x1, Pallas kernels, finish(): pl.pallas_call(functools.partial(final_kernel, owners, chunk, tile_count,...  3.94 us
  transfers between devices with their start and end apart: 14, of which 10 were waited for; matrix products, arithmetic and copies ran while one was open for 8% of the time, Pallas kernels for 12%

profile of v2, /device:TPU:12, one launch (start us, length us, event | category | flops | bytes accessed | tf_op | source)
XLA Modules:
  0.0 101.7 jit_solution(10775263883002857147)
XLA Ops:
  0.0 0.7 pad_add_fusion
  0.8 0.1 broadcast_select_fusion
  0.8 0.1 reshape.24
  0.9 11.1 %psum.7.lists_ref = s32[128]{0:T(128)} all-reduce(s32[128]{0:T(128)S(1)} %reshape.24), channel_id=1, replica_groups=mesh['mol'=2,'tile'=8,'rep'=2] {'tile'}, use_global_device_ids=true, to_apply=%region_0.1 | all-reduce | flops 128 | bytes 1024 | tf_op jit(solution)/shard_map/psum | solution.py:264
  12.0 4.4 %pack_tiles.1 = (f32[2,64,384]{2,1,0:T(8,128)}, f32[2,64,384]{2,1,0:T(8,128)}, f32[2,64,384]{2,1,0:T(8,128)}, f32[2,64,384]{2,1,0:T(8,128)}, f32[2,64,384]{2,1,0...) custom-call(s32[1]{0:T(128)} %bitcast.me_ref, s32[128]{0:T(128)} %psum.7.lists_ref, s32[200]{0:T(256)} %amp_slot_ref.3, ...), custom_call_target="tpu_custom_call" | custom-call | bytes 1572864 | tf_op jit(solution)/shard_map/pack_tiles/pallas_call | solution.py:275
  16.3 0.7 collective-permute-start
  17.0 1.7 %collective-permute-start.1 = (f32[2,64,384]{2,1,0:T(8,128)}, f32[2,64,384]{2,1,0:T(8,128)S(1)}, u32[]{:S(2)}, u32[]{:S(2)}) collective-permute-start(f32[2,64,384]{2,1,0:T(8,128)} %get-tuple-element.31), channel_id=1, source_target_pairs={{0,4},{2,6},{4,0},{6,2},{8,12},{10,14},{12,8},{14,10},{1,5},{3,7},... | collective-permute-start | bytes 589832 | tf_op jit(solution)/shard_map/ppermute | solution.py:269
  18.7 1.2 %collective-permute-start.2 = (f32[2,64,384]{2,1,0:T(8,128)}, f32[2,64,384]{2,1,0:T(8,128)S(1)}, u32[]{:S(2)}, u32[]{:S(2)}) collective-permute-start(f32[2,64,384]{2,1,0:T(8,128)} %get-tuple-element.32), channel_id=1, source_target_pairs={{0,6},{2,4},{4,2},{6,0},{8,14},{10,12},{12,10},{14,8},{1,7},{3,5},... | collective-permute-start | bytes 589832 | tf_op jit(solution)/shard_map/ppermute | solution.py:269
  19.9 0.4 collective-permute-start.3
  20.3 2.5 %collective-permute-start.4 = (f32[2,64,384]{2,1,0:T(8,128)}, f32[2,64,384]{2,1,0:T(8,128)S(1)}, u32[]{:S(2)}, u32[]{:S(2)}) collective-permute-start(f32[2,64,384]{2,1,0:T(8,128)} %get-tuple-element.34), channel_id=1, source_target_pairs={{0,10},{2,8},{4,14},{6,12},{8,2},{10,0},{12,6},{14,4},{1,11},{3,9}... | collective-permute-start | bytes 589832 | tf_op jit(solution)/shard_map/ppermute | solution.py:269
  22.8 1.1 %collective-permute-done.rest_0_ = f32[2,64,384]{2,1,0:T(8,128)S(1)} collective-permute-done((f32[2,64,384]{2,1,0:T(8,128)}, f32[2,64,384]{2,1,0:T(8,128)S(1)}, u32[]{:S(2)}, u32[]{:S(2)}) %collective-permute-start) | collective-permute-done | bytes 196640 | tf_op jit(solution)/shard_map/ppermute | solution.py:269
  23.9 0.0 copy-start
  23.9 0.2 collective-permute-start.5
  24.1 1.3 %collective-permute-done.1.rest_1_ = f32[2,64,384]{2,1,0:T(8,128)S(1)} collective-permute-done((f32[2,64,384]{2,1,0:T(8,128)}, f32[2,64,384]{2,1,0:T(8,128)S(1)}, u32[]{:S(2)}, u32[]{:S(2)}) %collective-permute-start.1) | collective-permute-done | bytes 196640 | tf_op jit(solution)/shard_map/ppermute | solution.py:269
  25.4 0.0 copy-start.1
  25.4 2.6 %collective-permute-start.6 = (f32[2,64,384]{2,1,0:T(8,128)}, f32[2,64,384]{2,1,0:T(8,128)S(1)}, u32[]{:S(2)}, u32[]{:S(2)}) collective-permute-start(f32[2,64,384]{2,1,0:T(8,128)} %get-tuple-element.36), channel_id=1, source_target_pairs={{0,14},{2,12},{4,10},{6,8},{8,6},{10,4},{12,2},{14,0},{1,15},{3,13... | collective-permute-start | bytes 589832 | tf_op jit(solution)/shard_map/ppermute | solution.py:269
  28.7 3.8 %list_maps.1 = (s32[16]{0:T(128)}, s32[2]{0:T(128)}, s32[16]{0:T(128)}, s32[16]{0:T(128)}, s32[16]{0:T(128)}) custom-call(s32[1]{0:T(128)} %bitcast.me_ref, s32[128]{0:T(128)} %psum.7.lists_ref, s32[200]{0:T(256)} %amp_slot_ref.3, s32[200]{0:T(256)} %res_slot_ref.1), custom_call_target="tpu_custom_call" | custom-call | tf_op jit(solution)/shard_map/list_maps/pallas_call | solution.py:295
  32.4 8.0 %sum_integrals.1 = f32[64,4096]{1,0:T(8,128)} custom-call(s32[1]{0:T(128)S(6)} %copy.15.count_ref, s32[2,512]{1,0:T(2,128)} %tasks_ref.1, f32[512,4096]{1,0:T(8,128)} %integrals_ref.1), custom_call_target="tpu_custom_call" | custom-call | flops 536870912 | bytes 9437184 | tf_op jit(solution)/shard_map/sum_integrals/pallas_call | solution.py:306
  40.4 0.0 copy-done
  40.4 0.0 copy-done.1
  40.4 2.0 %reshape.26 = f32[8,8,64,64]{3,2,1,0:T(8,128)S(1)} reshape(f32[64,4096]{1,0:T(8,128)} %sum_integrals.1) | data formatting | bytes 2097152 | tf_op jit(solution)/shard_map/reshape | solution.py:322
  42.4 2.5 %copy.14 = f32[8,8,64,64]{3,1,2,0:T(8,128)} copy(f32[8,8,64,64]{3,2,1,0:T(8,128)S(1)} %reshape.26) | data formatting | bytes 2097152 | tf_op jit(solution)/shard_map/reshape | solution.py:322
  44.9 2.7 %reshape.27.operator = f32[512,512]{1,0:T(8,128)} reshape(f32[8,64,8,64]{3,2,1,0:T(8,128)} %bitcast.6) | data formatting | bytes 2097152 | tf_op jit(solution)/shard_map/reshape | solution.py:324
  47.6 0.0 collective-permute-done.2.rest_2_
  47.6 0.0 copy-start.2
  47.6 0.0 collective-permute-done.3.rest_3_
  47.6 0.0 copy-start.3
  47.7 0.0 collective-permute-done.4.rest_4_
  47.7 0.0 copy-start.4
  47.7 3.8 %collective-permute-done.5.rest_5_ = f32[2,64,384]{2,1,0:T(8,128)S(1)} collective-permute-done((f32[2,64,384]{2,1,0:T(8,128)}, f32[2,64,384]{2,1,0:T(8,128)S(1)}, u32[]{:S(2)}, u32[]{:S(2)}) %collective-permute-start.5) | collective-permute-done | bytes 196640 | tf_op jit(solution)/shard_map/ppermute | solution.py:269
  51.5 2.2 %collective-permute-done.6.rest_6_ = f32[2,64,384]{2,1,0:T(8,128)S(1)} collective-permute-done((f32[2,64,384]{2,1,0:T(8,128)}, f32[2,64,384]{2,1,0:T(8,128)S(1)}, u32[]{:S(2)}, u32[]{:S(2)}) %collective-permute-start.6) | collective-permute-done | bytes 196640 | tf_op jit(solution)/shard_map/ppermute | solution.py:269
  53.7 0.0 copy-done.2
  53.7 0.0 copy-done.3
  53.7 0.0 copy-done.4
  53.7 0.0 copy-done.6
  53.7 0.7 copy-done.10
  54.4 5.2 %multiply_tiles.1 = (f32[2,64,384]{2,1,0:T(8,128)}, f32[2,64,384]{2,1,0:T(8,128)}, f32[2,64,384]{2,1,0:T(8,128)}, f32[2,64,384]{2,1,0:T(8,128)}, f32[2,64,384]{2...) custom-call(s32[16]{0:T(128)} %get-tuple-element.27.amp_from, ...), custom_call_target="tpu_custom_call" | custom-call | flops 603979776 | bytes 2621440 | tf_op jit(solution)/shard_map/multiply_tiles/pallas_call | solution.py:330
  59.6 1.4 %collective-permute-start.7 = (f32[2,64,384]{2,1,0:T(8,128)}, f32[2,64,384]{2,1,0:T(8,128)S(1)}, u32[]{:S(2)}, u32[]{:S(2)}) collective-permute-start(f32[2,64,384]{2,1,0:T(8,128)} %get-tuple-element.38), channel_id=1, source_target_pairs={{0,2},{2,0},{4,6},{6,4},{8,10},{10,8},{12,14},{14,12},{1,3},{3,1},... | collective-permute-start | bytes 589832 | tf_op jit(solution)/shard_map/ppermute | solution.py:269
  61.0 0.0 collective-permute-start.8
  61.1 2.1 %collective-permute-start.9 = (f32[2,64,384]{2,1,0:T(8,128)}, f32[2,64,384]{2,1,0:T(8,128)S(1)}, u32[]{:S(2)}, u32[]{:S(2)}) collective-permute-start(f32[2,64,384]{2,1,0:T(8,128)} %get-tuple-element.40), channel_id=1, source_target_pairs={{0,6},{2,4},{4,2},{6,0},{8,14},{10,12},{12,10},{14,8},{1,7},{3,5},... | collective-permute-start | bytes 589832 | tf_op jit(solution)/shard_map/ppermute | solution.py:269
  63.2 0.0 collective-permute-start.10
  63.2 3.7 %collective-permute-start.11 = (f32[2,64,384]{2,1,0:T(8,128)}, f32[2,64,384]{2,1,0:T(8,128)S(1)}, u32[]{:S(2)}, u32[]{:S(2)}) collective-permute-start(f32[2,64,384]{2,1,0:T(8,128)} %get-tuple-element.42), channel_id=1, source_target_pairs={{0,10},{2,8},{4,14},{6,12},{8,2},{10,0},{12,6},{14,4},{1,11},{3,9}... | collective-permute-start | bytes 589832 | tf_op jit(solution)/shard_map/ppermute | solution.py:269
  66.9 0.0 collective-permute-done.7.rest_1_
  66.9 0.4 collective-permute-start.12
  67.3 2.4 %collective-permute-done.8.rest_2_ = f32[2,64,384]{2,1,0:T(8,128)S(1)} collective-permute-done((f32[2,64,384]{2,1,0:T(8,128)}, f32[2,64,384]{2,1,0:T(8,128)S(1)}, u32[]{:S(2)}, u32[]{:S(2)}) %collective-permute-start.8) | collective-permute-done | bytes 196640 | tf_op jit(solution)/shard_map/ppermute | solution.py:269
  69.7 0.6 collective-permute-start.13
  70.2 0.0 copy-done.15
  70.2 0.6 reshape.25.pair
  70.8 0.0 copy-done.14
  70.8 0.1 broadcast_in_dim.32
  70.9 4.0 %collective-permute-done.9.rest_3_ = f32[2,64,384]{2,1,0:T(8,128)S(1)} collective-permute-done((f32[2,64,384]{2,1,0:T(8,128)}, f32[2,64,384]{2,1,0:T(8,128)S(1)}, u32[]{:S(2)}, u32[]{:S(2)}) %collective-permute-start.9) | collective-permute-done | bytes 196640 | tf_op jit(solution)/shard_map/ppermute | solution.py:269
  74.9 1.8 %collective-permute-done.10.rest_4_ = f32[2,64,384]{2,1,0:T(8,128)S(1)} collective-permute-done((f32[2,64,384]{2,1,0:T(8,128)}, f32[2,64,384]{2,1,0:T(8,128)S(1)}, u32[]{:S(2)}, u32[]{:S(2)}) %collective-permute-start.10) | collective-permute-done | bytes 196640 | tf_op jit(solution)/shard_map/ppermute | solution.py:269
  76.7 12.9 %collective-permute-done.11.rest_5_ = f32[2,64,384]{2,1,0:T(8,128)S(1)} collective-permute-done((f32[2,64,384]{2,1,0:T(8,128)}, f32[2,64,384]{2,1,0:T(8,128)S(1)}, u32[]{:S(2)}, u32[]{:S(2)}) %collective-permute-start.11) | collective-permute-done | bytes 196640 | tf_op jit(solution)/shard_map/ppermute | solution.py:269
  89.6 4.0 %collective-permute-done.12.rest_6_ = f32[2,64,384]{2,1,0:T(8,128)S(1)} collective-permute-done((f32[2,64,384]{2,1,0:T(8,128)}, f32[2,64,384]{2,1,0:T(8,128)S(1)}, u32[]{:S(2)}, u32[]{:S(2)}) %collective-permute-start.12) | collective-permute-done | bytes 196640 | tf_op jit(solution)/shard_map/ppermute | solution.py:269
  93.6 3.0 %collective-permute-done.13.rest_7_ = f32[2,64,384]{2,1,0:T(8,128)S(1)} collective-permute-done((f32[2,64,384]{2,1,0:T(8,128)}, f32[2,64,384]{2,1,0:T(8,128)S(1)}, u32[]{:S(2)}, u32[]{:S(2)}) %collective-permute-start.13) | collective-permute-done | bytes 196640 | tf_op jit(solution)/shard_map/ppermute | solution.py:269
  96.6 1.2 %broadcast_in_dim.33.virt = f32[25,64,128]{2,1,0:T(8,128)} broadcast(f32[25,64]{1,0:T(8,128)S(1)} %broadcast_in_dim.32), dimensions={0,1} | broadcast | bytes 825600 | tf_op jit(solution)/shard_map/broadcast_in_dim | solution.py:348
  97.7 0.0 copy-done.5
  97.7 0.0 copy-done.7
  97.7 0.0 copy-done.8
  97.7 0.0 copy-done.9
  97.8 0.0 copy-done.11
  97.8 0.0 copy-done.12
  97.8 0.0 copy-done.13
  97.8 3.9 %finish_tiles.1 = f32[25,64,384]{2,1,0:T(8,128)} custom-call(s32[16]{0:T(128)} %get-tuple-element.25.res_from, s32[16]{0:T(128)} %get-tuple-element.26.res_tile, f32[8]{0:T(128)} %window.1, f32[1,384]{1,0:T(1,128)} %reshape.25.pair, f32[25,64,128]{2,1,0:T(8,128)} %broadcast_in_dim.33.virt, f32[2,64,384]{2,1,0:T(8,128)} %get-tuple-element.37.rest_0_, ...), custom_call_target="tpu_custom_call" | custom-call | bytes 2457600 | tf_op jit(solution)/shard_map/finish_tiles/pallas_call | solution.py:352
  (12 shorter events, 0.0 us)
Async XLA Ops:
  16.3 7.6 %collective-permute-start = (f32[2,64,384]{2,1,0:T(8,128)}, f32[2,64,384]{2,1,0:T(8,128)S(1)}, u32[]{:S(2)}, u32[]{:S(2)}) collective-permute-start(f32[2,64,384]{2,1,0:T(8,128)} %get-tuple-element.30), channel_id=1, source_target_pairs={{0,2},{2,0},{4,6},{6,4},{8,10},{10,8},{12,14},{14,12},{1,3},{3,1},... | collective-permute-start | bytes 589832 | tf_op jit(solution)/shard_map/ppermute | solution.py:269
  17.0 8.4 %collective-permute-start.1 = (f32[2,64,384]{2,1,0:T(8,128)}, f32[2,64,384]{2,1,0:T(8,128)S(1)}, u32[]{:S(2)}, u32[]{:S(2)}) collective-permute-start(f32[2,64,384]{2,1,0:T(8,128)} %get-tuple-element.31), channel_id=1, source_target_pairs={{0,4},{2,6},{4,0},{6,2},{8,12},{10,14},{12,8},{14,10},{1,5},{3,7},... | collective-permute-start | bytes 589832 | tf_op jit(solution)/shard_map/ppermute | solution.py:269
  18.7 28.9 %collective-permute-start.2 = (f32[2,64,384]{2,1,0:T(8,128)}, f32[2,64,384]{2,1,0:T(8,128)S(1)}, u32[]{:S(2)}, u32[]{:S(2)}) collective-permute-start(f32[2,64,384]{2,1,0:T(8,128)} %get-tuple-element.32), channel_id=1, source_target_pairs={{0,6},{2,4},{4,2},{6,0},{8,14},{10,12},{12,10},{14,8},{1,7},{3,5},... | collective-permute-start | bytes 589832 | tf_op jit(solution)/shard_map/ppermute | solution.py:269
  19.9 27.8 %collective-permute-start.3 = (f32[2,64,384]{2,1,0:T(8,128)}, f32[2,64,384]{2,1,0:T(8,128)S(1)}, u32[]{:S(2)}, u32[]{:S(2)}) collective-permute-start(f32[2,64,384]{2,1,0:T(8,128)} %get-tuple-element.33), channel_id=1, source_target_pairs={{0,8},{2,10},{4,12},{6,14},{8,0},{10,2},{12,4},{14,6},{1,9},{3,11}... | collective-permute-start | bytes 589832 | tf_op jit(solution)/shard_map/ppermute | solution.py:269
  20.3 27.4 %collective-permute-start.4 = (f32[2,64,384]{2,1,0:T(8,128)}, f32[2,64,384]{2,1,0:T(8,128)S(1)}, u32[]{:S(2)}, u32[]{:S(2)}) collective-permute-start(f32[2,64,384]{2,1,0:T(8,128)} %get-tuple-element.34), channel_id=1, source_target_pairs={{0,10},{2,8},{4,14},{6,12},{8,2},{10,0},{12,6},{14,4},{1,11},{3,9}... | collective-permute-start | bytes 589832 | tf_op jit(solution)/shard_map/ppermute | solution.py:269
  23.9 16.5 %copy-start = (f32[2,64,384]{2,1,0:T(8,128)}, f32[2,64,384]{2,1,0:T(8,128)S(1)}, u32[]{:S(2)}) copy-start(f32[2,64,384]{2,1,0:T(8,128)S(1)} %collective-permute-done.rest_0_) | copy-start | bytes 589828
  23.9 27.6 %collective-permute-start.5 = (f32[2,64,384]{2,1,0:T(8,128)}, f32[2,64,384]{2,1,0:T(8,128)S(1)}, u32[]{:S(2)}, u32[]{:S(2)}) collective-permute-start(f32[2,64,384]{2,1,0:T(8,128)} %get-tuple-element.35), channel_id=1, source_target_pairs={{0,12},{2,14},{4,8},{6,10},{8,4},{10,6},{12,0},{14,2},{1,13},{3,15... | collective-permute-start | bytes 589832 | tf_op jit(solution)/shard_map/ppermute | solution.py:269
  25.4 15.0 %copy-start.1 = (f32[2,64,384]{2,1,0:T(8,128)}, f32[2,64,384]{2,1,0:T(8,128)S(1)}, u32[]{:S(2)}) copy-start(f32[2,64,384]{2,1,0:T(8,128)S(1)} %collective-permute-done.1.rest_1_) | copy-start | bytes 589828
  25.4 28.3 %collective-permute-start.6 = (f32[2,64,384]{2,1,0:T(8,128)}, f32[2,64,384]{2,1,0:T(8,128)S(1)}, u32[]{:S(2)}, u32[]{:S(2)}) collective-permute-start(f32[2,64,384]{2,1,0:T(8,128)} %get-tuple-element.36), channel_id=1, source_target_pairs={{0,14},{2,12},{4,10},{6,8},{8,6},{10,4},{12,2},{14,0},{1,15},{3,13... | collective-permute-start | bytes 589832 | tf_op jit(solution)/shard_map/ppermute | solution.py:269
  47.6 22.6 %copy-start.15 = (f32[384]{0:T(512)S(1)}, f32[384]{0:T(512)}, u32[]{:S(2)}) copy-start(f32[384]{0:T(512)} %param.19) | copy-start | bytes 4612
  47.6 23.2 %copy-start.14 = (f32[1600]{0:T(1024)S(1)}, f32[1600]{0:T(1024)}, u32[]{:S(2)}) copy-start(f32[1600]{0:T(1024)} %param.20) | copy-start | bytes 19204
  47.6 6.1 %copy-start.2 = (f32[2,64,384]{2,1,0:T(8,128)}, f32[2,64,384]{2,1,0:T(8,128)S(1)}, u32[]{:S(2)}) copy-start(f32[2,64,384]{2,1,0:T(8,128)S(1)} %collective-permute-done.2.rest_2_) | copy-start | bytes 589828
  47.6 6.1 %copy-start.3 = (f32[2,64,384]{2,1,0:T(8,128)}, f32[2,64,384]{2,1,0:T(8,128)S(1)}, u32[]{:S(2)}) copy-start(f32[2,64,384]{2,1,0:T(8,128)S(1)} %collective-permute-done.3.rest_3_) | copy-start | bytes 589828
  47.7 6.1 %copy-start.4 = (f32[2,64,384]{2,1,0:T(8,128)}, f32[2,64,384]{2,1,0:T(8,128)S(1)}, u32[]{:S(2)}) copy-start(f32[2,64,384]{2,1,0:T(8,128)S(1)} %collective-permute-done.4.rest_4_) | copy-start | bytes 589828
  51.5 2.2 %copy-start.6 = (f32[2,64,384]{2,1,0:T(8,128)}, f32[2,64,384]{2,1,0:T(8,128)S(1)}, u32[]{:S(2)}) copy-start(f32[2,64,384]{2,1,0:T(8,128)S(1)} %collective-permute-done.5.rest_5_) | copy-start | bytes 589828
  53.7 0.7 copy-start.10
  59.6 7.3 %collective-permute-start.7 = (f32[2,64,384]{2,1,0:T(8,128)}, f32[2,64,384]{2,1,0:T(8,128)S(1)}, u32[]{:S(2)}, u32[]{:S(2)}) collective-permute-start(f32[2,64,384]{2,1,0:T(8,128)} %get-tuple-element.38), channel_id=1, source_target_pairs={{0,2},{2,0},{4,6},{6,4},{8,10},{10,8},{12,14},{14,12},{1,3},{3,1},... | collective-permute-start | bytes 589832 | tf_op jit(solution)/shard_map/ppermute | solution.py:269
  61.0 8.6 %collective-permute-start.8 = (f32[2,64,384]{2,1,0:T(8,128)}, f32[2,64,384]{2,1,0:T(8,128)S(1)}, u32[]{:S(2)}, u32[]{:S(2)}) collective-permute-start(f32[2,64,384]{2,1,0:T(8,128)} %get-tuple-element.39), channel_id=1, source_target_pairs={{0,4},{2,6},{4,0},{6,2},{8,12},{10,14},{12,8},{14,10},{1,5},{3,7},... | collective-permute-start | bytes 589832 | tf_op jit(solution)/shard_map/ppermute | solution.py:269
  61.1 13.8 %collective-permute-start.9 = (f32[2,64,384]{2,1,0:T(8,128)}, f32[2,64,384]{2,1,0:T(8,128)S(1)}, u32[]{:S(2)}, u32[]{:S(2)}) collective-permute-start(f32[2,64,384]{2,1,0:T(8,128)} %get-tuple-element.40), channel_id=1, source_target_pairs={{0,6},{2,4},{4,2},{6,0},{8,14},{10,12},{12,10},{14,8},{1,7},{3,5},... | collective-permute-start | bytes 589832 | tf_op jit(solution)/shard_map/ppermute | solution.py:269
  63.2 13.5 %collective-permute-start.10 = (f32[2,64,384]{2,1,0:T(8,128)}, f32[2,64,384]{2,1,0:T(8,128)S(1)}, u32[]{:S(2)}, u32[]{:S(2)}) collective-permute-start(f32[2,64,384]{2,1,0:T(8,128)} %get-tuple-element.41), channel_id=1, source_target_pairs={{0,8},{2,10},{4,12},{6,14},{8,0},{10,2},{12,4},{14,6},{1,9},{3,11}... | collective-permute-start | bytes 589832 | tf_op jit(solution)/shard_map/ppermute | solution.py:269
  63.2 26.5 %collective-permute-start.11 = (f32[2,64,384]{2,1,0:T(8,128)}, f32[2,64,384]{2,1,0:T(8,128)S(1)}, u32[]{:S(2)}, u32[]{:S(2)}) collective-permute-start(f32[2,64,384]{2,1,0:T(8,128)} %get-tuple-element.42), channel_id=1, source_target_pairs={{0,10},{2,8},{4,14},{6,12},{8,2},{10,0},{12,6},{14,4},{1,11},{3,9}... | collective-permute-start | bytes 589832 | tf_op jit(solution)/shard_map/ppermute | solution.py:269
  66.9 30.8 %copy-start.5 = (f32[2,64,384]{2,1,0:T(8,128)}, f32[2,64,384]{2,1,0:T(8,128)S(1)}, u32[]{:S(2)}) copy-start(f32[2,64,384]{2,1,0:T(8,128)S(1)} %collective-permute-done.7.rest_1_) | copy-start | bytes 589828
  66.9 26.7 %collective-permute-start.12 = (f32[2,64,384]{2,1,0:T(8,128)}, f32[2,64,384]{2,1,0:T(8,128)S(1)}, u32[]{:S(2)}, u32[]{:S(2)}) collective-permute-start(f32[2,64,384]{2,1,0:T(8,128)} %get-tuple-element.43), channel_id=1, source_target_pairs={{0,12},{2,14},{4,8},{6,10},{8,4},{10,6},{12,0},{14,2},{1,13},{3,15... | collective-permute-start | bytes 589832 | tf_op jit(solution)/shard_map/ppermute | solution.py:269
  69.7 28.1 %copy-start.7 = (f32[2,64,384]{2,1,0:T(8,128)}, f32[2,64,384]{2,1,0:T(8,128)S(1)}, u32[]{:S(2)}) copy-start(f32[2,64,384]{2,1,0:T(8,128)S(1)} %collective-permute-done.8.rest_2_) | copy-start | bytes 589828
  69.7 26.9 %collective-permute-start.13 = (f32[2,64,384]{2,1,0:T(8,128)}, f32[2,64,384]{2,1,0:T(8,128)S(1)}, u32[]{:S(2)}, u32[]{:S(2)}) collective-permute-start(f32[2,64,384]{2,1,0:T(8,128)} %get-tuple-element.44), channel_id=1, source_target_pairs={{0,14},{2,12},{4,10},{6,8},{8,6},{10,4},{12,2},{14,0},{1,15},{3,13... | collective-permute-start | bytes 589832 | tf_op jit(solution)/shard_map/ppermute | solution.py:269
  74.9 22.9 %copy-start.8 = (f32[2,64,384]{2,1,0:T(8,128)}, f32[2,64,384]{2,1,0:T(8,128)S(1)}, u32[]{:S(2)}) copy-start(f32[2,64,384]{2,1,0:T(8,128)S(1)} %collective-permute-done.9.rest_3_) | copy-start | bytes 589828
  76.7 21.1 %copy-start.9 = (f32[2,64,384]{2,1,0:T(8,128)}, f32[2,64,384]{2,1,0:T(8,128)S(1)}, u32[]{:S(2)}) copy-start(f32[2,64,384]{2,1,0:T(8,128)S(1)} %collective-permute-done.10.rest_4_) | copy-start | bytes 589828
  89.6 8.1 %copy-start.11 = (f32[2,64,384]{2,1,0:T(8,128)}, f32[2,64,384]{2,1,0:T(8,128)S(1)}, u32[]{:S(2)}) copy-start(f32[2,64,384]{2,1,0:T(8,128)S(1)} %collective-permute-done.11.rest_5_) | copy-start | bytes 589828
  93.6 4.2 %copy-start.12 = (f32[2,64,384]{2,1,0:T(8,128)}, f32[2,64,384]{2,1,0:T(8,128)S(1)}, u32[]{:S(2)}) copy-start(f32[2,64,384]{2,1,0:T(8,128)S(1)} %collective-permute-done.12.rest_6_) | copy-start | bytes 589828
  96.6 1.2 %copy-start.13 = (f32[2,64,384]{2,1,0:T(8,128)}, f32[2,64,384]{2,1,0:T(8,128)S(1)}, u32[]{:S(2)}) copy-start(f32[2,64,384]{2,1,0:T(8,128)S(1)} %collective-permute-done.13.rest_7_) | copy-start | bytes 589828

commit v3 on v1

v3 whole, which is shorter than its diff:
```python
import functools

import jax
import jax.numpy as jnp
from jax import lax
from jax.experimental import pallas as pl
from jax.experimental.pallas import tpu as pltpu
from jax.sharding import PartitionSpec as P

TW = 64
CAP = 2
VMEM_LIMIT = 56 * 1024 * 1024
F32 = jnp.float32
BF16 = jnp.bfloat16

HBM_SPEC = pl.BlockSpec(memory_space=pl.ANY)
SMEM_SPEC = pl.BlockSpec(memory_space=pltpu.SMEM)
VMEM_SPEC = pl.BlockSpec(memory_space=pltpu.VMEM)


def params(limit=VMEM_LIMIT):
    return pltpu.CompilerParams(vmem_limit_bytes=limit)


def cost(flops, touched):
    return pl.CostEstimate(flops=flops, bytes_accessed=touched, transcendentals=0)


def clear(ref, count, value):
    @pl.loop(0, count)
    def _(i):
        ref[i] = value


def pack_kernel(owners, per_owner, me_ref, lists_ref, amp_slot_ref, amplitudes, *rest):
    outs, (picked, sems) = rest[: owners - 1], rest[-2:]
    list_length = lists_ref.shape[0] // owners // 2
    me = me_ref[0]
    low = me * per_owner
    clear(picked, owners * CAP, -1)

    @pl.loop(0, owners)
    def _(partner):
        def note(j, count):
            local = amp_slot_ref[lists_ref[partner * 2 * list_length + j]] - low
            mine = (local >= 0) & (local < per_owner)
            picked[jnp.where(mine, partner * CAP + count, owners * CAP)] = local
            return count + mine.astype(jnp.int32)

        lax.fori_loop(0, list_length, note, jnp.int32(0), unroll=8)

    for step in ("start", "wait"):
        for d in range(owners - 1, 0, -1):
            for k in range(CAP):
                local = picked[jnp.bitwise_xor(me, d) * CAP + k]
                moved = pltpu.make_async_copy(
                    amplitudes.at[jnp.maximum(local, 0)], outs[d - 1].at[k], sems.at[d * CAP + k]
                )
                pl.when(local >= 0)(getattr(moved, step))


def maps_kernel(
    owners, per_amp, per_res, me_ref, lists_ref, amp_slot_ref, res_slot_ref,
    amp_from, amp_self, res_to, res_from, res_tile, res_first, seen, taken,
):
    list_length = lists_ref.shape[0] // owners // 2
    me = me_ref[0]
    for ref in (amp_from, res_to, res_from):
        clear(ref, owners * CAP, -1)
    clear(amp_self, CAP, 0)
    clear(res_tile, owners * CAP, 0)
    clear(res_first, owners * CAP, -1)
    clear(taken, per_res, -1)

    def own_list(offset, slot_map, per_owner, place):
        clear(seen, owners, 0)

        @pl.loop(0, list_length)
        def _(g):
            slot = slot_map[lists_ref[me * 2 * list_length + offset + g]]
            owner = slot // per_owner
            d = jnp.bitwise_xor(owner, me)
            count = seen[d]
            place(d * CAP + count, g, slot - owner * per_owner, d, count)
            seen[d] = count + 1

    def place_amp(at, g, local, d, count):
        amp_from[at] = g

        @pl.when(d == 0)
        def _():
            amp_self[count] = local

    def place_res(at, g, local, d, count):
        res_to[at] = g

    own_list(0, amp_slot_ref, per_amp, place_amp)
    own_list(list_length, res_slot_ref, per_res, place_res)
    clear(seen, owners, 0)
    low = me * per_res

    @pl.loop(0, owners * list_length)
    def _(i):
        partner = i // list_length
        tile = lists_ref[partner * 2 * list_length + list_length + i % list_length]
        local = res_slot_ref[tile] - low

        @pl.when((local >= 0) & (local < per_res))
        def _():
            d = jnp.bitwise_xor(partner, me)
            count = seen[d]
            res_from[d * CAP + count] = local
            res_tile[d * CAP + count] = tile
            seen[d] = count + 1

    @pl.loop(0, owners * CAP)
    def _(spot):
        local = res_from[spot]

        @pl.when(local >= 0)
        def _():
            @pl.when(taken[local] < 0)
            def _():
                taken[local] = spot

            res_first[spot] = taken[local]


def sum_kernel(count_ref, tasks_ref, integrals_ref, sums_ref, blank_ref, hits):
    slots = sums_ref.shape[0]
    tasks_here = integrals_ref.shape[0]
    list_length = int(round(slots**0.5))

    @pl.when(pl.program_id(0) == 0)
    def _():
        pair = tasks_ref[0:1, :] * list_length + tasks_ref[1:2, :]
        spot = lax.broadcasted_iota(jnp.int32, (1, tasks_here), 1)
        pair = jnp.where(spot < count_ref[0], pair, -1)
        row = lax.broadcasted_iota(jnp.int32, (slots, tasks_here), 0)
        hits[...] = jnp.where(row == pair, 1.0, 0.0).astype(BF16)

    blank_ref[...] = jnp.zeros_like(blank_ref)
    rows = integrals_ref[...]
    high = rows.astype(BF16)
    low = (rows - high.astype(F32)).astype(BF16)
    sums_ref[...] = jnp.dot(hits[...], high, preferred_element_type=F32) + jnp.dot(
        hits[...], low, preferred_element_type=F32
    )


def product_kernel(owners, amp_from, amp_self, res_to, operator, amplitudes, *rest):
    arrived, outs = rest[: owners - 1], rest[owners - 1 : 2 * owners - 1]
    own, high, low, totals, sems = rest[2 * owners - 1 :]
    rows, columns = high.shape

    def fetch(k):
        source = amplitudes.at[amp_self[k]]
        return pltpu.make_async_copy(source, own.at[k], sems.at[k])

    def split(d, k):
        g = amp_from[d * CAP + k]

        @pl.when(g >= 0)
        def _():
            if d == 0:
                fetch(k).wait()
                values = own[k]
            else:
                values = arrived[d - 1][k]
            top = values.astype(BF16)
            spot = pl.ds(pl.multiple_of(g * TW, TW), TW)
            high[spot, :] = top
            low[spot, :] = (values - top.astype(F32)).astype(BF16)

    for k in range(CAP):
        pl.when(amp_from[k] >= 0)(fetch(k).start)
    for d in range(owners - 1, -1, -1):
        for k in range(CAP):
            split(d, k)
    step = min(rows, 8 * TW)

    @pl.loop(0, rows // step)
    def _(i):
        left = operator[pl.ds(pl.multiple_of(i * step, step), step), :]
        left_high = left.astype(BF16)
        left_low = (left - left_high.astype(F32)).astype(BF16)
        total = jnp.dot(left_high, low[...], preferred_element_type=F32)
        total += jnp.dot(left_low, high[...], preferred_element_type=F32)
        total += jnp.dot(left_high, high[...], preferred_element_type=F32)
        totals[pl.ds(i * (step // TW), step // TW)] = total.reshape(step // TW, TW, columns)

    for d in range(owners):
        for k in range(CAP):
            g = res_to[d * CAP + k]

            @pl.when(g >= 0)
            def _():
                outs[d][k] = totals[g]


def final_kernel(owners, tiles, res_from, res_tile, res_first, window, pair, virt, *rest):
    arrived, (_, out, sums, sems) = rest[:owners], rest[-4:]
    spots = [(d, k, d * CAP + k) for d in range(owners) for k in range(CAP)]
    for d, k, spot in spots:
        first = res_first[spot]

        @pl.when(first == spot)
        def _():
            sums[spot] = arrived[d][k]

        @pl.when((first >= 0) & (first < spot))
        def _():
            sums[first] = sums[first] + arrived[d][k]

    def write(spot):
        return pltpu.make_async_copy(sums.at[spot], out.at[jnp.maximum(res_from[spot], 0)], sems.at[spot])

    for d, k, spot in spots:

        @pl.when(res_first[spot] == spot)
        def _():
            tile = res_tile[spot]
            base = pair[...] - window[tile // tiles]
            below = base - jnp.concatenate([virt[tile % tiles]] * (base.shape[1] // 128), axis=1)
            sums[spot] = sums[spot] / below
            write(spot).start()

    for d, k, spot in spots:
        pl.when(res_first[spot] == spot)(write(spot).wait)


def local(
    tasks,
    task_count,
    integrals,
    amplitudes,
    amp_slot,
    need_amp,
    res_slot,
    needed_residual_tiles,
    pair_energy,
    virt_energy,
    window_energy,
):
    owners = lax.axis_size("tile")
    me = lax.axis_index("tile").astype(jnp.int32)
    per_amp, _, row_count = amplitudes.shape
    per_res = res_slot.shape[0] // owners
    list_length = need_amp.shape[0]
    tile_count = virt_energy.shape[0] // TW
    slots = list_length * list_length
    task_slots = tasks.shape[1]

    own_lists = jnp.concatenate([need_amp, needed_residual_tiles])
    spots = jnp.arange(owners, dtype=jnp.int32)[:, None] == me
    lists = lax.psum(jnp.where(spots, own_lists[None, :], 0), "tile").reshape(-1)
    me_ref = me.reshape(1)

    def exchange(buffers):
        moved = {}
        for d in range(owners - 1, 0, -1):
            moved[d] = lax.ppermute(buffers[d - 1], "tile", [(i, i ^ d) for i in range(owners)])
        return [moved[d] for d in range(1, owners)]

    piece = pltpu.VMEM((CAP, TW, row_count), F32)
    packed = pl.pallas_call(
        functools.partial(pack_kernel, owners, per_amp),
        out_shape=[piece] * (owners - 1),
        in_specs=[SMEM_SPEC] * 3 + [HBM_SPEC],
        out_specs=[VMEM_SPEC] * (owners - 1),
        scratch_shapes=[
            pltpu.SMEM((owners * CAP + 1,), jnp.int32),
            pltpu.SemaphoreType.DMA((owners * CAP,)),
        ],
        compiler_params=params(),
        cost_estimate=cost(0, 2 * list_length * TW * row_count * 4),
        name="pack_tiles",
    )(me_ref, lists, amp_slot, amplitudes)
    fetched = exchange(packed)

    small = jax.ShapeDtypeStruct((owners * CAP,), jnp.int32)
    amp_from, amp_self, res_to, res_from, res_tile, res_first = pl.pallas_call(
        functools.partial(maps_kernel, owners, per_amp, per_res),
        out_shape=[small, jax.ShapeDtypeStruct((CAP,), jnp.int32), small, small, small, small],
        in_specs=[SMEM_SPEC] * 4,
        out_specs=[SMEM_SPEC] * 6,
        scratch_shapes=[pltpu.SMEM((owners,), jnp.int32), pltpu.SMEM((per_res,), jnp.int32)],
        compiler_params=params(),
        name="list_maps",
    )(me_ref, lists, amp_slot, res_slot)

    block = 512
    steps = TW * TW // block
    blank_rows = per_res * TW // steps
    sums, blank = pl.pallas_call(
        sum_kernel,
        grid=(steps,),
        out_shape=[
            jax.ShapeDtypeStruct((slots, TW * TW), F32),
            jax.ShapeDtypeStruct((per_res * TW, row_count), F32),
        ],
        in_specs=[
            SMEM_SPEC,
            pl.BlockSpec((2, task_slots), lambda i: (0, 0)),
            pl.BlockSpec((task_slots, block), lambda i: (0, i)),
        ],
        out_specs=[
            pl.BlockSpec((slots, block), lambda i: (0, i)),
            pl.BlockSpec((blank_rows, row_count), lambda i: (i, 0)),
        ],
        scratch_shapes=[pltpu.VMEM((slots, task_slots), BF16)],
        compiler_params=params(),
        cost_estimate=cost(4 * slots * task_slots * TW * TW, (task_slots + slots) * TW * TW * 4),
        name="sum_integrals",
    )(task_count, tasks, integrals)
    operator = (
        sums.reshape(list_length, list_length, TW, TW)
        .transpose(0, 2, 1, 3)
        .reshape(list_length * TW, list_length * TW)
    )

    virt = jnp.broadcast_to(virt_energy.reshape(tile_count, TW, 1), (tile_count, TW, 128))
    pair = pair_energy.reshape(1, row_count)
    blank = blank.reshape(per_res, TW, row_count)
    operator, virt, pair = lax.optimization_barrier((operator, virt, pair))
    depth = list_length * TW
    products = pl.pallas_call(
        functools.partial(product_kernel, owners),
        out_shape=[piece] * owners,
        in_specs=[SMEM_SPEC] * 3 + [VMEM_SPEC, HBM_SPEC] + [VMEM_SPEC] * (owners - 1),
        out_specs=[VMEM_SPEC] * owners,
        scratch_shapes=[
            pltpu.VMEM((CAP, TW, row_count), F32),
            pltpu.VMEM((depth, row_count), BF16),
            pltpu.VMEM((depth, row_count), BF16),
            pltpu.VMEM((list_length, TW, row_count), F32),
            pltpu.SemaphoreType.DMA((CAP,)),
        ],
        compiler_params=params(),
        cost_estimate=cost(6 * depth * depth * row_count, 4 * depth * (depth + 2 * row_count)),
        name="multiply_tiles",
    )(amp_from, amp_self, res_to, operator, amplitudes, *fetched)
    returned = [products[0]] + exchange(products[1:])
    return pl.pallas_call(
        functools.partial(final_kernel, owners, tile_count),
        out_shape=jax.ShapeDtypeStruct((per_res, TW, row_count), F32),
        in_specs=[SMEM_SPEC] * 4 + [VMEM_SPEC] * (2 + owners) + [HBM_SPEC],
        out_specs=HBM_SPEC,
        scratch_shapes=[
            pltpu.VMEM((owners * CAP, TW, row_count), F32),
            pltpu.SemaphoreType.DMA((owners * CAP,)),
        ],
        input_output_aliases={6 + owners: 0},
        compiler_params=params(),
        cost_estimate=cost(0, per_res * TW * row_count * 4),
        name="finish_tiles",
    )(res_from, res_tile, res_first, window_energy, pair, virt, *returned, blank)


def solution(mesh):
    in_specs = (
        P(None, ("mol", "tile")),
        P(("mol", "tile")),
        P(("mol", "tile"), None),
        P(("mol", "tile"), None, "rep"),
        P("mol"),
        P(("mol", "tile")),
        P("mol"),
        P(("mol", "tile")),
        P(("mol", "rep")),
        P("mol"),
        P("mol"),
    )
    out_specs = P(("mol", "tile"), None, "rep")
    return jax.shard_map(local, mesh=mesh, in_specs=in_specs, out_specs=out_specs, check_vma=False)
```

time: 135 us -> 96.6 us (0.72); the launches traced: 137 us -> 95.7 us
  Pallas kernels: 60.1 us -> 21.7 us
  waiting for transfers between devices: 35.8 us -> 34 us
  starting transfers between devices: 18.7 us -> 17 us
    pallas_call x4, Pallas kernels: 56.3 us -> 17.4 us  [the longest x1 8.12 us: local(): pl.pallas_call(sum_kernel, grid=(steps,), out_shape=[jax.ShapeDtypeStruct...]
    ppermute x14, waiting for transfers between devices: 35.8 us -> 34 us  [exchange(): lax.ppermute(buffers[d - 1], 'tile', [(i, i ^ d) for i in range(owners)])]
    ppermute x14, starting transfers between devices: 18.7 us -> 17 us  [exchange(): lax.ppermute(buffers[d - 1], 'tile', [(i, i ^ d) for i in range(owners)])]
  transfers between devices with their start and end apart: 14 -> 14, of which waited for: 9 -> 10; matrix products, arithmetic and copies ran while one was open for 6% -> 9% of each run, Pallas kernels for 9% -> 13%
where the time goes in v3:
time: 96.6 us; the launch traced here: 95.7 us
  waiting for transfers between devices  34 us (35%)
  Pallas kernels  21.7 us (22%)
  starting transfers between devices  17 us (18%)
  blocking collectives  11 us (11%)
  local copies, waits for them, and re-layouts  10.5 us (11%)
    ppermute x14, waiting for transfers between devices, exchange(): lax.ppermute(buffers[d - 1], 'tile', [(i, i ^ d) for i in range(owners)])  34 us
    ppermute x14, starting transfers between devices, exchange(): lax.ppermute(buffers[d - 1], 'tile', [(i, i ^ d) for i in range(owners)])  17 us
    psum x1, blocking collectives, local(): lax.psum(jnp.where(spots, own_lists[None, :], 0), 'tile').reshape(-1)  11 us
    pallas_call x1, Pallas kernels, local(): pl.pallas_call(sum_kernel, grid=(steps,), out_shape=[jax.ShapeDtypeStruct...  8.12 us
    reshape x2, local copies, waits for them, and re-layouts, local(): sums.reshape(list_length, list_length, TW, TW).transpose(0, 2, 1, 3)  4.53 us
    pallas_call x1, Pallas kernels, local(): pl.pallas_call(functools.partial(maps_kernel, owners, per_amp, per_res),...  4.26 us
    pallas_call x1, Pallas kernels, local(): pl.pallas_call(functools.partial(product_kernel, owners), out_shape=[piec...  3.84 us
    pallas_call x1, Pallas kernels, local(): pl.pallas_call(functools.partial(final_kernel, owners, tile_count), out_s...  3.02 us
  transfers between devices with their start and end apart: 14, of which 10 were waited for; matrix products, arithmetic and copies ran while one was open for 9% of the time, Pallas kernels for 13%

profile of v3, /device:TPU:12, one launch (start us, length us, event | category | flops | bytes accessed | tf_op | source)
XLA Modules:
  0.0 95.7 jit_solution(13791237427065701670)
XLA Ops:
  0.0 0.7 pad_add_fusion
  0.8 0.1 broadcast_select_fusion
  0.8 0.1 reshape.27
  0.9 11.0 %psum.7.lists_ref = s32[128]{0:T(128)} all-reduce(s32[128]{0:T(128)S(1)} %reshape.27), channel_id=1, replica_groups=mesh['mol'=2,'tile'=8,'rep'=2] {'tile'}, use_global_device_ids=true, to_apply=%region_0.1 | all-reduce | flops 128 | bytes 1024 | tf_op jit(solution)/shard_map/psum | solution.py:256
  11.9 2.4 %pack_tiles.1 = (f32[2,64,384]{2,1,0:T(8,128)S(1)}, f32[2,64,384]{2,1,0:T(8,128)S(1)}, f32[2,64,384]{2,1,0:T(8,128)S(1)}, f32[2,64,384]{2,1,0:T(8,128)S(1)}, f32...) custom-call(s32[1]{0:T(128)} %bitcast.me_ref, s32[128]{0:T(128)} %psum.7.lists_ref, ...), custom_call_target="tpu_custom_call" | custom-call | bytes 1572864 | tf_op jit(solution)/shard_map/pack_tiles/pallas_call | solution.py:266
  14.3 0.6 collective-permute-start
  15.0 1.4 %collective-permute-start.1 = (f32[2,64,384]{2,1,0:T(8,128)S(1)}, f32[2,64,384]{2,1,0:T(8,128)S(1)}, u32[]{:S(2)}, u32[]{:S(2)}) collective-permute-start(f32[2,64,384]{2,1,0:T(8,128)S(1)} %get-tuple-element.42), channel_id=1, source_target_pairs={{0,4},{2,6},{4,0},{6,2},{8,12},{10,14},{12,8},{14,10},{1,5},{3,7},... | collective-permute-start | bytes 589832 | tf_op jit(solution)/shard_map/ppermute | solution.py:262
  16.4 1.5 %collective-permute-start.2 = (f32[2,64,384]{2,1,0:T(8,128)S(1)}, f32[2,64,384]{2,1,0:T(8,128)}, u32[]{:S(2)}, u32[]{:S(2)}) collective-permute-start(f32[2,64,384]{2,1,0:T(8,128)S(1)} %get-tuple-element.43), channel_id=1, source_target_pairs={{0,6},{2,4},{4,2},{6,0},{8,14},{10,12},{12,10},{14,8},{1,7},{3,5},... | collective-permute-start | bytes 589832 | tf_op jit(solution)/shard_map/ppermute | solution.py:262
  17.9 0.3 collective-permute-start.3
  18.2 2.7 %collective-permute-start.4 = (f32[2,64,384]{2,1,0:T(8,128)S(1)}, f32[2,64,384]{2,1,0:T(8,128)}, u32[]{:S(2)}, u32[]{:S(2)}) collective-permute-start(f32[2,64,384]{2,1,0:T(8,128)S(1)} %get-tuple-element.45), channel_id=1, source_target_pairs={{0,10},{2,8},{4,14},{6,12},{8,2},{10,0},{12,6},{14,4},{1,11},{3,9}... | collective-permute-start | bytes 589832 | tf_op jit(solution)/shard_map/ppermute | solution.py:262
  20.8 0.9 collective-permute-done.rest_0_
  21.7 0.0 copy-start.1
  21.7 0.2 collective-permute-start.5
  21.9 0.9 collective-permute-done.1.rest_1_
  22.8 0.0 copy-start.2
  22.8 2.7 %collective-permute-start.6 = (f32[2,64,384]{2,1,0:T(8,128)S(1)}, f32[2,64,384]{2,1,0:T(8,128)}, u32[]{:S(2)}, u32[]{:S(2)}) collective-permute-start(f32[2,64,384]{2,1,0:T(8,128)S(1)} %get-tuple-element.47), channel_id=1, source_target_pairs={{0,14},{2,12},{4,10},{6,8},{8,6},{10,4},{12,2},{14,0},{1,15},{3,13... | collective-permute-start | bytes 589832 | tf_op jit(solution)/shard_map/ppermute | solution.py:262
  25.5 4.3 %list_maps.1 = (s32[16]{0:T(128)}, s32[2]{0:T(128)}, s32[16]{0:T(128)}, s32[16]{0:T(128)}, s32[16]{0:T(128)}, /*index=5*/s32[16]{0:T(128)}) custom-call(s32[1]{0:T(128)} %bitcast.me_ref, s32[128]{0:T(128)} %psum.7.lists_ref, s32[200]{0:T(256)} %amp_slot_ref.3, s32[200]{0:T(256)} %res_slot_ref.1), custom_call_target="tpu_custom_call" | custom-call | tf_op jit(solution)/shard_map/list_maps/pallas_call | solution.py:282
  30.4 8.1 %sum_integrals.1 = (f32[64,4096]{1,0:T(8,128)}, f32[1600,384]{1,0:T(8,128)}) custom-call(s32[1]{0:T(128)S(6)} %copy.17.count_ref, s32[2,512]{1,0:T(2,128)} %tasks_ref.1, f32[512,4096]{1,0:T(8,128)} %integrals_ref.1), custom_call_target="tpu_custom_call" | custom-call | flops 536870912 | bytes 9437184 | tf_op jit(solution)/shard_map/sum_integrals/pallas_call | solution.py:295
  38.5 0.0 copy-done.1
  38.5 0.0 copy-done.2
  38.6 2.0 %reshape.28 = f32[8,8,64,64]{3,2,1,0:T(8,128)S(1)} reshape(f32[64,4096]{1,0:T(8,128)} %get-tuple-element.34) | data formatting | bytes 2097152 | tf_op jit(solution)/shard_map/reshape | solution.py:317
  40.6 2.5 %copy.15 = f32[8,8,64,64]{3,1,2,0:T(8,128)} copy(f32[8,8,64,64]{3,2,1,0:T(8,128)S(1)} %reshape.28) | data formatting | bytes 2097152 | tf_op jit(solution)/shard_map/reshape | solution.py:317
  43.1 0.0 copy-start.10
  43.1 0.0 copy-start.11
  43.1 2.7 %reshape.29.operator = f32[512,512]{1,0:T(8,128)} reshape(f32[8,64,8,64]{3,2,1,0:T(8,128)} %bitcast.7) | data formatting | bytes 2097152 | tf_op jit(solution)/shard_map/reshape | solution.py:319
  45.8 0.0 copy-done.10
  45.8 0.1 broadcast_in_dim.32
  45.9 0.0 copy-done.11
  45.9 0.6 reshape.30.pair
  46.5 1.2 %broadcast_in_dim.33.virt = f32[25,64,128]{2,1,0:T(8,128)} broadcast(f32[25,64]{1,0:T(8,128)S(1)} %broadcast_in_dim.32), dimensions={0,1} | broadcast | bytes 825600 | tf_op jit(solution)/shard_map/broadcast_in_dim | solution.py:322
  47.7 0.0 collective-permute-done.2.rest_2_
  47.7 0.0 collective-permute-done.3.rest_3_
  47.7 0.0 collective-permute-done.4.rest_4_
  47.7 1.7 %collective-permute-done.5.rest_5_ = f32[2,64,384]{2,1,0:T(8,128)} collective-permute-done((f32[2,64,384]{2,1,0:T(8,128)S(1)}, f32[2,64,384]{2,1,0:T(8,128)}, u32[]{:S(2)}, u32[]{:S(2)}) %collective-permute-start.5) | collective-permute-done | bytes 196640 | tf_op jit(solution)/shard_map/ppermute | solution.py:262
  49.4 2.0 %collective-permute-done.6.rest_6_ = f32[2,64,384]{2,1,0:T(8,128)} collective-permute-done((f32[2,64,384]{2,1,0:T(8,128)S(1)}, f32[2,64,384]{2,1,0:T(8,128)}, u32[]{:S(2)}, u32[]{:S(2)}) %collective-permute-start.6) | collective-permute-done | bytes 196640 | tf_op jit(solution)/shard_map/ppermute | solution.py:262
  51.3 3.8 %multiply_tiles.1 = (f32[2,64,384]{2,1,0:T(8,128)S(1)}, f32[2,64,384]{2,1,0:T(8,128)S(1)}, f32[2,64,384]{2,1,0:T(8,128)S(1)}, f32[2,64,384]{2,1,0:T(8,128)S(1)},...) custom-call(s32[16]{0:T(128)} %get-tuple-element.37.amp_from, ...), custom_call_target="tpu_custom_call" | custom-call | flops 603979776 | bytes 2621440 | tf_op jit(solution)/shard_map/multiply_tiles/pallas_call | solution.py:327
  55.2 0.0 copy-start
  55.2 0.7 copy-done
  55.9 0.9 collective-permute-start.7
  56.7 0.0 collective-permute-start.8
  56.7 2.6 %collective-permute-start.9 = (f32[2,64,384]{2,1,0:T(8,128)S(1)}, f32[2,64,384]{2,1,0:T(8,128)S(1)}, u32[]{:S(2)}, u32[]{:S(2)}) collective-permute-start(f32[2,64,384]{2,1,0:T(8,128)S(1)} %get-tuple-element.51), channel_id=1, source_target_pairs={{0,6},{2,4},{4,2},{6,0},{8,14},{10,12},{12,10},{14,8},{1,7},{3,5},... | collective-permute-start | bytes 589832 | tf_op jit(solution)/shard_map/ppermute | solution.py:262
  59.4 1.6 %collective-permute-start.10 = (f32[2,64,384]{2,1,0:T(8,128)S(1)}, f32[2,64,384]{2,1,0:T(8,128)S(1)}, u32[]{:S(2)}, u32[]{:S(2)}) collective-permute-start(f32[2,64,384]{2,1,0:T(8,128)S(1)} %get-tuple-element.52), channel_id=1, source_target_pairs={{0,8},{2,10},{4,12},{6,14},{8,0},{10,2},{12,4},{14,6},{1,9},{3,11}... | collective-permute-start | bytes 589832 | tf_op jit(solution)/shard_map/ppermute | solution.py:262
  61.0 1.6 %collective-permute-start.11 = (f32[2,64,384]{2,1,0:T(8,128)S(1)}, f32[2,64,384]{2,1,0:T(8,128)S(1)}, u32[]{:S(2)}, u32[]{:S(2)}) collective-permute-start(f32[2,64,384]{2,1,0:T(8,128)S(1)} %get-tuple-element.53), channel_id=1, source_target_pairs={{0,10},{2,8},{4,14},{6,12},{8,2},{10,0},{12,6},{14,4},{1,11},{3,9}... | collective-permute-start | bytes 589832 | tf_op jit(solution)/shard_map/ppermute | solution.py:262
  62.6 0.0 collective-permute-done.7.rest_1_
  62.6 0.0 copy-start.3
  62.6 0.5 collective-permute-start.12
  63.1 2.0 %collective-permute-done.8.rest_2_ = f32[2,64,384]{2,1,0:T(8,128)S(1)} collective-permute-done((f32[2,64,384]{2,1,0:T(8,128)S(1)}, f32[2,64,384]{2,1,0:T(8,128)S(1)}, u32[]{:S(2)}, u32[]{:S(2)}) %collective-permute-start.8) | collective-permute-done | bytes 196640 | tf_op jit(solution)/shard_map/ppermute | solution.py:262
  65.0 0.0 copy-start.4
  65.0 0.4 collective-permute-start.13
  65.5 5.0 %collective-permute-done.9.rest_3_ = f32[2,64,384]{2,1,0:T(8,128)S(1)} collective-permute-done((f32[2,64,384]{2,1,0:T(8,128)S(1)}, f32[2,64,384]{2,1,0:T(8,128)S(1)}, u32[]{:S(2)}, u32[]{:S(2)}) %collective-permute-start.9) | collective-permute-done | bytes 196640 | tf_op jit(solution)/shard_map/ppermute | solution.py:262
  70.5 0.0 copy-start.5
  70.5 11.4 %collective-permute-done.10.rest_4_ = f32[2,64,384]{2,1,0:T(8,128)S(1)} collective-permute-done((f32[2,64,384]{2,1,0:T(8,128)S(1)}, f32[2,64,384]{2,1,0:T(8,128)S(1)}, u32[]{:S(2)}, u32[]{:S(2)}) %collective-permute-start.10) | collective-permute-done | bytes 196640 | tf_op jit(solution)/shard_map/ppermute | solution.py:262
  81.9 0.0 copy-start.6
  81.9 4.2 %collective-permute-done.11.rest_5_ = f32[2,64,384]{2,1,0:T(8,128)S(1)} collective-permute-done((f32[2,64,384]{2,1,0:T(8,128)S(1)}, f32[2,64,384]{2,1,0:T(8,128)S(1)}, u32[]{:S(2)}, u32[]{:S(2)}) %collective-permute-start.11) | collective-permute-done | bytes 196640 | tf_op jit(solution)/shard_map/ppermute | solution.py:262
  86.1 2.9 %collective-permute-done.12.rest_6_ = f32[2,64,384]{2,1,0:T(8,128)S(1)} collective-permute-done((f32[2,64,384]{2,1,0:T(8,128)S(1)}, f32[2,64,384]{2,1,0:T(8,128)S(1)}, u32[]{:S(2)}, u32[]{:S(2)}) %collective-permute-start.12) | collective-permute-done | bytes 196640 | tf_op jit(solution)/shard_map/ppermute | solution.py:262
  89.1 3.0 %collective-permute-done.13.rest_7_ = f32[2,64,384]{2,1,0:T(8,128)S(1)} collective-permute-done((f32[2,64,384]{2,1,0:T(8,128)S(1)}, f32[2,64,384]{2,1,0:T(8,128)S(1)}, u32[]{:S(2)}, u32[]{:S(2)}) %collective-permute-start.13) | collective-permute-done | bytes 196640 | tf_op jit(solution)/shard_map/ppermute | solution.py:262
  92.1 0.0 copy-done.3
  92.1 0.0 copy-done.4
  92.1 0.0 copy-done.5
  92.1 0.0 copy-done.6
  92.1 0.0 copy-done.7
  92.1 0.0 copy-done.8
  92.1 0.6 copy-done.9
  92.7 3.0 %finish_tiles.1 = f32[25,64,384]{2,1,0:T(8,128)} custom-call(s32[16]{0:T(128)} %get-tuple-element.31.res_from, s32[16]{0:T(128)} %get-tuple-element.32.res_tile, s32[16]{0:T(128)} %get-tuple-element.33.res_first, f32[8]{0:T(128)} %window.1, f32[1,384]{1,0:T(1,128)} %reshape.30.pair, ...), custom_call_target="tpu_custom_call", output_to_operand_aliasing={{}: (14, {})} | custom-call | bytes 2457600 | tf_op jit(solution)/shard_map/finish_tiles/pallas_call | solution.py:344
  (4 shorter events, 0.0 us)
Async XLA Ops:
  14.3 7.4 %collective-permute-start = (f32[2,64,384]{2,1,0:T(8,128)S(1)}, f32[2,64,384]{2,1,0:T(8,128)S(1)}, u32[]{:S(2)}, u32[]{:S(2)}) collective-permute-start(f32[2,64,384]{2,1,0:T(8,128)S(1)} %get-tuple-element.41), channel_id=1, source_target_pairs={{0,2},{2,0},{4,6},{6,4},{8,10},{10,8},{12,14},{14,12},{1,3},{3,1},... | collective-permute-start | bytes 589832 | tf_op jit(solution)/shard_map/ppermute | solution.py:262
  15.0 7.8 %collective-permute-start.1 = (f32[2,64,384]{2,1,0:T(8,128)S(1)}, f32[2,64,384]{2,1,0:T(8,128)S(1)}, u32[]{:S(2)}, u32[]{:S(2)}) collective-permute-start(f32[2,64,384]{2,1,0:T(8,128)S(1)} %get-tuple-element.42), channel_id=1, source_target_pairs={{0,4},{2,6},{4,0},{6,2},{8,12},{10,14},{12,8},{14,10},{1,5},{3,7},... | collective-permute-start | bytes 589832 | tf_op jit(solution)/shard_map/ppermute | solution.py:262
  16.4 31.2 %collective-permute-start.2 = (f32[2,64,384]{2,1,0:T(8,128)S(1)}, f32[2,64,384]{2,1,0:T(8,128)}, u32[]{:S(2)}, u32[]{:S(2)}) collective-permute-start(f32[2,64,384]{2,1,0:T(8,128)S(1)} %get-tuple-element.43), channel_id=1, source_target_pairs={{0,6},{2,4},{4,2},{6,0},{8,14},{10,12},{12,10},{14,8},{1,7},{3,5},... | collective-permute-start | bytes 589832 | tf_op jit(solution)/shard_map/ppermute | solution.py:262
  17.9 29.8 %collective-permute-start.3 = (f32[2,64,384]{2,1,0:T(8,128)S(1)}, f32[2,64,384]{2,1,0:T(8,128)}, u32[]{:S(2)}, u32[]{:S(2)}) collective-permute-start(f32[2,64,384]{2,1,0:T(8,128)S(1)} %get-tuple-element.44), channel_id=1, source_target_pairs={{0,8},{2,10},{4,12},{6,14},{8,0},{10,2},{12,4},{14,6},{1,9},{3,11}... | collective-permute-start | bytes 589832 | tf_op jit(solution)/shard_map/ppermute | solution.py:262
  18.2 29.5 %collective-permute-start.4 = (f32[2,64,384]{2,1,0:T(8,128)S(1)}, f32[2,64,384]{2,1,0:T(8,128)}, u32[]{:S(2)}, u32[]{:S(2)}) collective-permute-start(f32[2,64,384]{2,1,0:T(8,128)S(1)} %get-tuple-element.45), channel_id=1, source_target_pairs={{0,10},{2,8},{4,14},{6,12},{8,2},{10,0},{12,6},{14,4},{1,11},{3,9}... | collective-permute-start | bytes 589832 | tf_op jit(solution)/shard_map/ppermute | solution.py:262
  21.7 16.8 %copy-start.1 = (f32[2,64,384]{2,1,0:T(8,128)}, f32[2,64,384]{2,1,0:T(8,128)S(1)}, u32[]{:S(2)}) copy-start(f32[2,64,384]{2,1,0:T(8,128)S(1)} %collective-permute-done.rest_0_) | copy-start | bytes 589828
  21.7 27.7 %collective-permute-start.5 = (f32[2,64,384]{2,1,0:T(8,128)S(1)}, f32[2,64,384]{2,1,0:T(8,128)}, u32[]{:S(2)}, u32[]{:S(2)}) collective-permute-start(f32[2,64,384]{2,1,0:T(8,128)S(1)} %get-tuple-element.46), channel_id=1, source_target_pairs={{0,12},{2,14},{4,8},{6,10},{8,4},{10,6},{12,0},{14,2},{1,13},{3,15... | collective-permute-start | bytes 589832 | tf_op jit(solution)/shard_map/ppermute | solution.py:262
  22.8 15.7 %copy-start.2 = (f32[2,64,384]{2,1,0:T(8,128)}, f32[2,64,384]{2,1,0:T(8,128)S(1)}, u32[]{:S(2)}) copy-start(f32[2,64,384]{2,1,0:T(8,128)S(1)} %collective-permute-done.1.rest_1_) | copy-start | bytes 589828
  22.8 28.5 %collective-permute-start.6 = (f32[2,64,384]{2,1,0:T(8,128)S(1)}, f32[2,64,384]{2,1,0:T(8,128)}, u32[]{:S(2)}, u32[]{:S(2)}) collective-permute-start(f32[2,64,384]{2,1,0:T(8,128)S(1)} %get-tuple-element.47), channel_id=1, source_target_pairs={{0,14},{2,12},{4,10},{6,8},{8,6},{10,4},{12,2},{14,0},{1,15},{3,13... | collective-permute-start | bytes 589832 | tf_op jit(solution)/shard_map/ppermute | solution.py:262
  43.1 2.7 %copy-start.10 = (f32[1600]{0:T(1024)S(1)}, f32[1600]{0:T(1024)}, u32[]{:S(2)}) copy-start(f32[1600]{0:T(1024)} %param.20) | copy-start | bytes 19204
  43.1 2.8 %copy-start.11 = (f32[384]{0:T(512)S(1)}, f32[384]{0:T(512)}, u32[]{:S(2)}) copy-start(f32[384]{0:T(512)} %param.19) | copy-start | bytes 4612
  55.2 0.7 copy-start
  55.9 6.7 %collective-permute-start.7 = (f32[2,64,384]{2,1,0:T(8,128)S(1)}, f32[2,64,384]{2,1,0:T(8,128)S(1)}, u32[]{:S(2)}, u32[]{:S(2)}) collective-permute-start(f32[2,64,384]{2,1,0:T(8,128)S(1)} %get-tuple-element.49), channel_id=1, source_target_pairs={{0,2},{2,0},{4,6},{6,4},{8,10},{10,8},{12,14},{14,12},{1,3},{3,1},... | collective-permute-start | bytes 589832 | tf_op jit(solution)/shard_map/ppermute | solution.py:262
  56.7 8.3 %collective-permute-start.8 = (f32[2,64,384]{2,1,0:T(8,128)S(1)}, f32[2,64,384]{2,1,0:T(8,128)S(1)}, u32[]{:S(2)}, u32[]{:S(2)}) collective-permute-start(f32[2,64,384]{2,1,0:T(8,128)S(1)} %get-tuple-element.50), channel_id=1, source_target_pairs={{0,4},{2,6},{4,0},{6,2},{8,12},{10,14},{12,8},{14,10},{1,5},{3,7},... | collective-permute-start | bytes 589832 | tf_op jit(solution)/shard_map/ppermute | solution.py:262
  56.7 13.7 %collective-permute-start.9 = (f32[2,64,384]{2,1,0:T(8,128)S(1)}, f32[2,64,384]{2,1,0:T(8,128)S(1)}, u32[]{:S(2)}, u32[]{:S(2)}) collective-permute-start(f32[2,64,384]{2,1,0:T(8,128)S(1)} %get-tuple-element.51), channel_id=1, source_target_pairs={{0,6},{2,4},{4,2},{6,0},{8,14},{10,12},{12,10},{14,8},{1,7},{3,5},... | collective-permute-start | bytes 589832 | tf_op jit(solution)/shard_map/ppermute | solution.py:262
  59.4 22.5 %collective-permute-start.10 = (f32[2,64,384]{2,1,0:T(8,128)S(1)}, f32[2,64,384]{2,1,0:T(8,128)S(1)}, u32[]{:S(2)}, u32[]{:S(2)}) collective-permute-start(f32[2,64,384]{2,1,0:T(8,128)S(1)} %get-tuple-element.52), channel_id=1, source_target_pairs={{0,8},{2,10},{4,12},{6,14},{8,0},{10,2},{12,4},{14,6},{1,9},{3,11}... | collective-permute-start | bytes 589832 | tf_op jit(solution)/shard_map/ppermute | solution.py:262
  61.0 25.1 %collective-permute-start.11 = (f32[2,64,384]{2,1,0:T(8,128)S(1)}, f32[2,64,384]{2,1,0:T(8,128)S(1)}, u32[]{:S(2)}, u32[]{:S(2)}) collective-permute-start(f32[2,64,384]{2,1,0:T(8,128)S(1)} %get-tuple-element.53), channel_id=1, source_target_pairs={{0,10},{2,8},{4,14},{6,12},{8,2},{10,0},{12,6},{14,4},{1,11},{3,9}... | collective-permute-start | bytes 589832 | tf_op jit(solution)/shard_map/ppermute | solution.py:262
  62.6 29.5 %copy-start.3 = (f32[2,64,384]{2,1,0:T(8,128)}, f32[2,64,384]{2,1,0:T(8,128)S(1)}, u32[]{:S(2)}) copy-start(f32[2,64,384]{2,1,0:T(8,128)S(1)} %collective-permute-done.7.rest_1_) | copy-start | bytes 589828
  62.6 26.5 %collective-permute-start.12 = (f32[2,64,384]{2,1,0:T(8,128)S(1)}, f32[2,64,384]{2,1,0:T(8,128)S(1)}, u32[]{:S(2)}, u32[]{:S(2)}) collective-permute-start(f32[2,64,384]{2,1,0:T(8,128)S(1)} %get-tuple-element.54), channel_id=1, source_target_pairs={{0,12},{2,14},{4,8},{6,10},{8,4},{10,6},{12,0},{14,2},{1,13},{3,15... | collective-permute-start | bytes 589832 | tf_op jit(solution)/shard_map/ppermute | solution.py:262
  65.0 27.0 %copy-start.4 = (f32[2,64,384]{2,1,0:T(8,128)}, f32[2,64,384]{2,1,0:T(8,128)S(1)}, u32[]{:S(2)}) copy-start(f32[2,64,384]{2,1,0:T(8,128)S(1)} %collective-permute-done.8.rest_2_) | copy-start | bytes 589828
  65.0 27.0 %collective-permute-start.13 = (f32[2,64,384]{2,1,0:T(8,128)S(1)}, f32[2,64,384]{2,1,0:T(8,128)S(1)}, u32[]{:S(2)}, u32[]{:S(2)}) collective-permute-start(f32[2,64,384]{2,1,0:T(8,128)S(1)} %get-tuple-element.55), channel_id=1, source_target_pairs={{0,14},{2,12},{4,10},{6,8},{8,6},{10,4},{12,2},{14,0},{1,15},{3,13... | collective-permute-start | bytes 589832 | tf_op jit(solution)/shard_map/ppermute | solution.py:262
  70.5 21.6 %copy-start.5 = (f32[2,64,384]{2,1,0:T(8,128)}, f32[2,64,384]{2,1,0:T(8,128)S(1)}, u32[]{:S(2)}) copy-start(f32[2,64,384]{2,1,0:T(8,128)S(1)} %collective-permute-done.9.rest_3_) | copy-start | bytes 589828
  81.9 10.2 %copy-start.6 = (f32[2,64,384]{2,1,0:T(8,128)}, f32[2,64,384]{2,1,0:T(8,128)S(1)}, u32[]{:S(2)}) copy-start(f32[2,64,384]{2,1,0:T(8,128)S(1)} %collective-permute-done.10.rest_4_) | copy-start | bytes 589828
  86.1 6.0 %copy-start.7 = (f32[2,64,384]{2,1,0:T(8,128)}, f32[2,64,384]{2,1,0:T(8,128)S(1)}, u32[]{:S(2)}) copy-start(f32[2,64,384]{2,1,0:T(8,128)S(1)} %collective-permute-done.11.rest_5_) | copy-start | bytes 589828
  89.0 3.0 %copy-start.8 = (f32[2,64,384]{2,1,0:T(8,128)}, f32[2,64,384]{2,1,0:T(8,128)S(1)}, u32[]{:S(2)}) copy-start(f32[2,64,384]{2,1,0:T(8,128)S(1)} %collective-permute-done.12.rest_6_) | copy-start | bytes 589828
  92.1 0.7 copy-start.9

commit v4 on v3

--- a/solution.py
+++ b/solution.py
@@ -16,6 +16,13 @@
 HBM_SPEC = pl.BlockSpec(memory_space=pl.ANY)
 SMEM_SPEC = pl.BlockSpec(memory_space=pltpu.SMEM)
 VMEM_SPEC = pl.BlockSpec(memory_space=pltpu.VMEM)
+
+
+def class_order(owners):
+    half = owners // 2
+    far = [owners - 2, *range(half, owners - 2), owners - 1]
+    near = [*range(2, half), 1]
+    return [d for pair in zip(far, near) for d in pair] + far[len(near) :]
 
 
 def params(limit=VMEM_LIMIT):
@@ -149,7 +156,7 @@
 
 
 def product_kernel(owners, amp_from, amp_self, res_to, operator, amplitudes, *rest):
-    arrived, outs = rest[: owners - 1], rest[owners - 1 : 2 * owners - 1]
+    arrived, outs = dict(zip(class_order(owners), rest[: owners - 1])), rest[owners - 1 : 2 * owners - 1]
     own, high, low, totals, sems = rest[2 * owners - 1 :]
     rows, columns = high.shape
 
@@ -166,7 +173,7 @@
                 fetch(k).wait()
                 values = own[k]
             else:
-                values = arrived[d - 1][k]
+                values = arrived[d][k]
             top = values.astype(BF16)
             spot = pl.ds(pl.multiple_of(g * TW, TW), TW)
             high[spot, :] = top
@@ -199,7 +206,7 @@
 
 
 def final_kernel(owners, tiles, res_from, res_tile, res_first, window, pair, virt, *rest):
-    arrived, (_, out, sums, sems) = rest[:owners], rest[-4:]
+    arrived, (_, out, sums, sems) = dict(zip([0] + class_order(owners), rest[:owners])), rest[-4:]
     spots = [(d, k, d * CAP + k) for d in range(owners) for k in range(CAP)]
     for d, k, spot in spots:
         first = res_first[spot]
@@ -257,10 +264,7 @@
     me_ref = me.reshape(1)
 
     def exchange(buffers):
-        moved = {}
-        for d in range(owners - 1, 0, -1):
-            moved[d] = lax.ppermute(buffers[d - 1], "tile", [(i, i ^ d) for i in range(owners)])
-        return [moved[d] for d in range(1, owners)]
+        return [lax.ppermute(buffers[d - 1], "tile", [(i, i ^ d) for i in range(owners)]) for d in class_order(owners)]
 
     piece = pltpu.VMEM((CAP, TW, row_count), F32)
     packed = pl.pallas_call(

time: 96.6 us -> 91.8 us (0.950)
  waiting for transfers between devices: 34 us -> 23.3 us
  starting transfers between devices: 17 us -> 22.2 us
    ppermute x14, waiting for transfers between devices: 34 us -> 23.3 us  [exchange(): lax.ppermute(buffers[d - 1], 'tile', [(i, i ^ d) for i in range(owners)])]
    ppermute x14, starting transfers between devices: 17 us -> 22.2 us  [exchange(): lax.ppermute(buffers[d - 1], 'tile', [(i, i ^ d) for i in range(owners)])]
  transfers between devices with their start and end apart: 14 -> 14, of which waited for: 10 -> 5; matrix products, arithmetic and copies ran while one was open for 9% -> 10% of each run, Pallas kernels for 13% -> 14%
where the time goes in v4:
time: 91.8 us; the launch traced here: 90.2 us
  waiting for transfers between devices  23.3 us (25%)
  starting transfers between devices  22.2 us (24%)
  Pallas kernels  21.7 us (24%)
  blocking collectives  11 us (12%)
  local copies, waits for them, and re-layouts  10.5 us (11%)
    ppermute x14, waiting for transfers between devices, exchange(): lax.ppermute(buffers[d - 1], 'tile', [(i, i ^ d) for i in range(owners)])  23.3 us
    ppermute x14, starting transfers between devices, exchange(): lax.ppermute(buffers[d - 1], 'tile', [(i, i ^ d) for i in range(owners)])  22.2 us
    psum x1, blocking collectives, local(): lax.psum(jnp.where(spots, own_lists[None, :], 0), 'tile').reshape(-1)  11 us
    pallas_call x1, Pallas kernels, local(): pl.pallas_call(sum_kernel, grid=(steps,), out_shape=[jax.ShapeDtypeStruct...  8.12 us
    reshape x2, local copies, waits for them, and re-layouts, local(): sums.reshape(list_length, list_length, TW, TW).transpose(0, 2, 1, 3)  4.53 us
    pallas_call x1, Pallas kernels, local(): pl.pallas_call(functools.partial(maps_kernel, owners, per_amp, per_res),...  4.26 us
    pallas_call x1, Pallas kernels, local(): pl.pallas_call(functools.partial(product_kernel, owners), out_shape=[piec...  3.85 us
    pallas_call x1, Pallas kernels, local(): pl.pallas_call(functools.partial(final_kernel, owners, tile_count), out_s...  3.03 us
  transfers between devices with their start and end apart: 14, of which 5 were waited for; matrix products, arithmetic and copies ran while one was open for 10% of the time, Pallas kernels for 14%

profile of v4, /device:TPU:12, one launch (start us, length us, event | category | flops | bytes accessed | tf_op | source)
XLA Modules:
  0.0 90.2 jit_solution(11145023098953413126)
XLA Ops:
  0.0 0.7 pad_add_fusion
  0.8 0.1 broadcast_select_fusion
  0.8 0.1 reshape.27
  0.9 11.0 %psum.7.lists_ref = s32[128]{0:T(128)} all-reduce(s32[128]{0:T(128)S(1)} %reshape.27), channel_id=1, replica_groups=mesh['mol'=2,'tile'=8,'rep'=2] {'tile'}, use_global_device_ids=true, to_apply=%region_0.1 | all-reduce | flops 128 | bytes 1024 | tf_op jit(solution)/shard_map/psum | solution.py:263
  11.9 2.4 %pack_tiles.1 = (f32[2,64,384]{2,1,0:T(8,128)S(1)}, f32[2,64,384]{2,1,0:T(8,128)S(1)}, f32[2,64,384]{2,1,0:T(8,128)S(1)}, f32[2,64,384]{2,1,0:T(8,128)S(1)}, f32...) custom-call(s32[1]{0:T(128)} %bitcast.me_ref, s32[128]{0:T(128)} %psum.7.lists_ref, ...), custom_call_target="tpu_custom_call" | custom-call | bytes 1572864 | tf_op jit(solution)/shard_map/pack_tiles/pallas_call | solution.py:270
  14.3 0.4 collective-permute-start
  14.8 1.3 %collective-permute-start.1 = (f32[2,64,384]{2,1,0:T(8,128)S(1)}, f32[2,64,384]{2,1,0:T(8,128)S(1)}, u32[]{:S(2)}, u32[]{:S(2)}) collective-permute-start(f32[2,64,384]{2,1,0:T(8,128)S(1)} %get-tuple-element.42), channel_id=1, source_target_pairs={{0,4},{2,6},{4,0},{6,2},{8,12},{10,14},{12,8},{14,10},{1,5},{3,7},... | collective-permute-start | bytes 589832 | tf_op jit(solution)/shard_map/ppermute | solution.py:267
  16.1 2.2 %collective-permute-start.2 = (f32[2,64,384]{2,1,0:T(8,128)S(1)}, f32[2,64,384]{2,1,0:T(8,128)}, u32[]{:S(2)}, u32[]{:S(2)}) collective-permute-start(f32[2,64,384]{2,1,0:T(8,128)S(1)} %get-tuple-element.43), channel_id=1, source_target_pairs={{0,8},{2,10},{4,12},{6,14},{8,0},{10,2},{12,4},{14,6},{1,9},{3,11}... | collective-permute-start | bytes 589832 | tf_op jit(solution)/shard_map/ppermute | solution.py:267
  18.3 2.1 %collective-permute-start.3 = (f32[2,64,384]{2,1,0:T(8,128)S(1)}, f32[2,64,384]{2,1,0:T(8,128)}, u32[]{:S(2)}, u32[]{:S(2)}) collective-permute-start(f32[2,64,384]{2,1,0:T(8,128)S(1)} %get-tuple-element.44), channel_id=1, source_target_pairs={{0,6},{2,4},{4,2},{6,0},{8,14},{10,12},{12,10},{14,8},{1,7},{3,5},... | collective-permute-start | bytes 589832 | tf_op jit(solution)/shard_map/ppermute | solution.py:267
  20.4 0.8 collective-permute-start.4
  21.2 5.3 %collective-permute-done.rest_0_ = f32[2,64,384]{2,1,0:T(8,128)S(1)} collective-permute-done((f32[2,64,384]{2,1,0:T(8,128)S(1)}, f32[2,64,384]{2,1,0:T(8,128)S(1)}, u32[]{:S(2)}, u32[]{:S(2)}) %collective-permute-start) | collective-permute-done | bytes 196640 | tf_op jit(solution)/shard_map/ppermute | solution.py:267
  26.5 0.0 copy-start.1
  26.5 0.6 collective-permute-start.5
  27.1 0.0 collective-permute-done.1.rest_1_
  27.1 0.0 copy-start.2
  27.1 1.9 %collective-permute-start.6 = (f32[2,64,384]{2,1,0:T(8,128)S(1)}, f32[2,64,384]{2,1,0:T(8,128)}, u32[]{:S(2)}, u32[]{:S(2)}) collective-permute-start(f32[2,64,384]{2,1,0:T(8,128)S(1)} %get-tuple-element.47), channel_id=1, source_target_pairs={{0,14},{2,12},{4,10},{6,8},{8,6},{10,4},{12,2},{14,0},{1,15},{3,13... | collective-permute-start | bytes 589832 | tf_op jit(solution)/shard_map/ppermute | solution.py:267
  29.0 4.3 %list_maps.1 = (s32[16]{0:T(128)}, s32[2]{0:T(128)}, s32[16]{0:T(128)}, s32[16]{0:T(128)}, s32[16]{0:T(128)}, /*index=5*/s32[16]{0:T(128)}) custom-call(s32[1]{0:T(128)} %bitcast.me_ref, s32[128]{0:T(128)} %psum.7.lists_ref, s32[200]{0:T(256)} %amp_slot_ref.3, s32[200]{0:T(256)} %res_slot_ref.1), custom_call_target="tpu_custom_call" | custom-call | tf_op jit(solution)/shard_map/list_maps/pallas_call | solution.py:286
  33.9 8.1 %sum_integrals.1 = (f32[64,4096]{1,0:T(8,128)}, f32[1600,384]{1,0:T(8,128)}) custom-call(s32[1]{0:T(128)S(6)} %copy.17.count_ref, s32[2,512]{1,0:T(2,128)} %tasks_ref.1, f32[512,4096]{1,0:T(8,128)} %integrals_ref.1), custom_call_target="tpu_custom_call" | custom-call | flops 536870912 | bytes 9437184 | tf_op jit(solution)/shard_map/sum_integrals/pallas_call | solution.py:299
  42.0 0.0 copy-done.1
  42.0 0.0 copy-done.2
  42.0 2.0 %reshape.28 = f32[8,8,64,64]{3,2,1,0:T(8,128)S(1)} reshape(f32[64,4096]{1,0:T(8,128)} %get-tuple-element.34) | data formatting | bytes 2097152 | tf_op jit(solution)/shard_map/reshape | solution.py:321
  44.0 2.5 %copy.15 = f32[8,8,64,64]{3,1,2,0:T(8,128)} copy(f32[8,8,64,64]{3,2,1,0:T(8,128)S(1)} %reshape.28) | data formatting | bytes 2097152 | tf_op jit(solution)/shard_map/reshape | solution.py:321
  46.6 0.0 copy-start.10
  46.6 0.0 copy-start.11
  46.6 2.7 %reshape.29.operator = f32[512,512]{1,0:T(8,128)} reshape(f32[8,64,8,64]{3,2,1,0:T(8,128)} %bitcast.7) | data formatting | bytes 2097152 | tf_op jit(solution)/shard_map/reshape | solution.py:323
  49.3 0.0 copy-done.10
  49.3 0.1 broadcast_in_dim.32
  49.4 0.0 copy-done.11
  49.4 0.6 reshape.30.pair
  49.9 1.2 %broadcast_in_dim.33.virt = f32[25,64,128]{2,1,0:T(8,128)} broadcast(f32[25,64]{1,0:T(8,128)S(1)} %broadcast_in_dim.32), dimensions={0,1} | broadcast | bytes 825600 | tf_op jit(solution)/shard_map/broadcast_in_dim | solution.py:326
  51.1 0.0 collective-permute-done.2.rest_2_
  51.1 0.0 collective-permute-done.3.rest_3_
  51.1 0.0 collective-permute-done.4.rest_4_
  51.1 0.0 collective-permute-done.5.rest_5_
  51.1 0.0 collective-permute-done.6.rest_6_
  51.2 3.9 %multiply_tiles.1 = (f32[2,64,384]{2,1,0:T(8,128)S(1)}, f32[2,64,384]{2,1,0:T(8,128)S(1)}, f32[2,64,384]{2,1,0:T(8,128)S(1)}, f32[2,64,384]{2,1,0:T(8,128)S(1)},...) custom-call(s32[16]{0:T(128)} %get-tuple-element.37.amp_from, ...), custom_call_target="tpu_custom_call" | custom-call | flops 603979776 | bytes 2621440 | tf_op jit(solution)/shard_map/multiply_tiles/pallas_call | solution.py:331
  55.0 0.0 copy-start
  55.0 0.7 copy-done
  55.7 1.0 %collective-permute-start.7 = (f32[2,64,384]{2,1,0:T(8,128)S(1)}, f32[2,64,384]{2,1,0:T(8,128)S(1)}, u32[]{:S(2)}, u32[]{:S(2)}) collective-permute-start(f32[2,64,384]{2,1,0:T(8,128)S(1)} %get-tuple-element.49), channel_id=1, source_target_pairs={{0,12},{2,14},{4,8},{6,10},{8,4},{10,6},{12,0},{14,2},{1,13},{3,15... | collective-permute-start | bytes 589832 | tf_op jit(solution)/shard_map/ppermute | solution.py:267
  56.7 3.9 %collective-permute-start.8 = (f32[2,64,384]{2,1,0:T(8,128)S(1)}, f32[2,64,384]{2,1,0:T(8,128)S(1)}, u32[]{:S(2)}, u32[]{:S(2)}) collective-permute-start(f32[2,64,384]{2,1,0:T(8,128)S(1)} %get-tuple-element.50), channel_id=1, source_target_pairs={{0,4},{2,6},{4,0},{6,2},{8,12},{10,14},{12,8},{14,10},{1,5},{3,7},... | collective-permute-start | bytes 589832 | tf_op jit(solution)/shard_map/ppermute | solution.py:267
  60.6 0.1 collective-permute-start.9
  60.7 2.1 %collective-permute-start.10 = (f32[2,64,384]{2,1,0:T(8,128)S(1)}, f32[2,64,384]{2,1,0:T(8,128)S(1)}, u32[]{:S(2)}, u32[]{:S(2)}) collective-permute-start(f32[2,64,384]{2,1,0:T(8,128)S(1)} %get-tuple-element.52), channel_id=1, source_target_pairs={{0,6},{2,4},{4,2},{6,0},{8,14},{10,12},{12,10},{14,8},{1,7},{3,5},... | collective-permute-start | bytes 589832 | tf_op jit(solution)/shard_map/ppermute | solution.py:267
  62.8 1.6 %collective-permute-start.11 = (f32[2,64,384]{2,1,0:T(8,128)S(1)}, f32[2,64,384]{2,1,0:T(8,128)S(1)}, u32[]{:S(2)}, u32[]{:S(2)}) collective-permute-start(f32[2,64,384]{2,1,0:T(8,128)S(1)} %get-tuple-element.53), channel_id=1, source_target_pairs={{0,10},{2,8},{4,14},{6,12},{8,2},{10,0},{12,6},{14,4},{1,11},{3,9}... | collective-permute-start | bytes 589832 | tf_op jit(solution)/shard_map/ppermute | solution.py:267
  64.4 6.0 %collective-permute-done.7.rest_1_ = f32[2,64,384]{2,1,0:T(8,128)S(1)} collective-permute-done((f32[2,64,384]{2,1,0:T(8,128)S(1)}, f32[2,64,384]{2,1,0:T(8,128)S(1)}, u32[]{:S(2)}, u32[]{:S(2)}) %collective-permute-start.7) | collective-permute-done | bytes 196640 | tf_op jit(solution)/shard_map/ppermute | solution.py:267
  70.4 0.0 copy-start.3
  70.4 3.0 %collective-permute-start.12 = (f32[2,64,384]{2,1,0:T(8,128)S(1)}, f32[2,64,384]{2,1,0:T(8,128)S(1)}, u32[]{:S(2)}, u32[]{:S(2)}) collective-permute-start(f32[2,64,384]{2,1,0:T(8,128)S(1)} %get-tuple-element.54), channel_id=1, source_target_pairs={{0,2},{2,0},{4,6},{6,4},{8,10},{10,8},{12,14},{14,12},{1,3},{3,1},... | collective-permute-start | bytes 589832 | tf_op jit(solution)/shard_map/ppermute | solution.py:267
  73.4 0.0 collective-permute-done.8.rest_2_
  73.4 0.0 copy-start.4
  73.4 1.1 %collective-permute-start.13 = (f32[2,64,384]{2,1,0:T(8,128)S(1)}, f32[2,64,384]{2,1,0:T(8,128)S(1)}, u32[]{:S(2)}, u32[]{:S(2)}) collective-permute-start(f32[2,64,384]{2,1,0:T(8,128)S(1)} %get-tuple-element.55), channel_id=1, source_target_pairs={{0,14},{2,12},{4,10},{6,8},{8,6},{10,4},{12,2},{14,0},{1,15},{3,13... | collective-permute-start | bytes 589832 | tf_op jit(solution)/shard_map/ppermute | solution.py:267
  74.5 4.5 %collective-permute-done.9.rest_3_ = f32[2,64,384]{2,1,0:T(8,128)S(1)} collective-permute-done((f32[2,64,384]{2,1,0:T(8,128)S(1)}, f32[2,64,384]{2,1,0:T(8,128)S(1)}, u32[]{:S(2)}, u32[]{:S(2)}) %collective-permute-start.9) | collective-permute-done | bytes 196640 | tf_op jit(solution)/shard_map/ppermute | solution.py:267
  79.0 0.0 copy-start.5
  79.0 0.0 collective-permute-done.10.rest_4_
  79.0 0.0 copy-start.6
  79.0 3.0 %collective-permute-done.11.rest_5_ = f32[2,64,384]{2,1,0:T(8,128)S(1)} collective-permute-done((f32[2,64,384]{2,1,0:T(8,128)S(1)}, f32[2,64,384]{2,1,0:T(8,128)S(1)}, u32[]{:S(2)}, u32[]{:S(2)}) %collective-permute-start.11) | collective-permute-done | bytes 196640 | tf_op jit(solution)/shard_map/ppermute | solution.py:267
  82.0 0.0 collective-permute-done.12.rest_6_
  82.0 4.5 %collective-permute-done.13.rest_7_ = f32[2,64,384]{2,1,0:T(8,128)S(1)} collective-permute-done((f32[2,64,384]{2,1,0:T(8,128)S(1)}, f32[2,64,384]{2,1,0:T(8,128)S(1)}, u32[]{:S(2)}, u32[]{:S(2)}) %collective-permute-start.13) | collective-permute-done | bytes 196640 | tf_op jit(solution)/shard_map/ppermute | solution.py:267
  86.5 0.0 copy-done.3
  86.5 0.0 copy-done.4
  86.5 0.0 copy-done.5
  86.5 0.0 copy-done.6
  86.5 0.0 copy-done.7
  86.5 0.0 copy-done.8
  86.5 0.6 copy-done.9
  87.2 3.0 %finish_tiles.1 = f32[25,64,384]{2,1,0:T(8,128)} custom-call(s32[16]{0:T(128)} %get-tuple-element.31.res_from, s32[16]{0:T(128)} %get-tuple-element.32.res_tile, s32[16]{0:T(128)} %get-tuple-element.33.res_first, f32[8]{0:T(128)} %window.1, f32[1,384]{1,0:T(1,128)} %reshape.30.pair, ...), custom_call_target="tpu_custom_call", output_to_operand_aliasing={{}: (14, {})} | custom-call | bytes 2457600 | tf_op jit(solution)/shard_map/finish_tiles/pallas_call | solution.py:348
  (4 shorter events, 0.0 us)
Async XLA Ops:
  14.3 12.1 %collective-permute-start = (f32[2,64,384]{2,1,0:T(8,128)S(1)}, f32[2,64,384]{2,1,0:T(8,128)S(1)}, u32[]{:S(2)}, u32[]{:S(2)}) collective-permute-start(f32[2,64,384]{2,1,0:T(8,128)S(1)} %get-tuple-element.41), channel_id=1, source_target_pairs={{0,12},{2,14},{4,8},{6,10},{8,4},{10,6},{12,0},{14,2},{1,13},{3,15... | collective-permute-start | bytes 589832 | tf_op jit(solution)/shard_map/ppermute | solution.py:267
  14.8 12.3 %collective-permute-start.1 = (f32[2,64,384]{2,1,0:T(8,128)S(1)}, f32[2,64,384]{2,1,0:T(8,128)S(1)}, u32[]{:S(2)}, u32[]{:S(2)}) collective-permute-start(f32[2,64,384]{2,1,0:T(8,128)S(1)} %get-tuple-element.42), channel_id=1, source_target_pairs={{0,4},{2,6},{4,0},{6,2},{8,12},{10,14},{12,8},{14,10},{1,5},{3,7},... | collective-permute-start | bytes 589832 | tf_op jit(solution)/shard_map/ppermute | solution.py:267
  16.1 35.0 %collective-permute-start.2 = (f32[2,64,384]{2,1,0:T(8,128)S(1)}, f32[2,64,384]{2,1,0:T(8,128)}, u32[]{:S(2)}, u32[]{:S(2)}) collective-permute-start(f32[2,64,384]{2,1,0:T(8,128)S(1)} %get-tuple-element.43), channel_id=1, source_target_pairs={{0,8},{2,10},{4,12},{6,14},{8,0},{10,2},{12,4},{14,6},{1,9},{3,11}... | collective-permute-start | bytes 589832 | tf_op jit(solution)/shard_map/ppermute | solution.py:267
  18.3 32.9 %collective-permute-start.3 = (f32[2,64,384]{2,1,0:T(8,128)S(1)}, f32[2,64,384]{2,1,0:T(8,128)}, u32[]{:S(2)}, u32[]{:S(2)}) collective-permute-start(f32[2,64,384]{2,1,0:T(8,128)S(1)} %get-tuple-element.44), channel_id=1, source_target_pairs={{0,6},{2,4},{4,2},{6,0},{8,14},{10,12},{12,10},{14,8},{1,7},{3,5},... | collective-permute-start | bytes 589832 | tf_op jit(solution)/shard_map/ppermute | solution.py:267
  20.4 30.8 %collective-permute-start.4 = (f32[2,64,384]{2,1,0:T(8,128)S(1)}, f32[2,64,384]{2,1,0:T(8,128)}, u32[]{:S(2)}, u32[]{:S(2)}) collective-permute-start(f32[2,64,384]{2,1,0:T(8,128)S(1)} %get-tuple-element.45), channel_id=1, source_target_pairs={{0,10},{2,8},{4,14},{6,12},{8,2},{10,0},{12,6},{14,4},{1,11},{3,9}... | collective-permute-start | bytes 589832 | tf_op jit(solution)/shard_map/ppermute | solution.py:267
  26.5 15.5 %copy-start.1 = (f32[2,64,384]{2,1,0:T(8,128)}, f32[2,64,384]{2,1,0:T(8,128)S(1)}, u32[]{:S(2)}) copy-start(f32[2,64,384]{2,1,0:T(8,128)S(1)} %collective-permute-done.rest_0_) | copy-start | bytes 589828
  26.5 24.7 %collective-permute-start.5 = (f32[2,64,384]{2,1,0:T(8,128)S(1)}, f32[2,64,384]{2,1,0:T(8,128)}, u32[]{:S(2)}, u32[]{:S(2)}) collective-permute-start(f32[2,64,384]{2,1,0:T(8,128)S(1)} %get-tuple-element.46), channel_id=1, source_target_pairs={{0,2},{2,0},{4,6},{6,4},{8,10},{10,8},{12,14},{14,12},{1,3},{3,1},... | collective-permute-start | bytes 589832 | tf_op jit(solution)/shard_map/ppermute | solution.py:267
  27.1 14.9 %copy-start.2 = (f32[2,64,384]{2,1,0:T(8,128)}, f32[2,64,384]{2,1,0:T(8,128)S(1)}, u32[]{:S(2)}) copy-start(f32[2,64,384]{2,1,0:T(8,128)S(1)} %collective-permute-done.1.rest_1_) | copy-start | bytes 589828
  27.1 24.0 %collective-permute-start.6 = (f32[2,64,384]{2,1,0:T(8,128)S(1)}, f32[2,64,384]{2,1,0:T(8,128)}, u32[]{:S(2)}, u32[]{:S(2)}) collective-permute-start(f32[2,64,384]{2,1,0:T(8,128)S(1)} %get-tuple-element.47), channel_id=1, source_target_pairs={{0,14},{2,12},{4,10},{6,8},{8,6},{10,4},{12,2},{14,0},{1,15},{3,13... | collective-permute-start | bytes 589832 | tf_op jit(solution)/shard_map/ppermute | solution.py:267
  46.6 2.7 %copy-start.10 = (f32[1600]{0:T(1024)S(1)}, f32[1600]{0:T(1024)}, u32[]{:S(2)}) copy-start(f32[1600]{0:T(1024)} %param.20) | copy-start | bytes 19204
  46.6 2.8 %copy-start.11 = (f32[384]{0:T(512)S(1)}, f32[384]{0:T(512)}, u32[]{:S(2)}) copy-start(f32[384]{0:T(512)} %param.19) | copy-start | bytes 4612
  55.0 0.7 copy-start
  55.7 14.7 %collective-permute-start.7 = (f32[2,64,384]{2,1,0:T(8,128)S(1)}, f32[2,64,384]{2,1,0:T(8,128)S(1)}, u32[]{:S(2)}, u32[]{:S(2)}) collective-permute-start(f32[2,64,384]{2,1,0:T(8,128)S(1)} %get-tuple-element.49), channel_id=1, source_target_pairs={{0,12},{2,14},{4,8},{6,10},{8,4},{10,6},{12,0},{14,2},{1,13},{3,15... | collective-permute-start | bytes 589832 | tf_op jit(solution)/shard_map/ppermute | solution.py:267
  56.7 16.7 %collective-permute-start.8 = (f32[2,64,384]{2,1,0:T(8,128)S(1)}, f32[2,64,384]{2,1,0:T(8,128)S(1)}, u32[]{:S(2)}, u32[]{:S(2)}) collective-permute-start(f32[2,64,384]{2,1,0:T(8,128)S(1)} %get-tuple-element.50), channel_id=1, source_target_pairs={{0,4},{2,6},{4,0},{6,2},{8,12},{10,14},{12,8},{14,10},{1,5},{3,7},... | collective-permute-start | bytes 589832 | tf_op jit(solution)/shard_map/ppermute | solution.py:267
  60.6 18.4 %collective-permute-start.9 = (f32[2,64,384]{2,1,0:T(8,128)S(1)}, f32[2,64,384]{2,1,0:T(8,128)S(1)}, u32[]{:S(2)}, u32[]{:S(2)}) collective-permute-start(f32[2,64,384]{2,1,0:T(8,128)S(1)} %get-tuple-element.51), channel_id=1, source_target_pairs={{0,8},{2,10},{4,12},{6,14},{8,0},{10,2},{12,4},{14,6},{1,9},{3,11}... | collective-permute-start | bytes 589832 | tf_op jit(solution)/shard_map/ppermute | solution.py:267
  60.7 18.3 %collective-permute-start.10 = (f32[2,64,384]{2,1,0:T(8,128)S(1)}, f32[2,64,384]{2,1,0:T(8,128)S(1)}, u32[]{:S(2)}, u32[]{:S(2)}) collective-permute-start(f32[2,64,384]{2,1,0:T(8,128)S(1)} %get-tuple-element.52), channel_id=1, source_target_pairs={{0,6},{2,4},{4,2},{6,0},{8,14},{10,12},{12,10},{14,8},{1,7},{3,5},... | collective-permute-start | bytes 589832 | tf_op jit(solution)/shard_map/ppermute | solution.py:267
  62.8 19.2 %collective-permute-start.11 = (f32[2,64,384]{2,1,0:T(8,128)S(1)}, f32[2,64,384]{2,1,0:T(8,128)S(1)}, u32[]{:S(2)}, u32[]{:S(2)}) collective-permute-start(f32[2,64,384]{2,1,0:T(8,128)S(1)} %get-tuple-element.53), channel_id=1, source_target_pairs={{0,10},{2,8},{4,14},{6,12},{8,2},{10,0},{12,6},{14,4},{1,11},{3,9}... | collective-permute-start | bytes 589832 | tf_op jit(solution)/shard_map/ppermute | solution.py:267
  70.4 16.1 %copy-start.3 = (f32[2,64,384]{2,1,0:T(8,128)}, f32[2,64,384]{2,1,0:T(8,128)S(1)}, u32[]{:S(2)}) copy-start(f32[2,64,384]{2,1,0:T(8,128)S(1)} %collective-permute-done.7.rest_1_) | copy-start | bytes 589828
  70.4 11.6 %collective-permute-start.12 = (f32[2,64,384]{2,1,0:T(8,128)S(1)}, f32[2,64,384]{2,1,0:T(8,128)S(1)}, u32[]{:S(2)}, u32[]{:S(2)}) collective-permute-start(f32[2,64,384]{2,1,0:T(8,128)S(1)} %get-tuple-element.54), channel_id=1, source_target_pairs={{0,2},{2,0},{4,6},{6,4},{8,10},{10,8},{12,14},{14,12},{1,3},{3,1},... | collective-permute-start | bytes 589832 | tf_op jit(solution)/shard_map/ppermute | solution.py:267
  73.4 13.1 %copy-start.4 = (f32[2,64,384]{2,1,0:T(8,128)}, f32[2,64,384]{2,1,0:T(8,128)S(1)}, u32[]{:S(2)}) copy-start(f32[2,64,384]{2,1,0:T(8,128)S(1)} %collective-permute-done.8.rest_2_) | copy-start | bytes 589828
  73.4 13.1 %collective-permute-start.13 = (f32[2,64,384]{2,1,0:T(8,128)S(1)}, f32[2,64,384]{2,1,0:T(8,128)S(1)}, u32[]{:S(2)}, u32[]{:S(2)}) collective-permute-start(f32[2,64,384]{2,1,0:T(8,128)S(1)} %get-tuple-element.55), channel_id=1, source_target_pairs={{0,14},{2,12},{4,10},{6,8},{8,6},{10,4},{12,2},{14,0},{1,15},{3,13... | collective-permute-start | bytes 589832 | tf_op jit(solution)/shard_map/ppermute | solution.py:267
  79.0 7.5 %copy-start.5 = (f32[2,64,384]{2,1,0:T(8,128)}, f32[2,64,384]{2,1,0:T(8,128)S(1)}, u32[]{:S(2)}) copy-start(f32[2,64,384]{2,1,0:T(8,128)S(1)} %collective-permute-done.9.rest_3_) | copy-start | bytes 589828
  79.0 7.5 %copy-start.6 = (f32[2,64,384]{2,1,0:T(8,128)}, f32[2,64,384]{2,1,0:T(8,128)S(1)}, u32[]{:S(2)}) copy-start(f32[2,64,384]{2,1,0:T(8,128)S(1)} %collective-permute-done.10.rest_4_) | copy-start | bytes 589828
  82.0 4.5 %copy-start.7 = (f32[2,64,384]{2,1,0:T(8,128)}, f32[2,64,384]{2,1,0:T(8,128)S(1)}, u32[]{:S(2)}) copy-start(f32[2,64,384]{2,1,0:T(8,128)S(1)} %collective-permute-done.11.rest_5_) | copy-start | bytes 589828
  82.0 4.5 %copy-start.8 = (f32[2,64,384]{2,1,0:T(8,128)}, f32[2,64,384]{2,1,0:T(8,128)S(1)}, u32[]{:S(2)}) copy-start(f32[2,64,384]{2,1,0:T(8,128)S(1)} %collective-permute-done.12.rest_6_) | copy-start | bytes 589828
  86.5 0.7 copy-start.9

commit v5 on v4

--- a/solution.py
+++ b/solution.py
@@ -9,7 +9,7 @@
 
 TW = 64
 CAP = 2
-VMEM_LIMIT = 56 * 1024 * 1024
+VMEM_LIMIT = 32 * 1024 * 1024
 F32 = jnp.float32
 BF16 = jnp.bfloat16
 
@@ -31,6 +31,10 @@
 
 def cost(flops, touched):
     return pl.CostEstimate(flops=flops, bytes_accessed=touched, transcendentals=0)
+
+
+def in_vmem(array):
+    return pltpu.with_memory_space_constraint(array, pltpu.VMEM)
 
 
 def clear(ref, count, value):
@@ -71,72 +75,63 @@
     amp_from, amp_self, res_to, res_from, res_tile, res_first, seen, taken,
 ):
     list_length = lists_ref.shape[0] // owners // 2
+    spots = owners * CAP
     me = me_ref[0]
     for ref in (amp_from, res_to, res_from):
-        clear(ref, owners * CAP, -1)
-    clear(amp_self, CAP, 0)
-    clear(res_tile, owners * CAP, 0)
-    clear(res_first, owners * CAP, -1)
-    clear(taken, per_res, -1)
-
-    def own_list(offset, slot_map, per_owner, place):
+        clear(ref, spots, -1)
+    clear(amp_self, CAP + 1, 0)
+    clear(res_tile, spots, 0)
+    clear(taken, per_res + 1, -1)
+
+    def own_list(offset, slot_map, per_owner, place, self_slots):
         clear(seen, owners, 0)
 
-        @pl.loop(0, list_length)
-        def _(g):
+        def note(g, carry):
             slot = slot_map[lists_ref[me * 2 * list_length + offset + g]]
-            owner = slot // per_owner
+            owner = lax.div(slot, jnp.int32(per_owner))
             d = jnp.bitwise_xor(owner, me)
             count = seen[d]
-            place(d * CAP + count, g, slot - owner * per_owner, d, count)
+            place[d * CAP + count] = g
             seen[d] = count + 1
-
-    def place_amp(at, g, local, d, count):
-        amp_from[at] = g
-
-        @pl.when(d == 0)
-        def _():
-            amp_self[count] = local
-
-    def place_res(at, g, local, d, count):
-        res_to[at] = g
-
-    own_list(0, amp_slot_ref, per_amp, place_amp)
-    own_list(list_length, res_slot_ref, per_res, place_res)
-    clear(seen, owners, 0)
+            if self_slots is not None:
+                self_slots[jnp.where(d == 0, count, CAP)] = slot - owner * per_owner
+            return carry
+
+        lax.fori_loop(0, list_length, note, 0, unroll=8)
+
+    own_list(0, amp_slot_ref, per_amp, amp_from, amp_self)
+    own_list(list_length, res_slot_ref, per_res, res_to, None)
     low = me * per_res
 
-    @pl.loop(0, owners * list_length)
-    def _(i):
-        partner = i // list_length
-        tile = lists_ref[partner * 2 * list_length + list_length + i % list_length]
-        local = res_slot_ref[tile] - low
-
-        @pl.when((local >= 0) & (local < per_res))
-        def _():
-            d = jnp.bitwise_xor(partner, me)
-            count = seen[d]
-            res_from[d * CAP + count] = local
-            res_tile[d * CAP + count] = tile
-            seen[d] = count + 1
-
-    @pl.loop(0, owners * CAP)
-    def _(spot):
+    @pl.loop(0, owners)
+    def _(partner):
+        d = jnp.bitwise_xor(partner, me)
+
+        def note(j, count):
+            tile = lists_ref[partner * 2 * list_length + list_length + j]
+            local = res_slot_ref[tile] - low
+            mine = (local >= 0) & (local < per_res)
+            spot = jnp.where(mine, d * CAP + count, spots)
+            res_from[spot] = local
+            res_tile[spot] = tile
+            return count + mine.astype(jnp.int32)
+
+        lax.fori_loop(0, list_length, note, jnp.int32(0), unroll=8)
+
+    def firsts(spot, carry):
         local = res_from[spot]
-
-        @pl.when(local >= 0)
-        def _():
-            @pl.when(taken[local] < 0)
-            def _():
-                taken[local] = spot
-
-            res_first[spot] = taken[local]
-
-
-def sum_kernel(count_ref, tasks_ref, integrals_ref, sums_ref, blank_ref, hits):
-    slots = sums_ref.shape[0]
-    tasks_here = integrals_ref.shape[0]
-    list_length = int(round(slots**0.5))
+        known = taken[jnp.where(local >= 0, local, per_res)]
+        first = jnp.where(known < 0, spot, known)
+        taken[jnp.where(local >= 0, local, per_res)] = jnp.where(local >= 0, first, -1)
+        res_first[spot] = jnp.where(local >= 0, first, -1)
+        return carry
+
+    lax.fori_loop(0, spots, firsts, 0, unroll=4)
+
+
+def sum_kernel(list_length, count_ref, tasks_ref, integrals_ref, high_ref, low_ref, blank_ref, hits, sums, matrix):
+    slots = list_length * list_length
+    tasks_here, block = integrals_ref.shape
 
     @pl.when(pl.program_id(0) == 0)
     def _():
@@ -150,12 +145,26 @@
     rows = integrals_ref[...]
     high = rows.astype(BF16)
     low = (rows - high.astype(F32)).astype(BF16)
-    sums_ref[...] = jnp.dot(hits[...], high, preferred_element_type=F32) + jnp.dot(
+    found = jnp.dot(hits[...], high, preferred_element_type=F32) + jnp.dot(
         hits[...], low, preferred_element_type=F32
     )
-
-
-def product_kernel(owners, amp_from, amp_self, res_to, operator, amplitudes, *rest):
+    for i in range(0, block // TW, 2):
+        sums[i // 2] = found[:, i * TW : (i + 2) * TW]
+    left = lax.broadcasted_iota(jnp.int32, (list_length, 2 * TW), 1) < TW
+    for i in range(0, block // TW, 2):
+        for a in range(0, list_length, 2):
+            even = sums[i // 2, pl.ds(a, list_length, stride=list_length), :]
+            odd = sums[i // 2, pl.ds(a + 1, list_length, stride=list_length), :]
+            lanes = pl.ds(a * TW, 2 * TW)
+            matrix[pl.ds(i * list_length, list_length), lanes] = jnp.where(left, even, pltpu.roll(odd, TW, 1))
+            matrix[pl.ds((i + 1) * list_length, list_length), lanes] = jnp.where(left, pltpu.roll(even, TW, 1), odd)
+    whole = matrix[...]
+    top = whole.astype(BF16)
+    high_ref[...] = top
+    low_ref[...] = (whole - top.astype(F32)).astype(BF16)
+
+
+def product_kernel(owners, amp_from, amp_self, res_to, operator_high, operator_low, amplitudes, *rest):
     arrived, outs = dict(zip(class_order(owners), rest[: owners - 1])), rest[owners - 1 : 2 * owners - 1]
     own, high, low, totals, sems = rest[2 * owners - 1 :]
     rows, columns = high.shape
@@ -188,13 +197,12 @@
 
     @pl.loop(0, rows // step)
     def _(i):
-        left = operator[pl.ds(pl.multiple_of(i * step, step), step), :]
-        left_high = left.astype(BF16)
-        left_low = (left - left_high.astype(F32)).astype(BF16)
-        total = jnp.dot(left_high, low[...], preferred_element_type=F32)
-        total += jnp.dot(left_low, high[...], preferred_element_type=F32)
-        total += jnp.dot(left_high, high[...], preferred_element_type=F32)
-        totals[pl.ds(i * (step // TW), step // TW)] = total.reshape(step // TW, TW, columns)
+        here = pl.ds(pl.multiple_of(i * step, step), step)
+        total = jnp.dot(operator_high[here, :], low[...], preferred_element_type=F32)
+        total += jnp.dot(operator_low[here, :], high[...], preferred_element_type=F32)
+        total += jnp.dot(operator_high[here, :], high[...], preferred_element_type=F32)
+        for c in range(columns // 128):
+            totals[c, here, :] = total[:, c * 128 : (c + 1) * 128]
 
     for d in range(owners):
         for k in range(CAP):
@@ -202,7 +210,8 @@
 
             @pl.when(g >= 0)
             def _():
-                outs[d][k] = totals[g]
+                for c in range(columns // 128):
+                    outs[d][k, :, c * 128 : (c + 1) * 128] = totals[c, pl.ds(g, TW, stride=rows // TW), :]
 
 
 def final_kernel(owners, tiles, res_from, res_tile, res_first, window, pair, virt, *rest):
@@ -258,13 +267,18 @@
     slots = list_length * list_length
     task_slots = tasks.shape[1]
 
+    amplitudes = pltpu.with_memory_space_constraint(amplitudes, pltpu.HBM)
+    integrals = pltpu.with_memory_space_constraint(integrals, pltpu.HBM)
     own_lists = jnp.concatenate([need_amp, needed_residual_tiles])
     spots = jnp.arange(owners, dtype=jnp.int32)[:, None] == me
     lists = lax.psum(jnp.where(spots, own_lists[None, :], 0), "tile").reshape(-1)
     me_ref = me.reshape(1)
 
     def exchange(buffers):
-        return [lax.ppermute(buffers[d - 1], "tile", [(i, i ^ d) for i in range(owners)]) for d in class_order(owners)]
+        return [
+            in_vmem(lax.ppermute(buffers[d - 1], "tile", [(i, i ^ d) for i in range(owners)]))
+            for d in class_order(owners)
+        ]
 
     piece = pltpu.VMEM((CAP, TW, row_count), F32)
     packed = pl.pallas_call(
@@ -282,69 +296,76 @@
     )(me_ref, lists, amp_slot, amplitudes)
     fetched = exchange(packed)
 
-    small = jax.ShapeDtypeStruct((owners * CAP,), jnp.int32)
+    small = pltpu.SMEM((owners * CAP + 1,), jnp.int32)
     amp_from, amp_self, res_to, res_from, res_tile, res_first = pl.pallas_call(
         functools.partial(maps_kernel, owners, per_amp, per_res),
-        out_shape=[small, jax.ShapeDtypeStruct((CAP,), jnp.int32), small, small, small, small],
+        out_shape=[small, pltpu.SMEM((CAP + 1,), jnp.int32), small, small, small, small],
         in_specs=[SMEM_SPEC] * 4,
         out_specs=[SMEM_SPEC] * 6,
-        scratch_shapes=[pltpu.SMEM((owners,), jnp.int32), pltpu.SMEM((per_res,), jnp.int32)],
+        scratch_shapes=[pltpu.SMEM((owners,), jnp.int32), pltpu.SMEM((per_res + 1,), jnp.int32)],
         compiler_params=params(),
         name="list_maps",
     )(me_ref, lists, amp_slot, res_slot)
 
-    block = 512
+    amp_from, amp_self, res_to, res_from, res_tile, res_first = (
+        pltpu.with_memory_space_constraint(x, pltpu.SMEM)
+        for x in (amp_from, amp_self, res_to, res_from, res_tile, res_first)
+    )
+    block = 1024
     steps = TW * TW // block
+    depth = list_length * TW
+    operator_rows = depth // steps
     blank_rows = per_res * TW // steps
-    sums, blank = pl.pallas_call(
-        sum_kernel,
+    keep = depth <= 1024
+    operator = pltpu.VMEM((depth, depth), BF16) if keep else jax.ShapeDtypeStruct((depth, depth), BF16)
+    operator_high, operator_low, blank = pl.pallas_call(
+        functools.partial(sum_kernel, list_length),
         grid=(steps,),
-        out_shape=[
-            jax.ShapeDtypeStruct((slots, TW * TW), F32),
-            jax.ShapeDtypeStruct((per_res * TW, row_count), F32),
-        ],
+        out_shape=[operator, operator, jax.ShapeDtypeStruct((per_res * TW, row_count), F32)],
         in_specs=[
             SMEM_SPEC,
             pl.BlockSpec((2, task_slots), lambda i: (0, 0)),
             pl.BlockSpec((task_slots, block), lambda i: (0, i)),
         ],
         out_specs=[
-            pl.BlockSpec((slots, block), lambda i: (0, i)),
+            pl.BlockSpec((operator_rows, depth), lambda i: (i, 0)),
+            pl.BlockSpec((operator_rows, depth), lambda i: (i, 0)),
             pl.BlockSpec((blank_rows, row_count), lambda i: (i, 0)),
         ],
-        scratch_shapes=[pltpu.VMEM((slots, task_slots), BF16)],
+        scratch_shapes=[
+            pltpu.VMEM((slots, task_slots), BF16),
+            pltpu.VMEM((block // (2 * TW), slots, 2 * TW), F32),
+            pltpu.VMEM((operator_rows, depth), F32),
+        ],
         compiler_params=params(),
         cost_estimate=cost(4 * slots * task_slots * TW * TW, (task_slots + slots) * TW * TW * 4),
         name="sum_integrals",
     )(task_count, tasks, integrals)
-    operator = (
-        sums.reshape(list_length, list_length, TW, TW)
-        .transpose(0, 2, 1, 3)
-        .reshape(list_length * TW, list_length * TW)
-    )
 
     virt = jnp.broadcast_to(virt_energy.reshape(tile_count, TW, 1), (tile_count, TW, 128))
     pair = pair_energy.reshape(1, row_count)
     blank = blank.reshape(per_res, TW, row_count)
-    operator, virt, pair = lax.optimization_barrier((operator, virt, pair))
-    depth = list_length * TW
+    operator_high, virt, pair = lax.optimization_barrier((operator_high, virt, pair))
+    virt, pair = in_vmem(virt), in_vmem(pair)
+    if keep:
+        operator_high, operator_low = in_vmem(operator_high), in_vmem(operator_low)
     products = pl.pallas_call(
         functools.partial(product_kernel, owners),
         out_shape=[piece] * owners,
-        in_specs=[SMEM_SPEC] * 3 + [VMEM_SPEC, HBM_SPEC] + [VMEM_SPEC] * (owners - 1),
+        in_specs=[SMEM_SPEC] * 3 + [VMEM_SPEC] * 2 + [HBM_SPEC] + [VMEM_SPEC] * (owners - 1),
         out_specs=[VMEM_SPEC] * owners,
         scratch_shapes=[
             pltpu.VMEM((CAP, TW, row_count), F32),
             pltpu.VMEM((depth, row_count), BF16),
             pltpu.VMEM((depth, row_count), BF16),
-            pltpu.VMEM((list_length, TW, row_count), F32),
+            pltpu.VMEM((row_count // 128, depth, 128), F32),
             pltpu.SemaphoreType.DMA((CAP,)),
         ],
         compiler_params=params(),
         cost_estimate=cost(6 * depth * depth * row_count, 4 * depth * (depth + 2 * row_count)),
         name="multiply_tiles",
-    )(amp_from, amp_self, res_to, operator, amplitudes, *fetched)
-    returned = [products[0]] + exchange(products[1:])
+    )(amp_from, amp_self, res_to, operator_high, operator_low, amplitudes, *fetched)
+    returned = [in_vmem(products[0])] + exchange(products[1:])
     return pl.pallas_call(
         functools.partial(final_kernel, owners, tile_count),
         out_shape=jax.ShapeDtypeStruct((per_res, TW, row_count), F32),

time: 91.8 us -> 86.3 us (0.940)
  waiting for transfers between devices: 23.3 us -> 40.4 us
  local copies, waits for them, and re-layouts: 10.5 us -> 1.12 us
  Pallas kernels: 21.7 us -> 14.9 us
  starting transfers between devices: 22.2 us -> 16.6 us
    ppermute x14, waiting for transfers between devices: 23.3 us -> 40.4 us  [exchange(): lax.ppermute(buffers[d - 1], 'tile', [(i, i ^ d) for i in range(owners)])]
    reshape x3 -> x0, local copies, waits for them, and re-layouts: 7.26 us -> none  [the longest x2 4.53 us: local(): sums.reshape(list_length, list_length, TW, TW).transpose(0, 2, 1, 3)]
    ppermute x14, starting transfers between devices: 22.2 us -> 16.6 us  [exchange(): lax.ppermute(buffers[d - 1], 'tile', [(i, i ^ d) for i in range(owners)])]
    pallas_call x1, Pallas kernels: 4.26 us -> 1.82 us  [local(): pl.pallas_call(functools.partial(maps_kernel, owners, per_amp, per_res),...]
    pallas_call x1, Pallas kernels: 8.12 us -> 6.48 us  [local(): pl.pallas_call(functools.partial(sum_kernel, list_length), grid=(steps,),...]
    pallas_call x1, Pallas kernels: 3.85 us -> 2.31 us  [local(): pl.pallas_call(functools.partial(product_kernel, owners), out_shape=[piec...]
    pallas_call x1, Pallas kernels: 3.03 us -> 2.05 us  [local(): pl.pallas_call(functools.partial(final_kernel, owners, tile_count), out_s...]
  transfers between devices with their start and end apart: 14 -> 14, of which waited for: 5 -> 8; matrix products, arithmetic and copies ran while one was open for 10% -> 0% of each run, Pallas kernels for 14% -> 10%
where the time goes in v5:
time: 86.3 us; the launch traced here: 85.1 us
  waiting for transfers between devices  40.4 us (47%)
  starting transfers between devices  16.6 us (19%)
  Pallas kernels  14.9 us (17%)
  blocking collectives  10.5 us (12%)
  local copies, waits for them, and re-layouts  1.12 us (1%)
    ppermute x14, waiting for transfers between devices, exchange(): lax.ppermute(buffers[d - 1], 'tile', [(i, i ^ d) for i in range(owners)])  40.4 us
    ppermute x14, starting transfers between devices, exchange(): lax.ppermute(buffers[d - 1], 'tile', [(i, i ^ d) for i in range(owners)])  16.6 us
    psum x1, blocking collectives, local(): lax.psum(jnp.where(spots, own_lists[None, :], 0), 'tile').reshape(-1)  10.5 us
    pallas_call x1, Pallas kernels, local(): pl.pallas_call(functools.partial(sum_kernel, list_length), grid=(steps,),...  6.48 us
    pallas_call x1, Pallas kernels, local(): pl.pallas_call(functools.partial(product_kernel, owners), out_shape=[piec...  2.31 us
    pallas_call x1, Pallas kernels, local(): pl.pallas_call(functools.partial(pack_kernel, owners, per_amp), out_shape...  2.28 us
    pallas_call x1, Pallas kernels, local(): pl.pallas_call(functools.partial(final_kernel, owners, tile_count), out_s...  2.05 us
    pallas_call x1, Pallas kernels, local(): pl.pallas_call(functools.partial(maps_kernel, owners, per_amp, per_res),...  1.82 us
  transfers between devices with their start and end apart: 14, of which 8 were waited for; matrix products, arithmetic and copies ran while one was open for 0% of the time, Pallas kernels for 10%

profile of v5, /device:TPU:12, one launch (start us, length us, event | category | flops | bytes accessed | tf_op | source)
XLA Modules:
  0.0 85.1 jit_solution(6772036324817532729)
XLA Ops:
  0.0 0.0 copy-start.5
  0.0 0.0 copy-start.2
  0.0 0.0 copy-start.4
  0.0 0.0 copy-start
  0.0 0.8 pad_add_fusion
  0.8 0.1 broadcast_select_fusion
  0.9 0.1 reshape.21
  1.0 10.5 %psum.7.lists_ref = s32[128]{0:T(128)S(1)} all-reduce(s32[128]{0:T(128)S(1)} %reshape.21), channel_id=1, replica_groups=mesh['mol'=2,'tile'=8,'rep'=2] {'tile'}, use_global_device_ids=true, to_apply=%region_0.1 | all-reduce | flops 128 | bytes 1024 | tf_op jit(solution)/shard_map/psum | solution.py:274
  11.5 0.0 copy-start.1
  11.5 0.7 copy-done.1
  12.1 2.3 %pack_tiles.1 = (f32[2,64,384]{2,1,0:T(8,128)S(1)}, f32[2,64,384]{2,1,0:T(8,128)S(1)}, f32[2,64,384]{2,1,0:T(8,128)S(1)}, f32[2,64,384]{2,1,0:T(8,128)S(1)}, f32...) custom-call(s32[1]{0:T(128)} %bitcast.me_ref, s32[128]{0:T(128)S(1)} %psum.7.lists_ref, ...), custom_call_target="tpu_custom_call" | custom-call | bytes 1572864 | tf_op jit(solution)/shard_map/pack_tiles/pallas_call | solution.py:284
  14.4 0.4 collective-permute-start
  14.9 1.5 %collective-permute-start.1 = (f32[2,64,384]{2,1,0:T(8,128)S(1)}, f32[2,64,384]{2,1,0:T(8,128)S(1)}, u32[]{:S(2)}, u32[]{:S(2)}) collective-permute-start(f32[2,64,384]{2,1,0:T(8,128)S(1)} %get-tuple-element.44), channel_id=1, source_target_pairs={{0,4},{2,6},{4,0},{6,2},{8,12},{10,14},{12,8},{14,10},{1,5},{3,7},... | collective-permute-start | bytes 589832 | tf_op jit(solution)/shard_map/ppermute | solution.py:279
  16.3 2.1 %collective-permute-start.2 = (f32[2,64,384]{2,1,0:T(8,128)S(1)}, f32[2,64,384]{2,1,0:T(8,128)S(1)}, u32[]{:S(2)}, u32[]{:S(2)}) collective-permute-start(f32[2,64,384]{2,1,0:T(8,128)S(1)} %get-tuple-element.45), channel_id=1, source_target_pairs={{0,8},{2,10},{4,12},{6,14},{8,0},{10,2},{12,4},{14,6},{1,9},{3,11}... | collective-permute-start | bytes 589832 | tf_op jit(solution)/shard_map/ppermute | solution.py:279
  18.4 1.8 %collective-permute-start.3 = (f32[2,64,384]{2,1,0:T(8,128)S(1)}, f32[2,64,384]{2,1,0:T(8,128)S(1)}, u32[]{:S(2)}, u32[]{:S(2)}) collective-permute-start(f32[2,64,384]{2,1,0:T(8,128)S(1)} %get-tuple-element.46), channel_id=1, source_target_pairs={{0,6},{2,4},{4,2},{6,0},{8,14},{10,12},{12,10},{14,8},{1,7},{3,5},... | collective-permute-start | bytes 589832 | tf_op jit(solution)/shard_map/ppermute | solution.py:279
  20.2 1.1 %collective-permute-start.4 = (f32[2,64,384]{2,1,0:T(8,128)S(1)}, f32[2,64,384]{2,1,0:T(8,128)S(1)}, u32[]{:S(2)}, u32[]{:S(2)}) collective-permute-start(f32[2,64,384]{2,1,0:T(8,128)S(1)} %get-tuple-element.47), channel_id=1, source_target_pairs={{0,10},{2,8},{4,14},{6,12},{8,2},{10,0},{12,6},{14,4},{1,11},{3,9}... | collective-permute-start | bytes 589832 | tf_op jit(solution)/shard_map/ppermute | solution.py:279
  21.4 5.3 %collective-permute-done.rest_0_ = f32[2,64,384]{2,1,0:T(8,128)S(1)} collective-permute-done((f32[2,64,384]{2,1,0:T(8,128)S(1)}, f32[2,64,384]{2,1,0:T(8,128)S(1)}, u32[]{:S(2)}, u32[]{:S(2)}) %collective-permute-start) | collective-permute-done | bytes 196640 | tf_op jit(solution)/shard_map/ppermute | solution.py:279
  26.6 0.3 collective-permute-start.5
  27.0 0.0 collective-permute-done.1.rest_1_
  27.0 1.8 %collective-permute-start.6 = (f32[2,64,384]{2,1,0:T(8,128)S(1)}, f32[2,64,384]{2,1,0:T(8,128)S(1)}, u32[]{:S(2)}, u32[]{:S(2)}) collective-permute-start(f32[2,64,384]{2,1,0:T(8,128)S(1)} %get-tuple-element.49), channel_id=1, source_target_pairs={{0,14},{2,12},{4,10},{6,8},{8,6},{10,4},{12,2},{14,0},{1,15},{3,13... | collective-permute-start | bytes 589832 | tf_op jit(solution)/shard_map/ppermute | solution.py:279
  29.5 0.0 copy-done.5
  29.5 0.0 copy-done.2
  29.5 1.8 %list_maps.1 = (s32[17]{0:T(128)S(4)}, s32[3]{0:T(128)S(4)}, s32[17]{0:T(128)S(4)}, s32[17]{0:T(128)S(4)}, s32[17]{0:T(128)S(4)}, /*index=5*/s32[17]{0:T(128)S(4)}) custom-call(s32[1]{0:T(128)} %bitcast.me_ref, s32[128]{0:T(128)S(1)} %psum.7.lists_ref, s32[200]{0:T(256)S(1)} %copy-done.1, s32[200]{0:T(256)S(1)} %copy-done.2), custom_call_target="tpu_custom_call" | custom-call | tf_op jit(solution)/shard_map/list_maps/pallas_call | solution.py:300
  31.3 0.0 copy-done.4
  31.3 0.1 broadcast_in_dim.32
  31.4 0.0 copy-done
  31.4 6.5 %sum_integrals.1 = (bf16[512,512]{1,0:T(8,128)(2,1)S(1)}, bf16[512,512]{1,0:T(8,128)(2,1)S(1)}, f32[1600,384]{1,0:T(8,128)}) custom-call(s32[1]{0:T(128)S(6)} %copy.14.count_ref, s32[2,512]{1,0:T(2,128)S(1)} %copy-done, f32[512,4096]{1,0:T(8,128)} %integrals_ref.1), custom_call_target="tpu_custom_call" | custom-call | flops 536870912 | bytes 9437184 | tf_op jit(solution)/shard_map/sum_integrals/pallas_call | solution.py:321
  37.9 0.3 broadcast_in_dim.33.virt
  38.2 0.9 %collective-permute-done.2.rest_2_ = f32[2,64,384]{2,1,0:T(8,128)S(1)} collective-permute-done((f32[2,64,384]{2,1,0:T(8,128)S(1)}, f32[2,64,384]{2,1,0:T(8,128)S(1)}, u32[]{:S(2)}, u32[]{:S(2)}) %collective-permute-start.2) | collective-permute-done | bytes 196640 | tf_op jit(solution)/shard_map/ppermute | solution.py:279
  39.0 0.0 collective-permute-done.3.rest_3_
  39.0 4.4 %collective-permute-done.4.rest_4_ = f32[2,64,384]{2,1,0:T(8,128)S(1)} collective-permute-done((f32[2,64,384]{2,1,0:T(8,128)S(1)}, f32[2,64,384]{2,1,0:T(8,128)S(1)}, u32[]{:S(2)}, u32[]{:S(2)}) %collective-permute-start.4) | collective-permute-done | bytes 196640 | tf_op jit(solution)/shard_map/ppermute | solution.py:279
  43.4 0.0 collective-permute-done.5.rest_5_
  43.4 4.5 %collective-permute-done.6.rest_6_ = f32[2,64,384]{2,1,0:T(8,128)S(1)} collective-permute-done((f32[2,64,384]{2,1,0:T(8,128)S(1)}, f32[2,64,384]{2,1,0:T(8,128)S(1)}, u32[]{:S(2)}, u32[]{:S(2)}) %collective-permute-start.6) | collective-permute-done | bytes 196640 | tf_op jit(solution)/shard_map/ppermute | solution.py:279
  47.9 0.0 copy-start.3
  47.9 2.3 %multiply_tiles.1 = (f32[2,64,384]{2,1,0:T(8,128)S(1)}, f32[2,64,384]{2,1,0:T(8,128)S(1)}, f32[2,64,384]{2,1,0:T(8,128)S(1)}, f32[2,64,384]{2,1,0:T(8,128)S(1)},...) custom-call(s32[17]{0:T(128)S(4)} %get-tuple-element.38.amp_from, ...), custom_call_target="tpu_custom_call" | custom-call | flops 603979776 | bytes 2621440 | tf_op jit(solution)/shard_map/multiply_tiles/pallas_call | solution.py:352
  50.2 0.1 collective-permute-start.7
  50.3 0.1 collective-permute-start.8
  50.4 3.4 %collective-permute-start.9 = (f32[2,64,384]{2,1,0:T(8,128)S(1)}, f32[2,64,384]{2,1,0:T(8,128)S(1)}, u32[]{:S(2)}, u32[]{:S(2)}) collective-permute-start(f32[2,64,384]{2,1,0:T(8,128)S(1)} %get-tuple-element.53), channel_id=1, source_target_pairs={{0,8},{2,10},{4,12},{6,14},{8,0},{10,2},{12,4},{14,6},{1,9},{3,11}... | collective-permute-start | bytes 589832 | tf_op jit(solution)/shard_map/ppermute | solution.py:279
  53.7 0.3 collective-permute-start.10
  54.1 2.1 %collective-permute-start.11 = (f32[2,64,384]{2,1,0:T(8,128)S(1)}, f32[2,64,384]{2,1,0:T(8,128)S(1)}, u32[]{:S(2)}, u32[]{:S(2)}) collective-permute-start(f32[2,64,384]{2,1,0:T(8,128)S(1)} %get-tuple-element.55), channel_id=1, source_target_pairs={{0,10},{2,8},{4,14},{6,12},{8,2},{10,0},{12,6},{14,4},{1,11},{3,9}... | collective-permute-start | bytes 589832 | tf_op jit(solution)/shard_map/ppermute | solution.py:279
  56.2 6.2 %collective-permute-done.7.rest_1_ = f32[2,64,384]{2,1,0:T(8,128)S(1)} collective-permute-done((f32[2,64,384]{2,1,0:T(8,128)S(1)}, f32[2,64,384]{2,1,0:T(8,128)S(1)}, u32[]{:S(2)}, u32[]{:S(2)}) %collective-permute-start.7) | collective-permute-done | bytes 196640 | tf_op jit(solution)/shard_map/ppermute | solution.py:279
  62.4 0.9 %collective-permute-start.12 = (f32[2,64,384]{2,1,0:T(8,128)S(1)}, f32[2,64,384]{2,1,0:T(8,128)S(1)}, u32[]{:S(2)}, u32[]{:S(2)}) collective-permute-start(f32[2,64,384]{2,1,0:T(8,128)S(1)} %get-tuple-element.56), channel_id=1, source_target_pairs={{0,2},{2,0},{4,6},{6,4},{8,10},{10,8},{12,14},{14,12},{1,3},{3,1},... | collective-permute-start | bytes 589832 | tf_op jit(solution)/shard_map/ppermute | solution.py:279
  63.2 0.0 collective-permute-done.8.rest_2_
  63.2 0.6 collective-permute-start.13
  63.8 10.2 %collective-permute-done.9.rest_3_ = f32[2,64,384]{2,1,0:T(8,128)S(1)} collective-permute-done((f32[2,64,384]{2,1,0:T(8,128)S(1)}, f32[2,64,384]{2,1,0:T(8,128)S(1)}, u32[]{:S(2)}, u32[]{:S(2)}) %collective-permute-start.9) | collective-permute-done | bytes 196640 | tf_op jit(solution)/shard_map/ppermute | solution.py:279
  74.0 0.0 collective-permute-done.10.rest_4_
  74.0 4.4 %collective-permute-done.11.rest_5_ = f32[2,64,384]{2,1,0:T(8,128)S(1)} collective-permute-done((f32[2,64,384]{2,1,0:T(8,128)S(1)}, f32[2,64,384]{2,1,0:T(8,128)S(1)}, u32[]{:S(2)}, u32[]{:S(2)}) %collective-permute-start.11) | collective-permute-done | bytes 196640 | tf_op jit(solution)/shard_map/ppermute | solution.py:279
  78.4 0.0 collective-permute-done.12.rest_6_
  78.4 4.7 %collective-permute-done.13.rest_7_ = f32[2,64,384]{2,1,0:T(8,128)S(1)} collective-permute-done((f32[2,64,384]{2,1,0:T(8,128)S(1)}, f32[2,64,384]{2,1,0:T(8,128)S(1)}, u32[]{:S(2)}, u32[]{:S(2)}) %collective-permute-start.13) | collective-permute-done | bytes 196640 | tf_op jit(solution)/shard_map/ppermute | solution.py:279
  83.1 0.0 copy-done.3
  83.1 2.1 %finish_tiles.1 = f32[25,64,384]{2,1,0:T(8,128)} custom-call(s32[17]{0:T(128)S(4)} %get-tuple-element.32.res_from, s32[17]{0:T(128)S(4)} %get-tuple-element.33.res_tile, s32[17]{0:T(128)S(4)} %get-tuple-element.34.res_first, f32[8]{0:T(128)S(1)} %copy-done.3, f32[1,384]{1,0:T(1,128)S(1)} %reshape.22.pair, ...), custom_call_target="tpu_custom_call", output_to_operand_aliasing={{}: (14, {})} | custom-call | bytes 2457600 | tf_op jit(solution)/shard_map/finish_tiles/pallas_call | solution.py:369
  (2 shorter events, 0.0 us)
Async XLA Ops:
  0.0 29.5 %copy-start.5 = (f32[384]{0:T(512)S(1)}, f32[384]{0:T(512)}, u32[]{:S(2)}) copy-start(f32[384]{0:T(512)} %param.19) | copy-start | bytes 4612
  0.0 29.5 %copy-start.2 = (s32[200]{0:T(256)S(1)}, s32[200]{0:T(256)}, u32[]{:S(2)}) copy-start(s32[200]{0:T(256)} %res_slot_ref.1) | copy-start | bytes 2404
  0.0 31.3 %copy-start.4 = (f32[1600]{0:T(1024)S(1)}, f32[1600]{0:T(1024)}, u32[]{:S(2)}) copy-start(f32[1600]{0:T(1024)} %param.20) | copy-start | bytes 19204
  0.0 31.4 %copy-start = (s32[2,512]{1,0:T(2,128)S(1)}, s32[2,512]{1,0:T(2,128)}, u32[]{:S(2)}) copy-start(s32[2,512]{1,0:T(2,128)} %tasks_ref.1) | copy-start | bytes 12292
  11.5 0.7 copy-start.1
  14.4 12.2 %collective-permute-start = (f32[2,64,384]{2,1,0:T(8,128)S(1)}, f32[2,64,384]{2,1,0:T(8,128)S(1)}, u32[]{:S(2)}, u32[]{:S(2)}) collective-permute-start(f32[2,64,384]{2,1,0:T(8,128)S(1)} %get-tuple-element.43), channel_id=1, source_target_pairs={{0,12},{2,14},{4,8},{6,10},{8,4},{10,6},{12,0},{14,2},{1,13},{3,15... | collective-permute-start | bytes 589832 | tf_op jit(solution)/shard_map/ppermute | solution.py:279
  14.9 12.1 %collective-permute-start.1 = (f32[2,64,384]{2,1,0:T(8,128)S(1)}, f32[2,64,384]{2,1,0:T(8,128)S(1)}, u32[]{:S(2)}, u32[]{:S(2)}) collective-permute-start(f32[2,64,384]{2,1,0:T(8,128)S(1)} %get-tuple-element.44), channel_id=1, source_target_pairs={{0,4},{2,6},{4,0},{6,2},{8,12},{10,14},{12,8},{14,10},{1,5},{3,7},... | collective-permute-start | bytes 589832 | tf_op jit(solution)/shard_map/ppermute | solution.py:279
  16.3 22.7 %collective-permute-start.2 = (f32[2,64,384]{2,1,0:T(8,128)S(1)}, f32[2,64,384]{2,1,0:T(8,128)S(1)}, u32[]{:S(2)}, u32[]{:S(2)}) collective-permute-start(f32[2,64,384]{2,1,0:T(8,128)S(1)} %get-tuple-element.45), channel_id=1, source_target_pairs={{0,8},{2,10},{4,12},{6,14},{8,0},{10,2},{12,4},{14,6},{1,9},{3,11}... | collective-permute-start | bytes 589832 | tf_op jit(solution)/shard_map/ppermute | solution.py:279
  18.4 20.6 %collective-permute-start.3 = (f32[2,64,384]{2,1,0:T(8,128)S(1)}, f32[2,64,384]{2,1,0:T(8,128)S(1)}, u32[]{:S(2)}, u32[]{:S(2)}) collective-permute-start(f32[2,64,384]{2,1,0:T(8,128)S(1)} %get-tuple-element.46), channel_id=1, source_target_pairs={{0,6},{2,4},{4,2},{6,0},{8,14},{10,12},{12,10},{14,8},{1,7},{3,5},... | collective-permute-start | bytes 589832 | tf_op jit(solution)/shard_map/ppermute | solution.py:279
  20.2 23.2 %collective-permute-start.4 = (f32[2,64,384]{2,1,0:T(8,128)S(1)}, f32[2,64,384]{2,1,0:T(8,128)S(1)}, u32[]{:S(2)}, u32[]{:S(2)}) collective-permute-start(f32[2,64,384]{2,1,0:T(8,128)S(1)} %get-tuple-element.47), channel_id=1, source_target_pairs={{0,10},{2,8},{4,14},{6,12},{8,2},{10,0},{12,6},{14,4},{1,11},{3,9}... | collective-permute-start | bytes 589832 | tf_op jit(solution)/shard_map/ppermute | solution.py:279
  26.6 16.8 %collective-permute-start.5 = (f32[2,64,384]{2,1,0:T(8,128)S(1)}, f32[2,64,384]{2,1,0:T(8,128)S(1)}, u32[]{:S(2)}, u32[]{:S(2)}) collective-permute-start(f32[2,64,384]{2,1,0:T(8,128)S(1)} %get-tuple-element.48), channel_id=1, source_target_pairs={{0,2},{2,0},{4,6},{6,4},{8,10},{10,8},{12,14},{14,12},{1,3},{3,1},... | collective-permute-start | bytes 589832 | tf_op jit(solution)/shard_map/ppermute | solution.py:279
  27.0 20.9 %collective-permute-start.6 = (f32[2,64,384]{2,1,0:T(8,128)S(1)}, f32[2,64,384]{2,1,0:T(8,128)S(1)}, u32[]{:S(2)}, u32[]{:S(2)}) collective-permute-start(f32[2,64,384]{2,1,0:T(8,128)S(1)} %get-tuple-element.49), channel_id=1, source_target_pairs={{0,14},{2,12},{4,10},{6,8},{8,6},{10,4},{12,2},{14,0},{1,15},{3,13... | collective-permute-start | bytes 589832 | tf_op jit(solution)/shard_map/ppermute | solution.py:279
  47.9 35.2 %copy-start.3 = (f32[8]{0:T(128)S(1)}, f32[8]{0:T(128)}, u32[]{:S(2)}) copy-start(f32[8]{0:T(128)} %window.1) | copy-start | bytes 100
  50.2 12.2 %collective-permute-start.7 = (f32[2,64,384]{2,1,0:T(8,128)S(1)}, f32[2,64,384]{2,1,0:T(8,128)S(1)}, u32[]{:S(2)}, u32[]{:S(2)}) collective-permute-start(f32[2,64,384]{2,1,0:T(8,128)S(1)} %get-tuple-element.51), channel_id=1, source_target_pairs={{0,12},{2,14},{4,8},{6,10},{8,4},{10,6},{12,0},{14,2},{1,13},{3,15... | collective-permute-start | bytes 589832 | tf_op jit(solution)/shard_map/ppermute | solution.py:279
  50.3 13.0 %collective-permute-start.8 = (f32[2,64,384]{2,1,0:T(8,128)S(1)}, f32[2,64,384]{2,1,0:T(8,128)S(1)}, u32[]{:S(2)}, u32[]{:S(2)}) collective-permute-start(f32[2,64,384]{2,1,0:T(8,128)S(1)} %get-tuple-element.52), channel_id=1, source_target_pairs={{0,4},{2,6},{4,0},{6,2},{8,12},{10,14},{12,8},{14,10},{1,5},{3,7},... | collective-permute-start | bytes 589832 | tf_op jit(solution)/shard_map/ppermute | solution.py:279
  50.4 23.7 %collective-permute-start.9 = (f32[2,64,384]{2,1,0:T(8,128)S(1)}, f32[2,64,384]{2,1,0:T(8,128)S(1)}, u32[]{:S(2)}, u32[]{:S(2)}) collective-permute-start(f32[2,64,384]{2,1,0:T(8,128)S(1)} %get-tuple-element.53), channel_id=1, source_target_pairs={{0,8},{2,10},{4,12},{6,14},{8,0},{10,2},{12,4},{14,6},{1,9},{3,11}... | collective-permute-start | bytes 589832 | tf_op jit(solution)/shard_map/ppermute | solution.py:279
  53.7 20.3 %collective-permute-start.10 = (f32[2,64,384]{2,1,0:T(8,128)S(1)}, f32[2,64,384]{2,1,0:T(8,128)S(1)}, u32[]{:S(2)}, u32[]{:S(2)}) collective-permute-start(f32[2,64,384]{2,1,0:T(8,128)S(1)} %get-tuple-element.54), channel_id=1, source_target_pairs={{0,6},{2,4},{4,2},{6,0},{8,14},{10,12},{12,10},{14,8},{1,7},{3,5},... | collective-permute-start | bytes 589832 | tf_op jit(solution)/shard_map/ppermute | solution.py:279
  54.1 24.3 %collective-permute-start.11 = (f32[2,64,384]{2,1,0:T(8,128)S(1)}, f32[2,64,384]{2,1,0:T(8,128)S(1)}, u32[]{:S(2)}, u32[]{:S(2)}) collective-permute-start(f32[2,64,384]{2,1,0:T(8,128)S(1)} %get-tuple-element.55), channel_id=1, source_target_pairs={{0,10},{2,8},{4,14},{6,12},{8,2},{10,0},{12,6},{14,4},{1,11},{3,9}... | collective-permute-start | bytes 589832 | tf_op jit(solution)/shard_map/ppermute | solution.py:279
  62.4 16.0 %collective-permute-start.12 = (f32[2,64,384]{2,1,0:T(8,128)S(1)}, f32[2,64,384]{2,1,0:T(8,128)S(1)}, u32[]{:S(2)}, u32[]{:S(2)}) collective-permute-start(f32[2,64,384]{2,1,0:T(8,128)S(1)} %get-tuple-element.56), channel_id=1, source_target_pairs={{0,2},{2,0},{4,6},{6,4},{8,10},{10,8},{12,14},{14,12},{1,3},{3,1},... | collective-permute-start | bytes 589832 | tf_op jit(solution)/shard_map/ppermute | solution.py:279
  63.2 19.8 %collective-permute-start.13 = (f32[2,64,384]{2,1,0:T(8,128)S(1)}, f32[2,64,384]{2,1,0:T(8,128)S(1)}, u32[]{:S(2)}, u32[]{:S(2)}) collective-permute-start(f32[2,64,384]{2,1,0:T(8,128)S(1)} %get-tuple-element.57), channel_id=1, source_target_pairs={{0,14},{2,12},{4,10},{6,8},{8,6},{10,4},{12,2},{14,0},{1,15},{3,13... | collective-permute-start | bytes 589832 | tf_op jit(solution)/shard_map/ppermute | solution.py:279

commit v6 on v5

--- a/solution.py
+++ b/solution.py
@@ -50,29 +50,33 @@
     low = me * per_owner
     clear(picked, owners * CAP, -1)
 
-    @pl.loop(0, owners)
-    def _(partner):
+    def copy(d, k):
+        local = picked[d * CAP + k]
+        source = amplitudes.at[jnp.maximum(local, 0)]
+        return local, pltpu.make_async_copy(source, outs[d - 1].at[k], sems.at[d * CAP + k])
+
+    for d in class_order(owners):
+        first = jnp.bitwise_xor(me, d) * 2 * list_length
+
         def note(j, count):
-            local = amp_slot_ref[lists_ref[partner * 2 * list_length + j]] - low
+            local = amp_slot_ref[lists_ref[first + j]] - low
             mine = (local >= 0) & (local < per_owner)
-            picked[jnp.where(mine, partner * CAP + count, owners * CAP)] = local
+            picked[jnp.where(mine, d * CAP + count, owners * CAP)] = local
             return count + mine.astype(jnp.int32)
 
         lax.fori_loop(0, list_length, note, jnp.int32(0), unroll=8)
-
-    for step in ("start", "wait"):
-        for d in range(owners - 1, 0, -1):
-            for k in range(CAP):
-                local = picked[jnp.bitwise_xor(me, d) * CAP + k]
-                moved = pltpu.make_async_copy(
-                    amplitudes.at[jnp.maximum(local, 0)], outs[d - 1].at[k], sems.at[d * CAP + k]
-                )
-                pl.when(local >= 0)(getattr(moved, step))
+        for k in range(CAP):
+            local, moved = copy(d, k)
+            pl.when(local >= 0)(moved.start)
+    for d in class_order(owners):
+        for k in range(CAP):
+            local, moved = copy(d, k)
+            pl.when(local >= 0)(moved.wait)
 
 
 def maps_kernel(
     owners, per_amp, per_res, me_ref, lists_ref, amp_slot_ref, res_slot_ref,
-    amp_from, amp_self, res_to, res_from, res_tile, res_first, seen, taken,
+    window, pair, virt, amp_from, amp_self, res_to, res_from, res_first, inverse, res_tile, seen, taken,
 ):
     list_length = lists_ref.shape[0] // owners // 2
     spots = owners * CAP
@@ -118,15 +122,24 @@
 
         lax.fori_loop(0, list_length, note, jnp.int32(0), unroll=8)
 
-    def firsts(spot, carry):
-        local = res_from[spot]
-        known = taken[jnp.where(local >= 0, local, per_res)]
-        first = jnp.where(known < 0, spot, known)
-        taken[jnp.where(local >= 0, local, per_res)] = jnp.where(local >= 0, first, -1)
-        res_first[spot] = jnp.where(local >= 0, first, -1)
-        return carry
-
-    lax.fori_loop(0, spots, firsts, 0, unroll=4)
+    for d in [0] + class_order(owners):
+        for spot in range(d * CAP, d * CAP + CAP):
+            local = res_from[spot]
+            at = jnp.where(local >= 0, local, per_res)
+            first = jnp.where(local < 0, -1, jnp.where(taken[at] < 0, spot, taken[at]))
+            taken[at] = first
+            res_first[spot] = first
+
+    tiles, columns = virt.shape[0], pair.shape[1]
+
+    @pl.loop(0, spots)
+    def _(spot):
+        @pl.when(res_from[spot] >= 0)
+        def _():
+            tile = res_tile[spot]
+            base = pair[...] - window[lax.div(tile, jnp.int32(tiles))]
+            column = virt[lax.rem(tile, jnp.int32(tiles))]
+            inverse[spot] = 1.0 / (base - jnp.concatenate([column] * (columns // 128), axis=1))
 
 
 def sum_kernel(list_length, count_ref, tasks_ref, integrals_ref, high_ref, low_ref, blank_ref, hits, sums, matrix):
@@ -214,34 +227,26 @@
                     outs[d][k, :, c * 128 : (c + 1) * 128] = totals[c, pl.ds(g, TW, stride=rows // TW), :]
 
 
-def final_kernel(owners, tiles, res_from, res_tile, res_first, window, pair, virt, *rest):
-    arrived, (_, out, sums, sems) = dict(zip([0] + class_order(owners), rest[:owners])), rest[-4:]
-    spots = [(d, k, d * CAP + k) for d in range(owners) for k in range(CAP)]
-    for d, k, spot in spots:
+def final_kernel(owners, res_from, res_first, inverse, *rest):
+    arrived, (_, out, sums, sems) = rest[:owners], rest[-4:]
+    spots = [(at, k, d * CAP + k) for at, d in enumerate([0] + class_order(owners)) for k in range(CAP)]
+    for at, k, spot in spots:
         first = res_first[spot]
 
         @pl.when(first == spot)
         def _():
-            sums[spot] = arrived[d][k]
-
-        @pl.when((first >= 0) & (first < spot))
+            sums[spot] = arrived[at][k] * inverse[spot]
+
+        @pl.when((first >= 0) & (first != spot))
         def _():
-            sums[first] = sums[first] + arrived[d][k]
+            sums[first] = sums[first] + arrived[at][k] * inverse[spot]
 
     def write(spot):
         return pltpu.make_async_copy(sums.at[spot], out.at[jnp.maximum(res_from[spot], 0)], sems.at[spot])
 
-    for d, k, spot in spots:
-
-        @pl.when(res_first[spot] == spot)
-        def _():
-            tile = res_tile[spot]
-            base = pair[...] - window[tile // tiles]
-            below = base - jnp.concatenate([virt[tile % tiles]] * (base.shape[1] // 128), axis=1)
-            sums[spot] = sums[spot] / below
-            write(spot).start()
-
-    for d, k, spot in spots:
+    for _, _, spot in spots:
+        pl.when(res_first[spot] == spot)(write(spot).start)
+    for _, _, spot in spots:
         pl.when(res_first[spot] == spot)(write(spot).wait)
 
 
@@ -269,6 +274,7 @@
 
     amplitudes = pltpu.with_memory_space_constraint(amplitudes, pltpu.HBM)
     integrals = pltpu.with_memory_space_constraint(integrals, pltpu.HBM)
+    amp_slot = pltpu.with_memory_space_constraint(amp_slot, pltpu.HBM)
     own_lists = jnp.concatenate([need_amp, needed_residual_tiles])
     spots = jnp.arange(owners, dtype=jnp.int32)[:, None] == me
     lists = lax.psum(jnp.where(spots, own_lists[None, :], 0), "tile").reshape(-1)
@@ -296,21 +302,28 @@
     )(me_ref, lists, amp_slot, amplitudes)
     fetched = exchange(packed)
 
+    virt = in_vmem(jnp.broadcast_to(virt_energy.reshape(tile_count, TW, 1), (tile_count, TW, 128)))
+    pair = in_vmem(pair_energy.reshape(1, row_count))
     small = pltpu.SMEM((owners * CAP + 1,), jnp.int32)
-    amp_from, amp_self, res_to, res_from, res_tile, res_first = pl.pallas_call(
+    *maps, inverse = pl.pallas_call(
         functools.partial(maps_kernel, owners, per_amp, per_res),
-        out_shape=[small, pltpu.SMEM((CAP + 1,), jnp.int32), small, small, small, small],
-        in_specs=[SMEM_SPEC] * 4,
-        out_specs=[SMEM_SPEC] * 6,
-        scratch_shapes=[pltpu.SMEM((owners,), jnp.int32), pltpu.SMEM((per_res + 1,), jnp.int32)],
+        out_shape=[small, pltpu.SMEM((CAP + 1,), jnp.int32), small, small, small]
+        + [pltpu.VMEM((owners * CAP, TW, row_count), F32)],
+        in_specs=[SMEM_SPEC] * 5 + [VMEM_SPEC] * 2,
+        out_specs=[SMEM_SPEC] * 5 + [VMEM_SPEC],
+        scratch_shapes=[
+            pltpu.SMEM((owners * CAP + 1,), jnp.int32),
+            pltpu.SMEM((owners,), jnp.int32),
+            pltpu.SMEM((per_res + 1,), jnp.int32),
+        ],
         compiler_params=params(),
+        cost_estimate=cost(0, owners * CAP * TW * row_count * 4),
         name="list_maps",
-    )(me_ref, lists, amp_slot, res_slot)
-
-    amp_from, amp_self, res_to, res_from, res_tile, res_first = (
-        pltpu.with_memory_space_constraint(x, pltpu.SMEM)
-        for x in (amp_from, amp_self, res_to, res_from, res_tile, res_first)
+    )(me_ref, lists, amp_slot, res_slot, window_energy, pair, virt)
+    amp_from, amp_self, res_to, res_from, res_first = (
+        pltpu.with_memory_space_constraint(x, pltpu.SMEM) for x in maps
     )
+    inverse = in_vmem(inverse)
     block = 1024
     steps = TW * TW // block
     depth = list_length * TW
@@ -342,11 +355,7 @@
         name="sum_integrals",
     )(task_count, tasks, integrals)
 
-    virt = jnp.broadcast_to(virt_energy.reshape(tile_count, TW, 1), (tile_count, TW, 128))
-    pair = pair_energy.reshape(1, row_count)
     blank = blank.reshape(per_res, TW, row_count)
-    operator_high, virt, pair = lax.optimization_barrier((operator_high, virt, pair))
-    virt, pair = in_vmem(virt), in_vmem(pair)
     if keep:
         operator_high, operator_low = in_vmem(operator_high), in_vmem(operator_low)
     products = pl.pallas_call(
@@ -367,19 +376,19 @@
     )(amp_from, amp_self, res_to, operator_high, operator_low, amplitudes, *fetched)
     returned = [in_vmem(products[0])] + exchange(products[1:])
     return pl.pallas_call(
-        functools.partial(final_kernel, owners, tile_count),
+        functools.partial(final_kernel, owners),
         out_shape=jax.ShapeDtypeStruct((per_res, TW, row_count), F32),
-        in_specs=[SMEM_SPEC] * 4 + [VMEM_SPEC] * (2 + owners) + [HBM_SPEC],
+        in_specs=[SMEM_SPEC] * 2 + [VMEM_SPEC] * (1 + owners) + [HBM_SPEC],
         out_specs=HBM_SPEC,
         scratch_shapes=[
             pltpu.VMEM((owners * CAP, TW, row_count), F32),
             pltpu.SemaphoreType.DMA((owners * CAP,)),
         ],
-        input_output_aliases={6 + owners: 0},
+        input_output_aliases={3 + owners: 0},
         compiler_params=params(),
         cost_estimate=cost(0, per_res * TW * row_count * 4),
         name="finish_tiles",
-    )(res_from, res_tile, res_first, window_energy, pair, virt, *returned, blank)
+    )(res_from, res_first, inverse, *returned, blank)
 
 
 def solution(mesh):

time: 86.3 us -> 84.9 us (0.984)
  starting transfers between devices: 16.6 us -> 17.6 us
  waiting for transfers between devices: 40.4 us -> 39.5 us
    ppermute x14, starting transfers between devices: 16.6 us -> 17.6 us  [exchange(): lax.ppermute(buffers[d - 1], 'tile', [(i, i ^ d) for i in range(owners)])]
    pallas_call x1, Pallas kernels: 2.05 us -> 1.18 us  [local(): pl.pallas_call(functools.partial(final_kernel, owners), out_shape=jax.Sha...]
  transfers between devices with their start and end apart: 14 -> 14, of which waited for: 8 -> 8; matrix products, arithmetic and copies ran while one was open for 0% -> 0% of each run, Pallas kernels for 10% -> 11%
where the time goes in v6:
time: 84.9 us; the launch traced here: 84 us
  waiting for transfers between devices  39.5 us (47%)
  starting transfers between devices  17.6 us (21%)
  Pallas kernels  14.4 us (17%)
  blocking collectives  10.5 us (12%)
  other arithmetic  0.86 us (1%)
    ppermute x14, waiting for transfers between devices, exchange(): lax.ppermute(buffers[d - 1], 'tile', [(i, i ^ d) for i in range(owners)])  39.5 us
    ppermute x14, starting transfers between devices, exchange(): lax.ppermute(buffers[d - 1], 'tile', [(i, i ^ d) for i in range(owners)])  17.6 us
    psum x1, blocking collectives, local(): lax.psum(jnp.where(spots, own_lists[None, :], 0), 'tile').reshape(-1)  10.5 us
    pallas_call x1, Pallas kernels, local(): pl.pallas_call(functools.partial(sum_kernel, list_length), grid=(steps,),...  6.49 us
    pallas_call x1, Pallas kernels, local(): pl.pallas_call(functools.partial(maps_kernel, owners, per_amp, per_res),...  2.35 us
    pallas_call x1, Pallas kernels, local(): pl.pallas_call(functools.partial(product_kernel, owners), out_shape=[piec...  2.3 us
    pallas_call x1, Pallas kernels, local(): pl.pallas_call(functools.partial(pack_kernel, owners, per_amp), out_shape...  2.06 us
  transfers between devices with their start and end apart: 14, of which 8 were waited for; matrix products, arithmetic and copies ran while one was open for 0% of the time, Pallas kernels for 11%

profile of v6, /device:TPU:12, one launch (start us, length us, event | category | flops | bytes accessed | tf_op | source)
XLA Modules:
  0.0 84.0 jit_solution(11096088526234339992)
XLA Ops:
  0.0 0.0 copy-start.4
  0.0 0.0 copy-start.3
  0.0 0.0 copy-start.2
  0.0 0.0 copy-start.1
  0.0 0.0 copy-start
  0.0 0.8 pad_add_fusion
  0.8 0.1 broadcast_select_fusion
  0.9 0.1 reshape.21
  1.0 10.5 %psum.7.lists_ref = s32[128]{0:T(128)S(1)} all-reduce(s32[128]{0:T(128)S(1)} %reshape.21), channel_id=1, replica_groups=mesh['mol'=2,'tile'=8,'rep'=2] {'tile'}, use_global_device_ids=true, to_apply=%region_0.1 | all-reduce | flops 128 | bytes 1024 | tf_op jit(solution)/shard_map/psum | solution.py:280
  11.5 2.1 %pack_tiles.1 = (f32[2,64,384]{2,1,0:T(8,128)S(1)}, f32[2,64,384]{2,1,0:T(8,128)S(1)}, f32[2,64,384]{2,1,0:T(8,128)S(1)}, f32[2,64,384]{2,1,0:T(8,128)S(1)}, f32...) custom-call(s32[1]{0:T(128)} %bitcast.me_ref, s32[128]{0:T(128)S(1)} %psum.7.lists_ref, ...), custom_call_target="tpu_custom_call" | custom-call | bytes 1572864 | tf_op jit(solution)/shard_map/pack_tiles/pallas_call | solution.py:290
  13.5 0.7 collective-permute-start
  14.3 1.3 %collective-permute-start.1 = (f32[2,64,384]{2,1,0:T(8,128)S(1)}, f32[2,64,384]{2,1,0:T(8,128)S(1)}, u32[]{:S(2)}, u32[]{:S(2)}) collective-permute-start(f32[2,64,384]{2,1,0:T(8,128)S(1)} %get-tuple-element.38), channel_id=1, source_target_pairs={{0,4},{2,6},{4,0},{6,2},{8,12},{10,14},{12,8},{14,10},{1,5},{3,7},... | collective-permute-start | bytes 589832 | tf_op jit(solution)/shard_map/ppermute | solution.py:285
  15.5 2.0 %collective-permute-start.2 = (f32[2,64,384]{2,1,0:T(8,128)S(1)}, f32[2,64,384]{2,1,0:T(8,128)S(1)}, u32[]{:S(2)}, u32[]{:S(2)}) collective-permute-start(f32[2,64,384]{2,1,0:T(8,128)S(1)} %get-tuple-element.39), channel_id=1, source_target_pairs={{0,8},{2,10},{4,12},{6,14},{8,0},{10,2},{12,4},{14,6},{1,9},{3,11}... | collective-permute-start | bytes 589832 | tf_op jit(solution)/shard_map/ppermute | solution.py:285
  17.6 2.2 %collective-permute-start.3 = (f32[2,64,384]{2,1,0:T(8,128)S(1)}, f32[2,64,384]{2,1,0:T(8,128)S(1)}, u32[]{:S(2)}, u32[]{:S(2)}) collective-permute-start(f32[2,64,384]{2,1,0:T(8,128)S(1)} %get-tuple-element.40), channel_id=1, source_target_pairs={{0,6},{2,4},{4,2},{6,0},{8,14},{10,12},{12,10},{14,8},{1,7},{3,5},... | collective-permute-start | bytes 589832 | tf_op jit(solution)/shard_map/ppermute | solution.py:285
  19.8 0.7 collective-permute-start.4
  20.5 5.3 %collective-permute-done.rest_0_ = f32[2,64,384]{2,1,0:T(8,128)S(1)} collective-permute-done((f32[2,64,384]{2,1,0:T(8,128)S(1)}, f32[2,64,384]{2,1,0:T(8,128)S(1)}, u32[]{:S(2)}, u32[]{:S(2)}) %collective-permute-start) | collective-permute-done | bytes 196640 | tf_op jit(solution)/shard_map/ppermute | solution.py:285
  25.8 0.7 collective-permute-start.5
  26.5 0.0 collective-permute-done.1.rest_1_
  26.5 1.9 %collective-permute-start.6 = (f32[2,64,384]{2,1,0:T(8,128)S(1)}, f32[2,64,384]{2,1,0:T(8,128)S(1)}, u32[]{:S(2)}, u32[]{:S(2)}) collective-permute-start(f32[2,64,384]{2,1,0:T(8,128)S(1)} %get-tuple-element.43), channel_id=1, source_target_pairs={{0,14},{2,12},{4,10},{6,8},{8,6},{10,4},{12,2},{14,0},{1,15},{3,13... | collective-permute-start | bytes 589832 | tf_op jit(solution)/shard_map/ppermute | solution.py:285
  29.0 0.0 copy-done.4
  29.0 0.0 copy-done.3
  29.1 0.1 broadcast_in_dim.32
  29.1 0.3 broadcast_in_dim.33.virt
  29.4 0.0 copy-done.2
  29.4 0.0 copy-done.1
  29.4 2.4 %list_maps.1 = (s32[17]{0:T(128)S(4)}, s32[3]{0:T(128)S(4)}, s32[17]{0:T(128)S(4)}, s32[17]{0:T(128)S(4)}, s32[17]{0:T(128)S(4)}, /*index=5*/f32[16,64,384]{2,1,0:T(8,128)S(1)}) custom-call(s32[1]{0:T(128)} %bitcast.me_ref, s32[128]{0:T(128)S(1)} %psum.7.lists_ref, s32[200]{0:T(256)} %amp_slot_ref.3, s32[200]{0:T(256)S(1)} %copy-done.1, f32[8]{0:T(128)S(1)} %copy-done.2, ...), custom_call_target="tpu_custom_call" | custom-call | bytes 1572864 | tf_op jit(solution)/shard_map/list_maps/pallas_call | solution.py:308
  31.8 0.0 copy-done
  31.8 6.5 %sum_integrals.1 = (bf16[512,512]{1,0:T(8,128)(2,1)S(1)}, bf16[512,512]{1,0:T(8,128)(2,1)S(1)}, f32[1600,384]{1,0:T(8,128)}) custom-call(s32[1]{0:T(128)S(6)} %copy.14.count_ref, s32[2,512]{1,0:T(2,128)S(1)} %copy-done, f32[512,4096]{1,0:T(8,128)} %integrals_ref.1), custom_call_target="tpu_custom_call" | custom-call | flops 536870912 | bytes 9437184 | tf_op jit(solution)/shard_map/sum_integrals/pallas_call | solution.py:334
  38.3 0.1 collective-permute-done.2.rest_2_
  38.4 0.0 collective-permute-done.3.rest_3_
  38.4 4.4 %collective-permute-done.4.rest_4_ = f32[2,64,384]{2,1,0:T(8,128)S(1)} collective-permute-done((f32[2,64,384]{2,1,0:T(8,128)S(1)}, f32[2,64,384]{2,1,0:T(8,128)S(1)}, u32[]{:S(2)}, u32[]{:S(2)}) %collective-permute-start.4) | collective-permute-done | bytes 196640 | tf_op jit(solution)/shard_map/ppermute | solution.py:285
  42.8 0.0 collective-permute-done.5.rest_5_
  42.8 4.4 %collective-permute-done.6.rest_6_ = f32[2,64,384]{2,1,0:T(8,128)S(1)} collective-permute-done((f32[2,64,384]{2,1,0:T(8,128)S(1)}, f32[2,64,384]{2,1,0:T(8,128)S(1)}, u32[]{:S(2)}, u32[]{:S(2)}) %collective-permute-start.6) | collective-permute-done | bytes 196640 | tf_op jit(solution)/shard_map/ppermute | solution.py:285
  47.2 2.3 %multiply_tiles.1 = (f32[2,64,384]{2,1,0:T(8,128)S(1)}, f32[2,64,384]{2,1,0:T(8,128)S(1)}, f32[2,64,384]{2,1,0:T(8,128)S(1)}, f32[2,64,384]{2,1,0:T(8,128)S(1)},...) custom-call(s32[17]{0:T(128)S(4)} %get-tuple-element.32.amp_from, ...), custom_call_target="tpu_custom_call" | custom-call | flops 603979776 | bytes 2621440 | tf_op jit(solution)/shard_map/multiply_tiles/pallas_call | solution.py:361
  49.5 0.4 collective-permute-start.7
  49.9 0.0 collective-permute-start.8
  49.9 3.1 %collective-permute-start.9 = (f32[2,64,384]{2,1,0:T(8,128)S(1)}, f32[2,64,384]{2,1,0:T(8,128)S(1)}, u32[]{:S(2)}, u32[]{:S(2)}) collective-permute-start(f32[2,64,384]{2,1,0:T(8,128)S(1)} %get-tuple-element.47), channel_id=1, source_target_pairs={{0,8},{2,10},{4,12},{6,14},{8,0},{10,2},{12,4},{14,6},{1,9},{3,11}... | collective-permute-start | bytes 589832 | tf_op jit(solution)/shard_map/ppermute | solution.py:285
  53.0 0.9 %collective-permute-start.10 = (f32[2,64,384]{2,1,0:T(8,128)S(1)}, f32[2,64,384]{2,1,0:T(8,128)S(1)}, u32[]{:S(2)}, u32[]{:S(2)}) collective-permute-start(f32[2,64,384]{2,1,0:T(8,128)S(1)} %get-tuple-element.48), channel_id=1, source_target_pairs={{0,6},{2,4},{4,2},{6,0},{8,14},{10,12},{12,10},{14,8},{1,7},{3,5},... | collective-permute-start | bytes 589832 | tf_op jit(solution)/shard_map/ppermute | solution.py:285
  53.9 1.8 %collective-permute-start.11 = (f32[2,64,384]{2,1,0:T(8,128)S(1)}, f32[2,64,384]{2,1,0:T(8,128)S(1)}, u32[]{:S(2)}, u32[]{:S(2)}) collective-permute-start(f32[2,64,384]{2,1,0:T(8,128)S(1)} %get-tuple-element.49), channel_id=1, source_target_pairs={{0,10},{2,8},{4,14},{6,12},{8,2},{10,0},{12,6},{14,4},{1,11},{3,9}... | collective-permute-start | bytes 589832 | tf_op jit(solution)/shard_map/ppermute | solution.py:285
  55.7 5.9 %collective-permute-done.7.rest_1_ = f32[2,64,384]{2,1,0:T(8,128)S(1)} collective-permute-done((f32[2,64,384]{2,1,0:T(8,128)S(1)}, f32[2,64,384]{2,1,0:T(8,128)S(1)}, u32[]{:S(2)}, u32[]{:S(2)}) %collective-permute-start.7) | collective-permute-done | bytes 196640 | tf_op jit(solution)/shard_map/ppermute | solution.py:285
  61.7 1.4 %collective-permute-start.12 = (f32[2,64,384]{2,1,0:T(8,128)S(1)}, f32[2,64,384]{2,1,0:T(8,128)S(1)}, u32[]{:S(2)}, u32[]{:S(2)}) collective-permute-start(f32[2,64,384]{2,1,0:T(8,128)S(1)} %get-tuple-element.50), channel_id=1, source_target_pairs={{0,2},{2,0},{4,6},{6,4},{8,10},{10,8},{12,14},{14,12},{1,3},{3,1},... | collective-permute-start | bytes 589832 | tf_op jit(solution)/shard_map/ppermute | solution.py:285
  63.1 0.0 collective-permute-done.8.rest_2_
  63.1 0.4 collective-permute-start.13
  63.4 10.1 %collective-permute-done.9.rest_3_ = f32[2,64,384]{2,1,0:T(8,128)S(1)} collective-permute-done((f32[2,64,384]{2,1,0:T(8,128)S(1)}, f32[2,64,384]{2,1,0:T(8,128)S(1)}, u32[]{:S(2)}, u32[]{:S(2)}) %collective-permute-start.9) | collective-permute-done | bytes 196640 | tf_op jit(solution)/shard_map/ppermute | solution.py:285
  73.5 0.0 collective-permute-done.10.rest_4_
  73.6 4.1 %collective-permute-done.11.rest_5_ = f32[2,64,384]{2,1,0:T(8,128)S(1)} collective-permute-done((f32[2,64,384]{2,1,0:T(8,128)S(1)}, f32[2,64,384]{2,1,0:T(8,128)S(1)}, u32[]{:S(2)}, u32[]{:S(2)}) %collective-permute-start.11) | collective-permute-done | bytes 196640 | tf_op jit(solution)/shard_map/ppermute | solution.py:285
  77.6 0.0 collective-permute-done.12.rest_6_
  77.6 5.3 %collective-permute-done.13.rest_7_ = f32[2,64,384]{2,1,0:T(8,128)S(1)} collective-permute-done((f32[2,64,384]{2,1,0:T(8,128)S(1)}, f32[2,64,384]{2,1,0:T(8,128)S(1)}, u32[]{:S(2)}, u32[]{:S(2)}) %collective-permute-start.13) | collective-permute-done | bytes 196640 | tf_op jit(solution)/shard_map/ppermute | solution.py:285
  82.9 1.2 %finish_tiles.1 = f32[25,64,384]{2,1,0:T(8,128)} custom-call(s32[17]{0:T(128)S(4)} %get-tuple-element.29.res_from, s32[17]{0:T(128)S(4)} %get-tuple-element.30.res_first, f32[16,64,384]{2,1,0:T(8,128)S(1)} %get-tuple-element.31.inverse, f32[2,64,384]{2,1,0:T(8,128)S(1)} %get-tuple-element.44.rest_0_, ...), custom_call_target="tpu_custom_call", output_to_operand_aliasing={{}: (11, {})} | custom-call | bytes 2457600 | tf_op jit(solution)/shard_map/finish_tiles/pallas_call | solution.py:378
  (2 shorter events, 0.0 us)
Async XLA Ops:
  0.0 29.0 %copy-start.4 = (f32[384]{0:T(512)S(1)}, f32[384]{0:T(512)}, u32[]{:S(2)}) copy-start(f32[384]{0:T(512)} %param.19) | copy-start | bytes 4612
  0.0 29.0 %copy-start.3 = (f32[1600]{0:T(1024)S(1)}, f32[1600]{0:T(1024)}, u32[]{:S(2)}) copy-start(f32[1600]{0:T(1024)} %param.20) | copy-start | bytes 19204
  0.0 29.4 %copy-start.2 = (f32[8]{0:T(128)S(1)}, f32[8]{0:T(128)}, u32[]{:S(2)}) copy-start(f32[8]{0:T(128)} %window.1) | copy-start | bytes 100
  0.0 29.4 %copy-start.1 = (s32[200]{0:T(256)S(1)}, s32[200]{0:T(256)}, u32[]{:S(2)}) copy-start(s32[200]{0:T(256)} %res_slot_ref.1) | copy-start | bytes 2404
  0.0 31.8 %copy-start = (s32[2,512]{1,0:T(2,128)S(1)}, s32[2,512]{1,0:T(2,128)}, u32[]{:S(2)}) copy-start(s32[2,512]{1,0:T(2,128)} %tasks_ref.1) | copy-start | bytes 12292
  13.5 12.2 %collective-permute-start = (f32[2,64,384]{2,1,0:T(8,128)S(1)}, f32[2,64,384]{2,1,0:T(8,128)S(1)}, u32[]{:S(2)}, u32[]{:S(2)}) collective-permute-start(f32[2,64,384]{2,1,0:T(8,128)S(1)} %get-tuple-element.37), channel_id=1, source_target_pairs={{0,12},{2,14},{4,8},{6,10},{8,4},{10,6},{12,0},{14,2},{1,13},{3,15... | collective-permute-start | bytes 589832 | tf_op jit(solution)/shard_map/ppermute | solution.py:285
  14.3 12.3 %collective-permute-start.1 = (f32[2,64,384]{2,1,0:T(8,128)S(1)}, f32[2,64,384]{2,1,0:T(8,128)S(1)}, u32[]{:S(2)}, u32[]{:S(2)}) collective-permute-start(f32[2,64,384]{2,1,0:T(8,128)S(1)} %get-tuple-element.38), channel_id=1, source_target_pairs={{0,4},{2,6},{4,0},{6,2},{8,12},{10,14},{12,8},{14,10},{1,5},{3,7},... | collective-permute-start | bytes 589832 | tf_op jit(solution)/shard_map/ppermute | solution.py:285
  15.5 22.9 %collective-permute-start.2 = (f32[2,64,384]{2,1,0:T(8,128)S(1)}, f32[2,64,384]{2,1,0:T(8,128)S(1)}, u32[]{:S(2)}, u32[]{:S(2)}) collective-permute-start(f32[2,64,384]{2,1,0:T(8,128)S(1)} %get-tuple-element.39), channel_id=1, source_target_pairs={{0,8},{2,10},{4,12},{6,14},{8,0},{10,2},{12,4},{14,6},{1,9},{3,11}... | collective-permute-start | bytes 589832 | tf_op jit(solution)/shard_map/ppermute | solution.py:285
  17.6 20.9 %collective-permute-start.3 = (f32[2,64,384]{2,1,0:T(8,128)S(1)}, f32[2,64,384]{2,1,0:T(8,128)S(1)}, u32[]{:S(2)}, u32[]{:S(2)}) collective-permute-start(f32[2,64,384]{2,1,0:T(8,128)S(1)} %get-tuple-element.40), channel_id=1, source_target_pairs={{0,6},{2,4},{4,2},{6,0},{8,14},{10,12},{12,10},{14,8},{1,7},{3,5},... | collective-permute-start | bytes 589832 | tf_op jit(solution)/shard_map/ppermute | solution.py:285
  19.8 23.0 %collective-permute-start.4 = (f32[2,64,384]{2,1,0:T(8,128)S(1)}, f32[2,64,384]{2,1,0:T(8,128)S(1)}, u32[]{:S(2)}, u32[]{:S(2)}) collective-permute-start(f32[2,64,384]{2,1,0:T(8,128)S(1)} %get-tuple-element.41), channel_id=1, source_target_pairs={{0,10},{2,8},{4,14},{6,12},{8,2},{10,0},{12,6},{14,4},{1,11},{3,9}... | collective-permute-start | bytes 589832 | tf_op jit(solution)/shard_map/ppermute | solution.py:285
  25.8 17.0 %collective-permute-start.5 = (f32[2,64,384]{2,1,0:T(8,128)S(1)}, f32[2,64,384]{2,1,0:T(8,128)S(1)}, u32[]{:S(2)}, u32[]{:S(2)}) collective-permute-start(f32[2,64,384]{2,1,0:T(8,128)S(1)} %get-tuple-element.42), channel_id=1, source_target_pairs={{0,2},{2,0},{4,6},{6,4},{8,10},{10,8},{12,14},{14,12},{1,3},{3,1},... | collective-permute-start | bytes 589832 | tf_op jit(solution)/shard_map/ppermute | solution.py:285
  26.5 20.6 %collective-permute-start.6 = (f32[2,64,384]{2,1,0:T(8,128)S(1)}, f32[2,64,384]{2,1,0:T(8,128)S(1)}, u32[]{:S(2)}, u32[]{:S(2)}) collective-permute-start(f32[2,64,384]{2,1,0:T(8,128)S(1)} %get-tuple-element.43), channel_id=1, source_target_pairs={{0,14},{2,12},{4,10},{6,8},{8,6},{10,4},{12,2},{14,0},{1,15},{3,13... | collective-permute-start | bytes 589832 | tf_op jit(solution)/shard_map/ppermute | solution.py:285
  49.5 12.2 %collective-permute-start.7 = (f32[2,64,384]{2,1,0:T(8,128)S(1)}, f32[2,64,384]{2,1,0:T(8,128)S(1)}, u32[]{:S(2)}, u32[]{:S(2)}) collective-permute-start(f32[2,64,384]{2,1,0:T(8,128)S(1)} %get-tuple-element.45), channel_id=1, source_target_pairs={{0,12},{2,14},{4,8},{6,10},{8,4},{10,6},{12,0},{14,2},{1,13},{3,15... | collective-permute-start | bytes 589832 | tf_op jit(solution)/shard_map/ppermute | solution.py:285
  49.9 13.2 %collective-permute-start.8 = (f32[2,64,384]{2,1,0:T(8,128)S(1)}, f32[2,64,384]{2,1,0:T(8,128)S(1)}, u32[]{:S(2)}, u32[]{:S(2)}) collective-permute-start(f32[2,64,384]{2,1,0:T(8,128)S(1)} %get-tuple-element.46), channel_id=1, source_target_pairs={{0,4},{2,6},{4,0},{6,2},{8,12},{10,14},{12,8},{14,10},{1,5},{3,7},... | collective-permute-start | bytes 589832 | tf_op jit(solution)/shard_map/ppermute | solution.py:285
  49.9 23.7 %collective-permute-start.9 = (f32[2,64,384]{2,1,0:T(8,128)S(1)}, f32[2,64,384]{2,1,0:T(8,128)S(1)}, u32[]{:S(2)}, u32[]{:S(2)}) collective-permute-start(f32[2,64,384]{2,1,0:T(8,128)S(1)} %get-tuple-element.47), channel_id=1, source_target_pairs={{0,8},{2,10},{4,12},{6,14},{8,0},{10,2},{12,4},{14,6},{1,9},{3,11}... | collective-permute-start | bytes 589832 | tf_op jit(solution)/shard_map/ppermute | solution.py:285
  53.0 20.5 %collective-permute-start.10 = (f32[2,64,384]{2,1,0:T(8,128)S(1)}, f32[2,64,384]{2,1,0:T(8,128)S(1)}, u32[]{:S(2)}, u32[]{:S(2)}) collective-permute-start(f32[2,64,384]{2,1,0:T(8,128)S(1)} %get-tuple-element.48), channel_id=1, source_target_pairs={{0,6},{2,4},{4,2},{6,0},{8,14},{10,12},{12,10},{14,8},{1,7},{3,5},... | collective-permute-start | bytes 589832 | tf_op jit(solution)/shard_map/ppermute | solution.py:285
  53.9 23.7 %collective-permute-start.11 = (f32[2,64,384]{2,1,0:T(8,128)S(1)}, f32[2,64,384]{2,1,0:T(8,128)S(1)}, u32[]{:S(2)}, u32[]{:S(2)}) collective-permute-start(f32[2,64,384]{2,1,0:T(8,128)S(1)} %get-tuple-element.49), channel_id=1, source_target_pairs={{0,10},{2,8},{4,14},{6,12},{8,2},{10,0},{12,6},{14,4},{1,11},{3,9}... | collective-permute-start | bytes 589832 | tf_op jit(solution)/shard_map/ppermute | solution.py:285
  61.7 16.0 %collective-permute-start.12 = (f32[2,64,384]{2,1,0:T(8,128)S(1)}, f32[2,64,384]{2,1,0:T(8,128)S(1)}, u32[]{:S(2)}, u32[]{:S(2)}) collective-permute-start(f32[2,64,384]{2,1,0:T(8,128)S(1)} %get-tuple-element.50), channel_id=1, source_target_pairs={{0,2},{2,0},{4,6},{6,4},{8,10},{10,8},{12,14},{14,12},{1,3},{3,1},... | collective-permute-start | bytes 589832 | tf_op jit(solution)/shard_map/ppermute | solution.py:285
  63.1 19.8 %collective-permute-start.13 = (f32[2,64,384]{2,1,0:T(8,128)S(1)}, f32[2,64,384]{2,1,0:T(8,128)S(1)}, u32[]{:S(2)}, u32[]{:S(2)}) collective-permute-start(f32[2,64,384]{2,1,0:T(8,128)S(1)} %get-tuple-element.51), channel_id=1, source_target_pairs={{0,14},{2,12},{4,10},{6,8},{8,6},{10,4},{12,2},{14,0},{1,15},{3,13... | collective-permute-start | bytes 589832 | tf_op jit(solution)/shard_map/ppermute | solution.py:285

commit v7 on v6

--- a/solution.py
+++ b/solution.py
@@ -43,34 +43,34 @@
         ref[i] = value
 
 
-def pack_kernel(owners, per_owner, me_ref, lists_ref, amp_slot_ref, amplitudes, *rest):
-    outs, (picked, sems) = rest[: owners - 1], rest[-2:]
-    list_length = lists_ref.shape[0] // owners // 2
+def pack_kernel(classes, list_length, per_owner, me_ref, lists_ref, amp_slot_ref, amplitudes, *rest):
+    outs, (picked, sems) = rest[: len(classes)], rest[-2:]
+    spare = len(classes) * CAP
     me = me_ref[0]
     low = me * per_owner
-    clear(picked, owners * CAP, -1)
-
-    def copy(d, k):
-        local = picked[d * CAP + k]
+    clear(picked, spare, -1)
+
+    def copy(at, k):
+        local = picked[at * CAP + k]
         source = amplitudes.at[jnp.maximum(local, 0)]
-        return local, pltpu.make_async_copy(source, outs[d - 1].at[k], sems.at[d * CAP + k])
-
-    for d in class_order(owners):
+        return local, pltpu.make_async_copy(source, outs[at].at[k], sems.at[at * CAP + k])
+
+    for at, d in enumerate(classes):
         first = jnp.bitwise_xor(me, d) * 2 * list_length
 
         def note(j, count):
             local = amp_slot_ref[lists_ref[first + j]] - low
             mine = (local >= 0) & (local < per_owner)
-            picked[jnp.where(mine, d * CAP + count, owners * CAP)] = local
+            picked[jnp.where(mine, at * CAP + count, spare)] = local
             return count + mine.astype(jnp.int32)
 
         lax.fori_loop(0, list_length, note, jnp.int32(0), unroll=8)
         for k in range(CAP):
-            local, moved = copy(d, k)
+            local, moved = copy(at, k)
             pl.when(local >= 0)(moved.start)
-    for d in class_order(owners):
+    for at in range(len(classes)):
         for k in range(CAP):
-            local, moved = copy(d, k)
+            local, moved = copy(at, k)
             pl.when(local >= 0)(moved.wait)
 
 
@@ -280,27 +280,31 @@
     lists = lax.psum(jnp.where(spots, own_lists[None, :], 0), "tile").reshape(-1)
     me_ref = me.reshape(1)
 
-    def exchange(buffers):
+    order = class_order(owners)
+
+    def exchange(buffers, classes):
         return [
-            in_vmem(lax.ppermute(buffers[d - 1], "tile", [(i, i ^ d) for i in range(owners)]))
-            for d in class_order(owners)
+            in_vmem(lax.ppermute(buffer, "tile", [(i, i ^ d) for i in range(owners)]))
+            for buffer, d in zip(buffers, classes)
         ]
 
     piece = pltpu.VMEM((CAP, TW, row_count), F32)
-    packed = pl.pallas_call(
-        functools.partial(pack_kernel, owners, per_amp),
-        out_shape=[piece] * (owners - 1),
-        in_specs=[SMEM_SPEC] * 3 + [HBM_SPEC],
-        out_specs=[VMEM_SPEC] * (owners - 1),
-        scratch_shapes=[
-            pltpu.SMEM((owners * CAP + 1,), jnp.int32),
-            pltpu.SemaphoreType.DMA((owners * CAP,)),
-        ],
-        compiler_params=params(),
-        cost_estimate=cost(0, 2 * list_length * TW * row_count * 4),
-        name="pack_tiles",
-    )(me_ref, lists, amp_slot, amplitudes)
-    fetched = exchange(packed)
+    fetched = []
+    for classes in order[:1], order[1:]:
+        packed = pl.pallas_call(
+            functools.partial(pack_kernel, classes, list_length, per_amp),
+            out_shape=[piece] * len(classes),
+            in_specs=[SMEM_SPEC] * 3 + [HBM_SPEC],
+            out_specs=[VMEM_SPEC] * len(classes),
+            scratch_shapes=[
+                pltpu.SMEM((len(classes) * CAP + 1,), jnp.int32),
+                pltpu.SemaphoreType.DMA((len(classes) * CAP,)),
+            ],
+            compiler_params=params(),
+            cost_estimate=cost(0, len(classes) * CAP * TW * row_count * 4),
+            name="pack_tiles",
+        )(me_ref, lists, amp_slot, amplitudes)
+        fetched += exchange(packed, classes)
 
     virt = in_vmem(jnp.broadcast_to(virt_energy.reshape(tile_count, TW, 1), (tile_count, TW, 128)))
     pair = in_vmem(pair_energy.reshape(1, row_count))
@@ -374,7 +378,7 @@
         cost_estimate=cost(6 * depth * depth * row_count, 4 * depth * (depth + 2 * row_count)),
         name="multiply_tiles",
     )(amp_from, amp_self, res_to, operator_high, operator_low, amplitudes, *fetched)
-    returned = [in_vmem(products[0])] + exchange(products[1:])
+    returned = [in_vmem(products[0])] + exchange([products[d] for d in order], order)
     return pl.pallas_call(
         functools.partial(final_kernel, owners),
         out_shape=jax.ShapeDtypeStruct((per_res, TW, row_count), F32),

time: 84.9 us -> 84.3 us (level)
  waiting for transfers between devices: 39.5 us -> 36.3 us
  starting transfers between devices: 17.6 us -> 19.9 us
    ppermute x14, waiting for transfers between devices: 39.5 us -> 36.3 us  [exchange(): lax.ppermute(buffer, 'tile', [(i, i ^ d) for i in range(owners)])]
    ppermute x14, starting transfers between devices: 17.6 us -> 19.9 us  [exchange(): lax.ppermute(buffer, 'tile', [(i, i ^ d) for i in range(owners)])]
    pallas_call x1 -> x2, Pallas kernels: 2.06 us -> 2.06 us  [local(): pl.pallas_call(functools.partial(pack_kernel, classes, list_length, per_a...]
  transfers between devices with their start and end apart: 14 -> 14, of which waited for: 8 -> 8; matrix products, arithmetic and copies ran while one was open for 0% -> 0% of each run, Pallas kernels for 11% -> 12%
where the time goes in v7:
time: 84.3 us; the launch traced here: 83.3 us
  waiting for transfers between devices  36.3 us (43%)
  starting transfers between devices  19.9 us (24%)
  Pallas kernels  14.5 us (17%)
  blocking collectives  10.5 us (12%)
    ppermute x14, waiting for transfers between devices, exchange(): lax.ppermute(buffer, 'tile', [(i, i ^ d) for i in range(owners)])  36.3 us
    ppermute x14, starting transfers between devices, exchange(): lax.ppermute(buffer, 'tile', [(i, i ^ d) for i in range(owners)])  19.9 us
    psum x1, blocking collectives, local(): lax.psum(jnp.where(spots, own_lists[None, :], 0), 'tile').reshape(-1)  10.5 us
    pallas_call x1, Pallas kernels, local(): pl.pallas_call(functools.partial(sum_kernel, list_length), grid=(steps,),...  6.5 us
    pallas_call x1, Pallas kernels, local(): pl.pallas_call(functools.partial(maps_kernel, owners, per_amp, per_res),...  2.41 us
    pallas_call x1, Pallas kernels, local(): pl.pallas_call(functools.partial(product_kernel, owners), out_shape=[piec...  2.31 us
    pallas_call x2, Pallas kernels, local(): pl.pallas_call(functools.partial(pack_kernel, classes, list_length, per_a...  2.06 us
  transfers between devices with their start and end apart: 14, of which 8 were waited for; matrix products, arithmetic and copies ran while one was open for 0% of the time, Pallas kernels for 12%

profile of v7, /device:TPU:12, one launch (start us, length us, event | category | flops | bytes accessed | tf_op | source)
XLA Modules:
  0.0 83.3 jit_solution(8594865807532271103)
XLA Ops:
  0.0 0.7 pad_add_fusion
  0.8 0.1 broadcast_select_fusion
  0.8 0.1 reshape.21
  0.9 10.5 %psum.7.lists_ref = s32[128]{0:T(128)S(1)} all-reduce(s32[128]{0:T(128)S(1)} %reshape.21), channel_id=1, replica_groups=mesh['mol'=2,'tile'=8,'rep'=2] {'tile'}, use_global_device_ids=true, to_apply=%region_0.1 | all-reduce | flops 128 | bytes 1024 | tf_op jit(solution)/shard_map/psum | solution.py:280
  11.4 0.0 copy-start.4
  11.4 0.0 copy-start.3
  11.4 0.0 copy-start.1
  11.4 0.0 copy-start.2
  11.4 0.9 %pack_tiles.2 = f32[2,64,384]{2,1,0:T(8,128)S(1)} custom-call(s32[1]{0:T(128)} %bitcast.me_ref, s32[128]{0:T(128)S(1)} %psum.7.lists_ref, s32[200]{0:T(256)} %amp_slot_ref.5, f32[25,64,384]{2,1,0:T(8,128)} %amplitudes.5), custom_call_target="tpu_custom_call" | custom-call | bytes 196608 | tf_op jit(solution)/shard_map/pack_tiles/pallas_call | solution.py:294
  12.3 0.0 copy-start
  12.4 0.5 collective-permute-start
  12.9 1.1 %pack_tiles.3 = (f32[2,64,384]{2,1,0:T(8,128)S(1)}, f32[2,64,384]{2,1,0:T(8,128)S(1)}, f32[2,64,384]{2,1,0:T(8,128)S(1)}, f32[2,64,384]{2,1,0:T(8,128)S(1)}, f32...) custom-call(s32[1]{0:T(128)} %bitcast.me_ref, s32[128]{0:T(128)S(1)} %psum.7.lists_ref, s32[200]{0:T(256)} %amp_slot_ref.5, ...), custom_call_target="tpu_custom_call" | custom-call | bytes 1179648 | tf_op jit(solution)/shard_map/pack_tiles/pallas_call | solution.py:294
  14.0 3.3 %collective-permute-start.1 = (f32[2,64,384]{2,1,0:T(8,128)S(1)}, f32[2,64,384]{2,1,0:T(8,128)S(1)}, u32[]{:S(2)}, u32[]{:S(2)}) collective-permute-start(f32[2,64,384]{2,1,0:T(8,128)S(1)} %get-tuple-element.36), channel_id=1, source_target_pairs={{0,4},{2,6},{4,0},{6,2},{8,12},{10,14},{12,8},{14,10},{1,5},{3,7},... | collective-permute-start | bytes 589832 | tf_op jit(solution)/shard_map/ppermute | solution.py:287
  17.4 2.2 %collective-permute-start.2 = (f32[2,64,384]{2,1,0:T(8,128)S(1)}, f32[2,64,384]{2,1,0:T(8,128)S(1)}, u32[]{:S(2)}, u32[]{:S(2)}) collective-permute-start(f32[2,64,384]{2,1,0:T(8,128)S(1)} %get-tuple-element.37), channel_id=1, source_target_pairs={{0,8},{2,10},{4,12},{6,14},{8,0},{10,2},{12,4},{14,6},{1,9},{3,11}... | collective-permute-start | bytes 589832 | tf_op jit(solution)/shard_map/ppermute | solution.py:287
  19.6 0.9 %collective-permute-start.3 = (f32[2,64,384]{2,1,0:T(8,128)S(1)}, f32[2,64,384]{2,1,0:T(8,128)S(1)}, u32[]{:S(2)}, u32[]{:S(2)}) collective-permute-start(f32[2,64,384]{2,1,0:T(8,128)S(1)} %get-tuple-element.38), channel_id=1, source_target_pairs={{0,6},{2,4},{4,2},{6,0},{8,14},{10,12},{12,10},{14,8},{1,7},{3,5},... | collective-permute-start | bytes 589832 | tf_op jit(solution)/shard_map/ppermute | solution.py:287
  20.5 1.9 %collective-permute-start.4 = (f32[2,64,384]{2,1,0:T(8,128)S(1)}, f32[2,64,384]{2,1,0:T(8,128)S(1)}, u32[]{:S(2)}, u32[]{:S(2)}) collective-permute-start(f32[2,64,384]{2,1,0:T(8,128)S(1)} %get-tuple-element.39), channel_id=1, source_target_pairs={{0,10},{2,8},{4,14},{6,12},{8,2},{10,0},{12,6},{14,4},{1,11},{3,9}... | collective-permute-start | bytes 589832 | tf_op jit(solution)/shard_map/ppermute | solution.py:287
  22.5 2.4 %collective-permute-done.rest_0_ = f32[2,64,384]{2,1,0:T(8,128)S(1)} collective-permute-done((f32[2,64,384]{2,1,0:T(8,128)S(1)}, f32[2,64,384]{2,1,0:T(8,128)S(1)}, u32[]{:S(2)}, u32[]{:S(2)}) %collective-permute-start) | collective-permute-done | bytes 196640 | tf_op jit(solution)/shard_map/ppermute | solution.py:287
  24.9 0.2 collective-permute-start.5
  25.1 3.1 %collective-permute-done.1.rest_1_ = f32[2,64,384]{2,1,0:T(8,128)S(1)} collective-permute-done((f32[2,64,384]{2,1,0:T(8,128)S(1)}, f32[2,64,384]{2,1,0:T(8,128)S(1)}, u32[]{:S(2)}, u32[]{:S(2)}) %collective-permute-start.1) | collective-permute-done | bytes 196640 | tf_op jit(solution)/shard_map/ppermute | solution.py:287
  28.2 0.1 collective-permute-start.6
  28.9 0.0 copy-done.4
  28.9 0.0 copy-done.3
  28.9 0.1 broadcast_in_dim.32
  29.0 0.3 broadcast_in_dim.33.virt
  29.3 0.0 copy-done.1
  29.3 0.0 copy-done.2
  29.3 2.4 %list_maps.1 = (s32[17]{0:T(128)S(4)}, s32[3]{0:T(128)S(4)}, s32[17]{0:T(128)S(4)}, s32[17]{0:T(128)S(4)}, s32[17]{0:T(128)S(4)}, /*index=5*/f32[16,64,384]{2,1,0:T(8,128)S(1)}) custom-call(s32[1]{0:T(128)} %bitcast.me_ref, s32[128]{0:T(128)S(1)} %psum.7.lists_ref, s32[200]{0:T(256)} %amp_slot_ref.5, s32[200]{0:T(256)S(1)} %copy-done.1, f32[8]{0:T(128)S(1)} %copy-done.2, ...), custom_call_target="tpu_custom_call" | custom-call | bytes 1572864 | tf_op jit(solution)/shard_map/list_maps/pallas_call | solution.py:312
  31.7 0.0 copy-done
  31.7 6.5 %sum_integrals.1 = (bf16[512,512]{1,0:T(8,128)(2,1)S(1)}, bf16[512,512]{1,0:T(8,128)(2,1)S(1)}, f32[1600,384]{1,0:T(8,128)}) custom-call(s32[1]{0:T(128)S(6)} %copy.14.count_ref, s32[2,512]{1,0:T(2,128)S(1)} %copy-done, f32[512,4096]{1,0:T(8,128)} %integrals_ref.1), custom_call_target="tpu_custom_call" | custom-call | flops 536870912 | bytes 9437184 | tf_op jit(solution)/shard_map/sum_integrals/pallas_call | solution.py:338
  38.2 0.0 collective-permute-done.2.rest_2_
  38.2 0.0 collective-permute-done.3.rest_3_
  38.2 2.1 %collective-permute-done.4.rest_4_ = f32[2,64,384]{2,1,0:T(8,128)S(1)} collective-permute-done((f32[2,64,384]{2,1,0:T(8,128)S(1)}, f32[2,64,384]{2,1,0:T(8,128)S(1)}, u32[]{:S(2)}, u32[]{:S(2)}) %collective-permute-start.4) | collective-permute-done | bytes 196640 | tf_op jit(solution)/shard_map/ppermute | solution.py:287
  40.3 0.0 collective-permute-done.5.rest_5_
  40.3 5.5 %collective-permute-done.6.rest_6_ = f32[2,64,384]{2,1,0:T(8,128)S(1)} collective-permute-done((f32[2,64,384]{2,1,0:T(8,128)S(1)}, f32[2,64,384]{2,1,0:T(8,128)S(1)}, u32[]{:S(2)}, u32[]{:S(2)}) %collective-permute-start.6) | collective-permute-done | bytes 196640 | tf_op jit(solution)/shard_map/ppermute | solution.py:287
  45.9 2.3 %multiply_tiles.1 = (f32[2,64,384]{2,1,0:T(8,128)S(1)}, f32[2,64,384]{2,1,0:T(8,128)S(1)}, f32[2,64,384]{2,1,0:T(8,128)S(1)}, f32[2,64,384]{2,1,0:T(8,128)S(1)},...) custom-call(s32[17]{0:T(128)S(4)} %get-tuple-element.31.amp_from, ...), custom_call_target="tpu_custom_call" | custom-call | flops 603979776 | bytes 2621440 | tf_op jit(solution)/shard_map/multiply_tiles/pallas_call | solution.py:365
  48.2 2.3 %collective-permute-start.7 = (f32[2,64,384]{2,1,0:T(8,128)S(1)}, f32[2,64,384]{2,1,0:T(8,128)S(1)}, u32[]{:S(2)}, u32[]{:S(2)}) collective-permute-start(f32[2,64,384]{2,1,0:T(8,128)S(1)} %get-tuple-element.43), channel_id=1, source_target_pairs={{0,12},{2,14},{4,8},{6,10},{8,4},{10,6},{12,0},{14,2},{1,13},{3,15... | collective-permute-start | bytes 589832 | tf_op jit(solution)/shard_map/ppermute | solution.py:287
  50.5 0.0 collective-permute-start.8
  50.5 1.5 %collective-permute-start.9 = (f32[2,64,384]{2,1,0:T(8,128)S(1)}, f32[2,64,384]{2,1,0:T(8,128)S(1)}, u32[]{:S(2)}, u32[]{:S(2)}) collective-permute-start(f32[2,64,384]{2,1,0:T(8,128)S(1)} %get-tuple-element.45), channel_id=1, source_target_pairs={{0,8},{2,10},{4,12},{6,14},{8,0},{10,2},{12,4},{14,6},{1,9},{3,11}... | collective-permute-start | bytes 589832 | tf_op jit(solution)/shard_map/ppermute | solution.py:287
  52.0 2.5 %collective-permute-start.10 = (f32[2,64,384]{2,1,0:T(8,128)S(1)}, f32[2,64,384]{2,1,0:T(8,128)S(1)}, u32[]{:S(2)}, u32[]{:S(2)}) collective-permute-start(f32[2,64,384]{2,1,0:T(8,128)S(1)} %get-tuple-element.46), channel_id=1, source_target_pairs={{0,6},{2,4},{4,2},{6,0},{8,14},{10,12},{12,10},{14,8},{1,7},{3,5},... | collective-permute-start | bytes 589832 | tf_op jit(solution)/shard_map/ppermute | solution.py:287
  54.5 1.8 %collective-permute-start.11 = (f32[2,64,384]{2,1,0:T(8,128)S(1)}, f32[2,64,384]{2,1,0:T(8,128)S(1)}, u32[]{:S(2)}, u32[]{:S(2)}) collective-permute-start(f32[2,64,384]{2,1,0:T(8,128)S(1)} %get-tuple-element.47), channel_id=1, source_target_pairs={{0,10},{2,8},{4,14},{6,12},{8,2},{10,0},{12,6},{14,4},{1,11},{3,9}... | collective-permute-start | bytes 589832 | tf_op jit(solution)/shard_map/ppermute | solution.py:287
  56.3 4.2 %collective-permute-done.7.rest_1_ = f32[2,64,384]{2,1,0:T(8,128)S(1)} collective-permute-done((f32[2,64,384]{2,1,0:T(8,128)S(1)}, f32[2,64,384]{2,1,0:T(8,128)S(1)}, u32[]{:S(2)}, u32[]{:S(2)}) %collective-permute-start.7) | collective-permute-done | bytes 196640 | tf_op jit(solution)/shard_map/ppermute | solution.py:287
  60.6 2.6 %collective-permute-start.12 = (f32[2,64,384]{2,1,0:T(8,128)S(1)}, f32[2,64,384]{2,1,0:T(8,128)S(1)}, u32[]{:S(2)}, u32[]{:S(2)}) collective-permute-start(f32[2,64,384]{2,1,0:T(8,128)S(1)} %get-tuple-element.48), channel_id=1, source_target_pairs={{0,2},{2,0},{4,6},{6,4},{8,10},{10,8},{12,14},{14,12},{1,3},{3,1},... | collective-permute-start | bytes 589832 | tf_op jit(solution)/shard_map/ppermute | solution.py:287
  63.1 0.0 collective-permute-done.8.rest_2_
  63.1 0.0 collective-permute-start.13
  63.1 9.6 %collective-permute-done.9.rest_3_ = f32[2,64,384]{2,1,0:T(8,128)S(1)} collective-permute-done((f32[2,64,384]{2,1,0:T(8,128)S(1)}, f32[2,64,384]{2,1,0:T(8,128)S(1)}, u32[]{:S(2)}, u32[]{:S(2)}) %collective-permute-start.9) | collective-permute-done | bytes 196640 | tf_op jit(solution)/shard_map/ppermute | solution.py:287
  72.7 0.0 collective-permute-done.10.rest_4_
  72.7 4.2 %collective-permute-done.11.rest_5_ = f32[2,64,384]{2,1,0:T(8,128)S(1)} collective-permute-done((f32[2,64,384]{2,1,0:T(8,128)S(1)}, f32[2,64,384]{2,1,0:T(8,128)S(1)}, u32[]{:S(2)}, u32[]{:S(2)}) %collective-permute-start.11) | collective-permute-done | bytes 196640 | tf_op jit(solution)/shard_map/ppermute | solution.py:287
  76.9 0.0 collective-permute-done.12.rest_6_
  76.9 5.1 %collective-permute-done.13.rest_7_ = f32[2,64,384]{2,1,0:T(8,128)S(1)} collective-permute-done((f32[2,64,384]{2,1,0:T(8,128)S(1)}, f32[2,64,384]{2,1,0:T(8,128)S(1)}, u32[]{:S(2)}, u32[]{:S(2)}) %collective-permute-start.13) | collective-permute-done | bytes 196640 | tf_op jit(solution)/shard_map/ppermute | solution.py:287
  82.1 1.2 %finish_tiles.1 = f32[25,64,384]{2,1,0:T(8,128)} custom-call(s32[17]{0:T(128)S(4)} %get-tuple-element.28.res_from, s32[17]{0:T(128)S(4)} %get-tuple-element.29.res_first, f32[16,64,384]{2,1,0:T(8,128)S(1)} %get-tuple-element.30.inverse, f32[2,64,384]{2,1,0:T(8,128)S(1)} %get-tuple-element.42.rest_0_, ...), custom_call_target="tpu_custom_call", output_to_operand_aliasing={{}: (11, {})} | custom-call | bytes 2457600 | tf_op jit(solution)/shard_map/finish_tiles/pallas_call | solution.py:382
  (2 shorter events, 0.0 us)
Async XLA Ops:
  11.4 17.5 %copy-start.4 = (f32[384]{0:T(512)S(1)}, f32[384]{0:T(512)}, u32[]{:S(2)}) copy-start(f32[384]{0:T(512)} %param.19) | copy-start | bytes 4612
  11.4 17.5 %copy-start.3 = (f32[1600]{0:T(1024)S(1)}, f32[1600]{0:T(1024)}, u32[]{:S(2)}) copy-start(f32[1600]{0:T(1024)} %param.20) | copy-start | bytes 19204
  11.4 17.9 %copy-start.1 = (s32[200]{0:T(256)S(1)}, s32[200]{0:T(256)}, u32[]{:S(2)}) copy-start(s32[200]{0:T(256)} %res_slot_ref.1) | copy-start | bytes 2404
  11.4 17.9 %copy-start.2 = (f32[8]{0:T(128)S(1)}, f32[8]{0:T(128)}, u32[]{:S(2)}) copy-start(f32[8]{0:T(128)} %window.1) | copy-start | bytes 100
  12.3 19.4 %copy-start = (s32[2,512]{1,0:T(2,128)S(1)}, s32[2,512]{1,0:T(2,128)}, u32[]{:S(2)}) copy-start(s32[2,512]{1,0:T(2,128)} %tasks_ref.1) | copy-start | bytes 12292
  12.4 12.5 %collective-permute-start = (f32[2,64,384]{2,1,0:T(8,128)S(1)}, f32[2,64,384]{2,1,0:T(8,128)S(1)}, u32[]{:S(2)}, u32[]{:S(2)}) collective-permute-start(f32[2,64,384]{2,1,0:T(8,128)S(1)} %pack_tiles.2), channel_id=1, source_target_pairs={{0,12},{2,14},{4,8},{6,10},{8,4},{10,6},{12,0},{14,2},{1,13},{3,15... | collective-permute-start | bytes 589832 | tf_op jit(solution)/shard_map/ppermute | solution.py:287
  14.0 14.1 %collective-permute-start.1 = (f32[2,64,384]{2,1,0:T(8,128)S(1)}, f32[2,64,384]{2,1,0:T(8,128)S(1)}, u32[]{:S(2)}, u32[]{:S(2)}) collective-permute-start(f32[2,64,384]{2,1,0:T(8,128)S(1)} %get-tuple-element.36), channel_id=1, source_target_pairs={{0,4},{2,6},{4,0},{6,2},{8,12},{10,14},{12,8},{14,10},{1,5},{3,7},... | collective-permute-start | bytes 589832 | tf_op jit(solution)/shard_map/ppermute | solution.py:287
  17.4 20.9 %collective-permute-start.2 = (f32[2,64,384]{2,1,0:T(8,128)S(1)}, f32[2,64,384]{2,1,0:T(8,128)S(1)}, u32[]{:S(2)}, u32[]{:S(2)}) collective-permute-start(f32[2,64,384]{2,1,0:T(8,128)S(1)} %get-tuple-element.37), channel_id=1, source_target_pairs={{0,8},{2,10},{4,12},{6,14},{8,0},{10,2},{12,4},{14,6},{1,9},{3,11}... | collective-permute-start | bytes 589832 | tf_op jit(solution)/shard_map/ppermute | solution.py:287
  19.6 18.6 %collective-permute-start.3 = (f32[2,64,384]{2,1,0:T(8,128)S(1)}, f32[2,64,384]{2,1,0:T(8,128)S(1)}, u32[]{:S(2)}, u32[]{:S(2)}) collective-permute-start(f32[2,64,384]{2,1,0:T(8,128)S(1)} %get-tuple-element.38), channel_id=1, source_target_pairs={{0,6},{2,4},{4,2},{6,0},{8,14},{10,12},{12,10},{14,8},{1,7},{3,5},... | collective-permute-start | bytes 589832 | tf_op jit(solution)/shard_map/ppermute | solution.py:287
  20.5 19.8 %collective-permute-start.4 = (f32[2,64,384]{2,1,0:T(8,128)S(1)}, f32[2,64,384]{2,1,0:T(8,128)S(1)}, u32[]{:S(2)}, u32[]{:S(2)}) collective-permute-start(f32[2,64,384]{2,1,0:T(8,128)S(1)} %get-tuple-element.39), channel_id=1, source_target_pairs={{0,10},{2,8},{4,14},{6,12},{8,2},{10,0},{12,6},{14,4},{1,11},{3,9}... | collective-permute-start | bytes 589832 | tf_op jit(solution)/shard_map/ppermute | solution.py:287
  24.9 15.4 %collective-permute-start.5 = (f32[2,64,384]{2,1,0:T(8,128)S(1)}, f32[2,64,384]{2,1,0:T(8,128)S(1)}, u32[]{:S(2)}, u32[]{:S(2)}) collective-permute-start(f32[2,64,384]{2,1,0:T(8,128)S(1)} %get-tuple-element.40), channel_id=1, source_target_pairs={{0,2},{2,0},{4,6},{6,4},{8,10},{10,8},{12,14},{14,12},{1,3},{3,1},... | collective-permute-start | bytes 589832 | tf_op jit(solution)/shard_map/ppermute | solution.py:287
  28.2 17.7 %collective-permute-start.6 = (f32[2,64,384]{2,1,0:T(8,128)S(1)}, f32[2,64,384]{2,1,0:T(8,128)S(1)}, u32[]{:S(2)}, u32[]{:S(2)}) collective-permute-start(f32[2,64,384]{2,1,0:T(8,128)S(1)} %get-tuple-element.41), channel_id=1, source_target_pairs={{0,14},{2,12},{4,10},{6,8},{8,6},{10,4},{12,2},{14,0},{1,15},{3,13... | collective-permute-start | bytes 589832 | tf_op jit(solution)/shard_map/ppermute | solution.py:287
  48.2 12.4 %collective-permute-start.7 = (f32[2,64,384]{2,1,0:T(8,128)S(1)}, f32[2,64,384]{2,1,0:T(8,128)S(1)}, u32[]{:S(2)}, u32[]{:S(2)}) collective-permute-start(f32[2,64,384]{2,1,0:T(8,128)S(1)} %get-tuple-element.43), channel_id=1, source_target_pairs={{0,12},{2,14},{4,8},{6,10},{8,4},{10,6},{12,0},{14,2},{1,13},{3,15... | collective-permute-start | bytes 589832 | tf_op jit(solution)/shard_map/ppermute | solution.py:287
  50.5 12.7 %collective-permute-start.8 = (f32[2,64,384]{2,1,0:T(8,128)S(1)}, f32[2,64,384]{2,1,0:T(8,128)S(1)}, u32[]{:S(2)}, u32[]{:S(2)}) collective-permute-start(f32[2,64,384]{2,1,0:T(8,128)S(1)} %get-tuple-element.44), channel_id=1, source_target_pairs={{0,4},{2,6},{4,0},{6,2},{8,12},{10,14},{12,8},{14,10},{1,5},{3,7},... | collective-permute-start | bytes 589832 | tf_op jit(solution)/shard_map/ppermute | solution.py:287
  50.5 22.2 %collective-permute-start.9 = (f32[2,64,384]{2,1,0:T(8,128)S(1)}, f32[2,64,384]{2,1,0:T(8,128)S(1)}, u32[]{:S(2)}, u32[]{:S(2)}) collective-permute-start(f32[2,64,384]{2,1,0:T(8,128)S(1)} %get-tuple-element.45), channel_id=1, source_target_pairs={{0,8},{2,10},{4,12},{6,14},{8,0},{10,2},{12,4},{14,6},{1,9},{3,11}... | collective-permute-start | bytes 589832 | tf_op jit(solution)/shard_map/ppermute | solution.py:287
  52.0 20.7 %collective-permute-start.10 = (f32[2,64,384]{2,1,0:T(8,128)S(1)}, f32[2,64,384]{2,1,0:T(8,128)S(1)}, u32[]{:S(2)}, u32[]{:S(2)}) collective-permute-start(f32[2,64,384]{2,1,0:T(8,128)S(1)} %get-tuple-element.46), channel_id=1, source_target_pairs={{0,6},{2,4},{4,2},{6,0},{8,14},{10,12},{12,10},{14,8},{1,7},{3,5},... | collective-permute-start | bytes 589832 | tf_op jit(solution)/shard_map/ppermute | solution.py:287
  54.5 22.4 %collective-permute-start.11 = (f32[2,64,384]{2,1,0:T(8,128)S(1)}, f32[2,64,384]{2,1,0:T(8,128)S(1)}, u32[]{:S(2)}, u32[]{:S(2)}) collective-permute-start(f32[2,64,384]{2,1,0:T(8,128)S(1)} %get-tuple-element.47), channel_id=1, source_target_pairs={{0,10},{2,8},{4,14},{6,12},{8,2},{10,0},{12,6},{14,4},{1,11},{3,9}... | collective-permute-start | bytes 589832 | tf_op jit(solution)/shard_map/ppermute | solution.py:287
  60.6 16.4 %collective-permute-start.12 = (f32[2,64,384]{2,1,0:T(8,128)S(1)}, f32[2,64,384]{2,1,0:T(8,128)S(1)}, u32[]{:S(2)}, u32[]{:S(2)}) collective-permute-start(f32[2,64,384]{2,1,0:T(8,128)S(1)} %get-tuple-element.48), channel_id=1, source_target_pairs={{0,2},{2,0},{4,6},{6,4},{8,10},{10,8},{12,14},{14,12},{1,3},{3,1},... | collective-permute-start | bytes 589832 | tf_op jit(solution)/shard_map/ppermute | solution.py:287
  63.1 19.0 %collective-permute-start.13 = (f32[2,64,384]{2,1,0:T(8,128)S(1)}, f32[2,64,384]{2,1,0:T(8,128)S(1)}, u32[]{:S(2)}, u32[]{:S(2)}) collective-permute-start(f32[2,64,384]{2,1,0:T(8,128)S(1)} %get-tuple-element.49), channel_id=1, source_target_pairs={{0,14},{2,12},{4,10},{6,8},{8,6},{10,4},{12,2},{14,0},{1,15},{3,13... | collective-permute-start | bytes 589832 | tf_op jit(solution)/shard_map/ppermute | solution.py:287

commit v8 on v7

--- a/solution.py
+++ b/solution.py
@@ -43,7 +43,18 @@
         ref[i] = value
 
 
-def pack_kernel(classes, list_length, per_owner, me_ref, lists_ref, amp_slot_ref, amplitudes, *rest):
+def spread_kernel(list_length, me_ref, need_ref, needed_ref, amp_slot_ref, spread):
+    shape = spread.shape
+    at = lax.broadcasted_iota(jnp.int32, shape, 0) * shape[1] + lax.broadcasted_iota(jnp.int32, shape, 1)
+    at = at - me_ref[0] * 2 * list_length
+    values = jnp.zeros(shape, jnp.int32)
+    for j in range(list_length):
+        values = jnp.where(at == j, amp_slot_ref[need_ref[j]], values)
+        values = jnp.where(at == list_length + j, needed_ref[j], values)
+    spread[...] = values
+
+
+def pack_kernel(classes, list_length, per_owner, me_ref, lists_ref, amplitudes, *rest):
     outs, (picked, sems) = rest[: len(classes)], rest[-2:]
     spare = len(classes) * CAP
     me = me_ref[0]
@@ -59,7 +70,7 @@
         first = jnp.bitwise_xor(me, d) * 2 * list_length
 
         def note(j, count):
-            local = amp_slot_ref[lists_ref[first + j]] - low
+            local = lists_ref[first + j] - low
             mine = (local >= 0) & (local < per_owner)
             picked[jnp.where(mine, at * CAP + count, spare)] = local
             return count + mine.astype(jnp.int32)
@@ -75,7 +86,7 @@
 
 
 def maps_kernel(
-    owners, per_amp, per_res, me_ref, lists_ref, amp_slot_ref, res_slot_ref,
+    owners, per_amp, per_res, me_ref, lists_ref, res_slot_ref,
     window, pair, virt, amp_from, amp_self, res_to, res_from, res_first, inverse, res_tile, seen, taken,
 ):
     list_length = lists_ref.shape[0] // owners // 2
@@ -91,7 +102,9 @@
         clear(seen, owners, 0)
 
         def note(g, carry):
-            slot = slot_map[lists_ref[me * 2 * list_length + offset + g]]
+            slot = lists_ref[me * 2 * list_length + offset + g]
+            if slot_map is not None:
+                slot = slot_map[slot]
             owner = lax.div(slot, jnp.int32(per_owner))
             d = jnp.bitwise_xor(owner, me)
             count = seen[d]
@@ -103,7 +116,7 @@
 
         lax.fori_loop(0, list_length, note, 0, unroll=8)
 
-    own_list(0, amp_slot_ref, per_amp, amp_from, amp_self)
+    own_list(0, None, per_amp, amp_from, amp_self)
     own_list(list_length, res_slot_ref, per_res, res_to, None)
     low = me * per_res
 
@@ -274,12 +287,18 @@
 
     amplitudes = pltpu.with_memory_space_constraint(amplitudes, pltpu.HBM)
     integrals = pltpu.with_memory_space_constraint(integrals, pltpu.HBM)
-    amp_slot = pltpu.with_memory_space_constraint(amp_slot, pltpu.HBM)
-    own_lists = jnp.concatenate([need_amp, needed_residual_tiles])
-    spots = jnp.arange(owners, dtype=jnp.int32)[:, None] == me
-    lists = lax.psum(jnp.where(spots, own_lists[None, :], 0), "tile").reshape(-1)
     me_ref = me.reshape(1)
-
+    in_hbm = functools.partial(pltpu.with_memory_space_constraint, memory_space=pltpu.HBM)
+    spread = pl.pallas_call(
+        functools.partial(spread_kernel, list_length),
+        out_shape=pltpu.VMEM((owners * 2 * list_length // 128, 128), jnp.int32),
+        in_specs=[SMEM_SPEC] * 4,
+        out_specs=VMEM_SPEC,
+        compiler_params=params(),
+        cost_estimate=cost(0, owners * 2 * list_length * 4),
+        name="spread_lists",
+    )(me_ref, in_hbm(need_amp), in_hbm(needed_residual_tiles), in_hbm(amp_slot))
+    lists = lax.psum(spread, "tile").reshape(-1)
     order = class_order(owners)
 
     def exchange(buffers, classes):
@@ -294,7 +313,7 @@
         packed = pl.pallas_call(
             functools.partial(pack_kernel, classes, list_length, per_amp),
             out_shape=[piece] * len(classes),
-            in_specs=[SMEM_SPEC] * 3 + [HBM_SPEC],
+            in_specs=[SMEM_SPEC] * 2 + [HBM_SPEC],
             out_specs=[VMEM_SPEC] * len(classes),
             scratch_shapes=[
                 pltpu.SMEM((len(classes) * CAP + 1,), jnp.int32),
@@ -303,7 +322,7 @@
             compiler_params=params(),
             cost_estimate=cost(0, len(classes) * CAP * TW * row_count * 4),
             name="pack_tiles",
-        )(me_ref, lists, amp_slot, amplitudes)
+        )(me_ref, lists, amplitudes)
         fetched += exchange(packed, classes)
 
     virt = in_vmem(jnp.broadcast_to(virt_energy.reshape(tile_count, TW, 1), (tile_count, TW, 128)))
@@ -313,7 +332,7 @@
         functools.partial(maps_kernel, owners, per_amp, per_res),
         out_shape=[small, pltpu.SMEM((CAP + 1,), jnp.int32), small, small, small]
         + [pltpu.VMEM((owners * CAP, TW, row_count), F32)],
-        in_specs=[SMEM_SPEC] * 5 + [VMEM_SPEC] * 2,
+        in_specs=[SMEM_SPEC] * 4 + [VMEM_SPEC] * 2,
         out_specs=[SMEM_SPEC] * 5 + [VMEM_SPEC],
         scratch_shapes=[
             pltpu.SMEM((owners * CAP + 1,), jnp.int32),
@@ -323,7 +342,7 @@
         compiler_params=params(),
         cost_estimate=cost(0, owners * CAP * TW * row_count * 4),
         name="list_maps",
-    )(me_ref, lists, amp_slot, res_slot, window_energy, pair, virt)
+    )(me_ref, lists, res_slot, window_energy, pair, virt)
     amp_from, amp_self, res_to, res_from, res_first = (
         pltpu.with_memory_space_constraint(x, pltpu.SMEM) for x in maps
     )

time: 84.3 us -> 83.4 us (0.989)
  starting transfers between devices: 19.9 us -> 17.9 us
  Pallas kernels: 14.5 us -> 15.5 us
    ppermute x14, starting transfers between devices: 19.9 us -> 17.9 us  [exchange(): lax.ppermute(buffer, 'tile', [(i, i ^ d) for i in range(owners)])]
  transfers between devices with their start and end apart: 14 -> 14, of which waited for: 8 -> 8; matrix products, arithmetic and copies ran while one was open for 0% -> 0% of each run, Pallas kernels for 12% -> 13%
where the time goes in v8:
time: 83.4 us; the launch traced here: 81.9 us
  waiting for transfers between devices  36.8 us (44%)
  starting transfers between devices  17.9 us (21%)
  Pallas kernels  15.5 us (19%)
  blocking collectives  10.5 us (13%)
    ppermute x14, waiting for transfers between devices, exchange(): lax.ppermute(buffer, 'tile', [(i, i ^ d) for i in range(owners)])  36.8 us
    ppermute x14, starting transfers between devices, exchange(): lax.ppermute(buffer, 'tile', [(i, i ^ d) for i in range(owners)])  17.9 us
    psum x1, blocking collectives, local(): lists = lax.psum(spread, 'tile').reshape(-1)  10.5 us
    pallas_call x1, Pallas kernels, local(): pl.pallas_call(functools.partial(sum_kernel, list_length), grid=(steps,),...  6.49 us
    pallas_call x2, Pallas kernels, local(): pl.pallas_call(functools.partial(pack_kernel, classes, list_length, per_a...  2.51 us
    pallas_call x1, Pallas kernels, local(): pl.pallas_call(functools.partial(product_kernel, owners), out_shape=[piec...  2.3 us
    pallas_call x1, Pallas kernels, local(): pl.pallas_call(functools.partial(maps_kernel, owners, per_amp, per_res),...  2.25 us
  transfers between devices with their start and end apart: 14, of which 8 were waited for; matrix products, arithmetic and copies ran while one was open for 0% of the time, Pallas kernels for 13%

profile of v8, /device:TPU:12, one launch (start us, length us, event | category | flops | bytes accessed | tf_op | source)
XLA Modules:
  0.0 81.9 jit_solution(4088862027886049684)
XLA Ops:
  0.0 0.7 spread_lists.1
  0.7 10.5 %psum.7.lists_ref = s32[128]{0:T(128)S(1)} all-reduce(s32[128]{0:T(128)S(1)} %bitcast.3), channel_id=1, replica_groups=mesh['mol'=2,'tile'=8,'rep'=2] {'tile'}, use_global_device_ids=true, to_apply=%region_0.0 | all-reduce | flops 128 | bytes 1024 | tf_op jit(solution)/shard_map/psum | solution.py:301
  11.2 0.0 copy-start.4
  11.2 0.0 copy-start.3
  11.2 0.0 copy-start.1
  11.2 0.0 copy-start.2
  11.3 0.6 pack_tiles.2
  11.9 0.0 copy-start
  11.9 0.5 collective-permute-start
  12.4 1.9 %pack_tiles.3 = (f32[2,64,384]{2,1,0:T(8,128)S(1)}, f32[2,64,384]{2,1,0:T(8,128)S(1)}, f32[2,64,384]{2,1,0:T(8,128)S(1)}, f32[2,64,384]{2,1,0:T(8,128)S(1)}, f32...) custom-call(s32[1]{0:T(128)} %bitcast.me_ref, s32[128]{0:T(128)S(1)} %psum.7.lists_ref, f32[25,64,384]{2,1,0:T(8,128)} %amplitudes.5), custom_call_target="tpu_custom_call" | custom-call | bytes 1179648 | tf_op jit(solution)/shard_map/pack_tiles/pallas_call | solution.py:313
  14.3 1.4 %collective-permute-start.1 = (f32[2,64,384]{2,1,0:T(8,128)S(1)}, f32[2,64,384]{2,1,0:T(8,128)S(1)}, u32[]{:S(2)}, u32[]{:S(2)}) collective-permute-start(f32[2,64,384]{2,1,0:T(8,128)S(1)} %get-tuple-element.36), channel_id=1, source_target_pairs={{0,4},{2,6},{4,0},{6,2},{8,12},{10,14},{12,8},{14,10},{1,5},{3,7},... | collective-permute-start | bytes 589832 | tf_op jit(solution)/shard_map/ppermute | solution.py:306
  15.7 2.1 %collective-permute-start.2 = (f32[2,64,384]{2,1,0:T(8,128)S(1)}, f32[2,64,384]{2,1,0:T(8,128)S(1)}, u32[]{:S(2)}, u32[]{:S(2)}) collective-permute-start(f32[2,64,384]{2,1,0:T(8,128)S(1)} %get-tuple-element.37), channel_id=1, source_target_pairs={{0,8},{2,10},{4,12},{6,14},{8,0},{10,2},{12,4},{14,6},{1,9},{3,11}... | collective-permute-start | bytes 589832 | tf_op jit(solution)/shard_map/ppermute | solution.py:306
  17.9 2.1 %collective-permute-start.3 = (f32[2,64,384]{2,1,0:T(8,128)S(1)}, f32[2,64,384]{2,1,0:T(8,128)S(1)}, u32[]{:S(2)}, u32[]{:S(2)}) collective-permute-start(f32[2,64,384]{2,1,0:T(8,128)S(1)} %get-tuple-element.38), channel_id=1, source_target_pairs={{0,6},{2,4},{4,2},{6,0},{8,14},{10,12},{12,10},{14,8},{1,7},{3,5},... | collective-permute-start | bytes 589832 | tf_op jit(solution)/shard_map/ppermute | solution.py:306
  20.0 0.8 collective-permute-start.4
  20.7 3.4 %collective-permute-done.rest_0_ = f32[2,64,384]{2,1,0:T(8,128)S(1)} collective-permute-done((f32[2,64,384]{2,1,0:T(8,128)S(1)}, f32[2,64,384]{2,1,0:T(8,128)S(1)}, u32[]{:S(2)}, u32[]{:S(2)}) %collective-permute-start) | collective-permute-done | bytes 196640 | tf_op jit(solution)/shard_map/ppermute | solution.py:306
  24.1 0.5 collective-permute-start.5
  24.6 1.7 %collective-permute-done.1.rest_1_ = f32[2,64,384]{2,1,0:T(8,128)S(1)} collective-permute-done((f32[2,64,384]{2,1,0:T(8,128)S(1)}, f32[2,64,384]{2,1,0:T(8,128)S(1)}, u32[]{:S(2)}, u32[]{:S(2)}) %collective-permute-start.1) | collective-permute-done | bytes 196640 | tf_op jit(solution)/shard_map/ppermute | solution.py:306
  26.3 0.9 %collective-permute-start.6 = (f32[2,64,384]{2,1,0:T(8,128)S(1)}, f32[2,64,384]{2,1,0:T(8,128)S(1)}, u32[]{:S(2)}, u32[]{:S(2)}) collective-permute-start(f32[2,64,384]{2,1,0:T(8,128)S(1)} %get-tuple-element.41), channel_id=1, source_target_pairs={{0,14},{2,12},{4,10},{6,8},{8,6},{10,4},{12,2},{14,0},{1,15},{3,13... | collective-permute-start | bytes 589832 | tf_op jit(solution)/shard_map/ppermute | solution.py:306
  27.9 0.0 copy-done.4
  27.9 0.0 copy-done.3
  27.9 0.1 broadcast_in_dim.7
  28.0 0.3 broadcast_in_dim.8.virt
  28.2 0.0 copy-done.1
  28.2 0.0 copy-done.2
  28.3 2.2 %list_maps.1 = (s32[17]{0:T(128)S(4)}, s32[3]{0:T(128)S(4)}, s32[17]{0:T(128)S(4)}, s32[17]{0:T(128)S(4)}, s32[17]{0:T(128)S(4)}, /*index=5*/f32[16,64,384]{2,1,0:T(8,128)S(1)}) custom-call(s32[1]{0:T(128)} %bitcast.me_ref, s32[128]{0:T(128)S(1)} %psum.7.lists_ref, s32[200]{0:T(256)S(1)} %copy-done.1, f32[8]{0:T(128)S(1)} %copy-done.2, ...), custom_call_target="tpu_custom_call" | custom-call | bytes 1572864 | tf_op jit(solution)/shard_map/list_maps/pallas_call | solution.py:331
  30.5 0.0 copy-done
  30.5 6.5 %sum_integrals.1 = (bf16[512,512]{1,0:T(8,128)(2,1)S(1)}, bf16[512,512]{1,0:T(8,128)(2,1)S(1)}, f32[1600,384]{1,0:T(8,128)}) custom-call(s32[1]{0:T(128)S(6)} %copy.14.count_ref, s32[2,512]{1,0:T(2,128)S(1)} %copy-done, f32[512,4096]{1,0:T(8,128)} %integrals_ref.1), custom_call_target="tpu_custom_call" | custom-call | flops 536870912 | bytes 9437184 | tf_op jit(solution)/shard_map/sum_integrals/pallas_call | solution.py:357
  37.0 0.0 collective-permute-done.2.rest_2_
  37.0 0.0 collective-permute-done.3.rest_3_
  37.0 3.4 %collective-permute-done.4.rest_4_ = f32[2,64,384]{2,1,0:T(8,128)S(1)} collective-permute-done((f32[2,64,384]{2,1,0:T(8,128)S(1)}, f32[2,64,384]{2,1,0:T(8,128)S(1)}, u32[]{:S(2)}, u32[]{:S(2)}) %collective-permute-start.4) | collective-permute-done | bytes 196640 | tf_op jit(solution)/shard_map/ppermute | solution.py:306
  40.4 0.0 collective-permute-done.5.rest_5_
  40.4 5.0 %collective-permute-done.6.rest_6_ = f32[2,64,384]{2,1,0:T(8,128)S(1)} collective-permute-done((f32[2,64,384]{2,1,0:T(8,128)S(1)}, f32[2,64,384]{2,1,0:T(8,128)S(1)}, u32[]{:S(2)}, u32[]{:S(2)}) %collective-permute-start.6) | collective-permute-done | bytes 196640 | tf_op jit(solution)/shard_map/ppermute | solution.py:306
  45.4 2.3 %multiply_tiles.1 = (f32[2,64,384]{2,1,0:T(8,128)S(1)}, f32[2,64,384]{2,1,0:T(8,128)S(1)}, f32[2,64,384]{2,1,0:T(8,128)S(1)}, f32[2,64,384]{2,1,0:T(8,128)S(1)},...) custom-call(s32[17]{0:T(128)S(4)} %get-tuple-element.31.amp_from, ...), custom_call_target="tpu_custom_call" | custom-call | flops 603979776 | bytes 2621440 | tf_op jit(solution)/shard_map/multiply_tiles/pallas_call | solution.py:384
  47.7 1.2 %collective-permute-start.7 = (f32[2,64,384]{2,1,0:T(8,128)S(1)}, f32[2,64,384]{2,1,0:T(8,128)S(1)}, u32[]{:S(2)}, u32[]{:S(2)}) collective-permute-start(f32[2,64,384]{2,1,0:T(8,128)S(1)} %get-tuple-element.43), channel_id=1, source_target_pairs={{0,12},{2,14},{4,8},{6,10},{8,4},{10,6},{12,0},{14,2},{1,13},{3,15... | collective-permute-start | bytes 589832 | tf_op jit(solution)/shard_map/ppermute | solution.py:306
  48.9 0.1 collective-permute-start.8
  49.0 2.3 %collective-permute-start.9 = (f32[2,64,384]{2,1,0:T(8,128)S(1)}, f32[2,64,384]{2,1,0:T(8,128)S(1)}, u32[]{:S(2)}, u32[]{:S(2)}) collective-permute-start(f32[2,64,384]{2,1,0:T(8,128)S(1)} %get-tuple-element.45), channel_id=1, source_target_pairs={{0,8},{2,10},{4,12},{6,14},{8,0},{10,2},{12,4},{14,6},{1,9},{3,11}... | collective-permute-start | bytes 589832 | tf_op jit(solution)/shard_map/ppermute | solution.py:306
  51.3 0.3 collective-permute-start.10
  51.5 3.2 %collective-permute-start.11 = (f32[2,64,384]{2,1,0:T(8,128)S(1)}, f32[2,64,384]{2,1,0:T(8,128)S(1)}, u32[]{:S(2)}, u32[]{:S(2)}) collective-permute-start(f32[2,64,384]{2,1,0:T(8,128)S(1)} %get-tuple-element.47), channel_id=1, source_target_pairs={{0,10},{2,8},{4,14},{6,12},{8,2},{10,0},{12,6},{14,4},{1,11},{3,9}... | collective-permute-start | bytes 589832 | tf_op jit(solution)/shard_map/ppermute | solution.py:306
  54.8 5.1 %collective-permute-done.7.rest_1_ = f32[2,64,384]{2,1,0:T(8,128)S(1)} collective-permute-done((f32[2,64,384]{2,1,0:T(8,128)S(1)}, f32[2,64,384]{2,1,0:T(8,128)S(1)}, u32[]{:S(2)}, u32[]{:S(2)}) %collective-permute-start.7) | collective-permute-done | bytes 196640 | tf_op jit(solution)/shard_map/ppermute | solution.py:306
  59.9 0.7 collective-permute-start.12
  60.5 0.0 collective-permute-done.8.rest_2_
  60.5 1.9 %collective-permute-start.13 = (f32[2,64,384]{2,1,0:T(8,128)S(1)}, f32[2,64,384]{2,1,0:T(8,128)S(1)}, u32[]{:S(2)}, u32[]{:S(2)}) collective-permute-start(f32[2,64,384]{2,1,0:T(8,128)S(1)} %get-tuple-element.49), channel_id=1, source_target_pairs={{0,14},{2,12},{4,10},{6,8},{8,6},{10,4},{12,2},{14,0},{1,15},{3,13... | collective-permute-start | bytes 589832 | tf_op jit(solution)/shard_map/ppermute | solution.py:306
  62.4 10.5 %collective-permute-done.9.rest_3_ = f32[2,64,384]{2,1,0:T(8,128)S(1)} collective-permute-done((f32[2,64,384]{2,1,0:T(8,128)S(1)}, f32[2,64,384]{2,1,0:T(8,128)S(1)}, u32[]{:S(2)}, u32[]{:S(2)}) %collective-permute-start.9) | collective-permute-done | bytes 196640 | tf_op jit(solution)/shard_map/ppermute | solution.py:306
  73.0 0.0 collective-permute-done.10.rest_4_
  73.0 3.7 %collective-permute-done.11.rest_5_ = f32[2,64,384]{2,1,0:T(8,128)S(1)} collective-permute-done((f32[2,64,384]{2,1,0:T(8,128)S(1)}, f32[2,64,384]{2,1,0:T(8,128)S(1)}, u32[]{:S(2)}, u32[]{:S(2)}) %collective-permute-start.11) | collective-permute-done | bytes 196640 | tf_op jit(solution)/shard_map/ppermute | solution.py:306
  76.7 0.0 collective-permute-done.12.rest_6_
  76.7 3.9 %collective-permute-done.13.rest_7_ = f32[2,64,384]{2,1,0:T(8,128)S(1)} collective-permute-done((f32[2,64,384]{2,1,0:T(8,128)S(1)}, f32[2,64,384]{2,1,0:T(8,128)S(1)}, u32[]{:S(2)}, u32[]{:S(2)}) %collective-permute-start.13) | collective-permute-done | bytes 196640 | tf_op jit(solution)/shard_map/ppermute | solution.py:306
  80.6 1.3 %finish_tiles.1 = f32[25,64,384]{2,1,0:T(8,128)} custom-call(s32[17]{0:T(128)S(4)} %get-tuple-element.28.res_from, s32[17]{0:T(128)S(4)} %get-tuple-element.29.res_first, f32[16,64,384]{2,1,0:T(8,128)S(1)} %get-tuple-element.30.inverse, f32[2,64,384]{2,1,0:T(8,128)S(1)} %get-tuple-element.42.rest_0_, ...), custom_call_target="tpu_custom_call", output_to_operand_aliasing={{}: (11, {})} | custom-call | bytes 2457600 | tf_op jit(solution)/shard_map/finish_tiles/pallas_call | solution.py:401
  (1 shorter events, 0.0 us)
Async XLA Ops:
  11.2 16.6 %copy-start.4 = (f32[384]{0:T(512)S(1)}, f32[384]{0:T(512)}, u32[]{:S(2)}) copy-start(f32[384]{0:T(512)} %param.19) | copy-start | bytes 4612
  11.2 16.6 %copy-start.3 = (f32[1600]{0:T(1024)S(1)}, f32[1600]{0:T(1024)}, u32[]{:S(2)}) copy-start(f32[1600]{0:T(1024)} %param.20) | copy-start | bytes 19204
  11.2 17.0 %copy-start.1 = (s32[200]{0:T(256)S(1)}, s32[200]{0:T(256)}, u32[]{:S(2)}) copy-start(s32[200]{0:T(256)} %res_slot_ref.1) | copy-start | bytes 2404
  11.2 17.0 %copy-start.2 = (f32[8]{0:T(128)S(1)}, f32[8]{0:T(128)}, u32[]{:S(2)}) copy-start(f32[8]{0:T(128)} %window.1) | copy-start | bytes 100
  11.9 18.6 %copy-start = (s32[2,512]{1,0:T(2,128)S(1)}, s32[2,512]{1,0:T(2,128)}, u32[]{:S(2)}) copy-start(s32[2,512]{1,0:T(2,128)} %tasks_ref.1) | copy-start | bytes 12292
  11.9 12.2 %collective-permute-start = (f32[2,64,384]{2,1,0:T(8,128)S(1)}, f32[2,64,384]{2,1,0:T(8,128)S(1)}, u32[]{:S(2)}, u32[]{:S(2)}) collective-permute-start(f32[2,64,384]{2,1,0:T(8,128)S(1)} %pack_tiles.2), channel_id=1, source_target_pairs={{0,12},{2,14},{4,8},{6,10},{8,4},{10,6},{12,0},{14,2},{1,13},{3,15... | collective-permute-start | bytes 589832 | tf_op jit(solution)/shard_map/ppermute | solution.py:306
  14.3 12.0 %collective-permute-start.1 = (f32[2,64,384]{2,1,0:T(8,128)S(1)}, f32[2,64,384]{2,1,0:T(8,128)S(1)}, u32[]{:S(2)}, u32[]{:S(2)}) collective-permute-start(f32[2,64,384]{2,1,0:T(8,128)S(1)} %get-tuple-element.36), channel_id=1, source_target_pairs={{0,4},{2,6},{4,0},{6,2},{8,12},{10,14},{12,8},{14,10},{1,5},{3,7},... | collective-permute-start | bytes 589832 | tf_op jit(solution)/shard_map/ppermute | solution.py:306
  15.7 21.3 %collective-permute-start.2 = (f32[2,64,384]{2,1,0:T(8,128)S(1)}, f32[2,64,384]{2,1,0:T(8,128)S(1)}, u32[]{:S(2)}, u32[]{:S(2)}) collective-permute-start(f32[2,64,384]{2,1,0:T(8,128)S(1)} %get-tuple-element.37), channel_id=1, source_target_pairs={{0,8},{2,10},{4,12},{6,14},{8,0},{10,2},{12,4},{14,6},{1,9},{3,11}... | collective-permute-start | bytes 589832 | tf_op jit(solution)/shard_map/ppermute | solution.py:306
  17.9 19.1 %collective-permute-start.3 = (f32[2,64,384]{2,1,0:T(8,128)S(1)}, f32[2,64,384]{2,1,0:T(8,128)S(1)}, u32[]{:S(2)}, u32[]{:S(2)}) collective-permute-start(f32[2,64,384]{2,1,0:T(8,128)S(1)} %get-tuple-element.38), channel_id=1, source_target_pairs={{0,6},{2,4},{4,2},{6,0},{8,14},{10,12},{12,10},{14,8},{1,7},{3,5},... | collective-permute-start | bytes 589832 | tf_op jit(solution)/shard_map/ppermute | solution.py:306
  20.0 20.4 %collective-permute-start.4 = (f32[2,64,384]{2,1,0:T(8,128)S(1)}, f32[2,64,384]{2,1,0:T(8,128)S(1)}, u32[]{:S(2)}, u32[]{:S(2)}) collective-permute-start(f32[2,64,384]{2,1,0:T(8,128)S(1)} %get-tuple-element.39), channel_id=1, source_target_pairs={{0,10},{2,8},{4,14},{6,12},{8,2},{10,0},{12,6},{14,4},{1,11},{3,9}... | collective-permute-start | bytes 589832 | tf_op jit(solution)/shard_map/ppermute | solution.py:306
  24.1 16.3 %collective-permute-start.5 = (f32[2,64,384]{2,1,0:T(8,128)S(1)}, f32[2,64,384]{2,1,0:T(8,128)S(1)}, u32[]{:S(2)}, u32[]{:S(2)}) collective-permute-start(f32[2,64,384]{2,1,0:T(8,128)S(1)} %get-tuple-element.40), channel_id=1, source_target_pairs={{0,2},{2,0},{4,6},{6,4},{8,10},{10,8},{12,14},{14,12},{1,3},{3,1},... | collective-permute-start | bytes 589832 | tf_op jit(solution)/shard_map/ppermute | solution.py:306
  26.3 19.1 %collective-permute-start.6 = (f32[2,64,384]{2,1,0:T(8,128)S(1)}, f32[2,64,384]{2,1,0:T(8,128)S(1)}, u32[]{:S(2)}, u32[]{:S(2)}) collective-permute-start(f32[2,64,384]{2,1,0:T(8,128)S(1)} %get-tuple-element.41), channel_id=1, source_target_pairs={{0,14},{2,12},{4,10},{6,8},{8,6},{10,4},{12,2},{14,0},{1,15},{3,13... | collective-permute-start | bytes 589832 | tf_op jit(solution)/shard_map/ppermute | solution.py:306
  47.7 12.2 %collective-permute-start.7 = (f32[2,64,384]{2,1,0:T(8,128)S(1)}, f32[2,64,384]{2,1,0:T(8,128)S(1)}, u32[]{:S(2)}, u32[]{:S(2)}) collective-permute-start(f32[2,64,384]{2,1,0:T(8,128)S(1)} %get-tuple-element.43), channel_id=1, source_target_pairs={{0,12},{2,14},{4,8},{6,10},{8,4},{10,6},{12,0},{14,2},{1,13},{3,15... | collective-permute-start | bytes 589832 | tf_op jit(solution)/shard_map/ppermute | solution.py:306
  48.9 11.6 %collective-permute-start.8 = (f32[2,64,384]{2,1,0:T(8,128)S(1)}, f32[2,64,384]{2,1,0:T(8,128)S(1)}, u32[]{:S(2)}, u32[]{:S(2)}) collective-permute-start(f32[2,64,384]{2,1,0:T(8,128)S(1)} %get-tuple-element.44), channel_id=1, source_target_pairs={{0,4},{2,6},{4,0},{6,2},{8,12},{10,14},{12,8},{14,10},{1,5},{3,7},... | collective-permute-start | bytes 589832 | tf_op jit(solution)/shard_map/ppermute | solution.py:306
  49.0 24.0 %collective-permute-start.9 = (f32[2,64,384]{2,1,0:T(8,128)S(1)}, f32[2,64,384]{2,1,0:T(8,128)S(1)}, u32[]{:S(2)}, u32[]{:S(2)}) collective-permute-start(f32[2,64,384]{2,1,0:T(8,128)S(1)} %get-tuple-element.45), channel_id=1, source_target_pairs={{0,8},{2,10},{4,12},{6,14},{8,0},{10,2},{12,4},{14,6},{1,9},{3,11}... | collective-permute-start | bytes 589832 | tf_op jit(solution)/shard_map/ppermute | solution.py:306
  51.3 21.7 %collective-permute-start.10 = (f32[2,64,384]{2,1,0:T(8,128)S(1)}, f32[2,64,384]{2,1,0:T(8,128)S(1)}, u32[]{:S(2)}, u32[]{:S(2)}) collective-permute-start(f32[2,64,384]{2,1,0:T(8,128)S(1)} %get-tuple-element.46), channel_id=1, source_target_pairs={{0,6},{2,4},{4,2},{6,0},{8,14},{10,12},{12,10},{14,8},{1,7},{3,5},... | collective-permute-start | bytes 589832 | tf_op jit(solution)/shard_map/ppermute | solution.py:306
  51.5 25.2 %collective-permute-start.11 = (f32[2,64,384]{2,1,0:T(8,128)S(1)}, f32[2,64,384]{2,1,0:T(8,128)S(1)}, u32[]{:S(2)}, u32[]{:S(2)}) collective-permute-start(f32[2,64,384]{2,1,0:T(8,128)S(1)} %get-tuple-element.47), channel_id=1, source_target_pairs={{0,10},{2,8},{4,14},{6,12},{8,2},{10,0},{12,6},{14,4},{1,11},{3,9}... | collective-permute-start | bytes 589832 | tf_op jit(solution)/shard_map/ppermute | solution.py:306
  59.9 16.8 %collective-permute-start.12 = (f32[2,64,384]{2,1,0:T(8,128)S(1)}, f32[2,64,384]{2,1,0:T(8,128)S(1)}, u32[]{:S(2)}, u32[]{:S(2)}) collective-permute-start(f32[2,64,384]{2,1,0:T(8,128)S(1)} %get-tuple-element.48), channel_id=1, source_target_pairs={{0,2},{2,0},{4,6},{6,4},{8,10},{10,8},{12,14},{14,12},{1,3},{3,1},... | collective-permute-start | bytes 589832 | tf_op jit(solution)/shard_map/ppermute | solution.py:306
  60.5 20.1 %collective-permute-start.13 = (f32[2,64,384]{2,1,0:T(8,128)S(1)}, f32[2,64,384]{2,1,0:T(8,128)S(1)}, u32[]{:S(2)}, u32[]{:S(2)}) collective-permute-start(f32[2,64,384]{2,1,0:T(8,128)S(1)} %get-tuple-element.49), channel_id=1, source_target_pairs={{0,14},{2,12},{4,10},{6,8},{8,6},{10,4},{12,2},{14,0},{1,15},{3,13... | collective-permute-start | bytes 589832 | tf_op jit(solution)/shard_map/ppermute | solution.py:306

commit v9 on v8

--- a/solution.py
+++ b/solution.py
@@ -87,7 +87,7 @@
 
 def maps_kernel(
     owners, per_amp, per_res, me_ref, lists_ref, res_slot_ref,
-    window, pair, virt, amp_from, amp_self, res_to, res_from, res_first, inverse, res_tile, seen, taken,
+    window, pair, virt, amp_from, amp_self, res_to, res_from, res_first, res_last, inverse, res_tile, seen, taken,
 ):
     list_length = lists_ref.shape[0] // owners // 2
     spots = owners * CAP
@@ -142,6 +142,14 @@
             first = jnp.where(local < 0, -1, jnp.where(taken[at] < 0, spot, taken[at]))
             taken[at] = first
             res_first[spot] = first
+
+    clear(taken, per_res + 1, -1)
+    for d in reversed([0] + class_order(owners)):
+        for spot in reversed(range(d * CAP, d * CAP + CAP)):
+            local = res_from[spot]
+            at = jnp.where(local >= 0, local, per_res)
+            res_last[spot] = jnp.where((local >= 0) & (taken[at] < 0), 1, 0)
+            taken[at] = jnp.where(local >= 0, spot, -1)
 
     tiles, columns = virt.shape[0], pair.shape[1]
 
@@ -240,9 +248,14 @@
                     outs[d][k, :, c * 128 : (c + 1) * 128] = totals[c, pl.ds(g, TW, stride=rows // TW), :]
 
 
-def final_kernel(owners, res_from, res_first, inverse, *rest):
+def final_kernel(owners, res_from, res_first, res_last, inverse, *rest):
     arrived, (_, out, sums, sems) = rest[:owners], rest[-4:]
     spots = [(at, k, d * CAP + k) for at, d in enumerate([0] + class_order(owners)) for k in range(CAP)]
+
+    def write(spot):
+        source = sums.at[jnp.maximum(res_first[spot], 0)]
+        return pltpu.make_async_copy(source, out.at[jnp.maximum(res_from[spot], 0)], sems.at[spot])
+
     for at, k, spot in spots:
         first = res_first[spot]
 
@@ -254,13 +267,9 @@
         def _():
             sums[first] = sums[first] + arrived[at][k] * inverse[spot]
 
-    def write(spot):
-        return pltpu.make_async_copy(sums.at[spot], out.at[jnp.maximum(res_from[spot], 0)], sems.at[spot])
-
+        pl.when(res_last[spot] == 1)(write(spot).start)
     for _, _, spot in spots:
-        pl.when(res_first[spot] == spot)(write(spot).start)
-    for _, _, spot in spots:
-        pl.when(res_first[spot] == spot)(write(spot).wait)
+        pl.when(res_last[spot] == 1)(write(spot).wait)
 
 
 def local(
@@ -309,7 +318,7 @@
 
     piece = pltpu.VMEM((CAP, TW, row_count), F32)
     fetched = []
-    for classes in order[:1], order[1:]:
+    for classes in order[:2], order[2:]:
         packed = pl.pallas_call(
             functools.partial(pack_kernel, classes, list_length, per_amp),
             out_shape=[piece] * len(classes),
@@ -330,10 +339,10 @@
     small = pltpu.SMEM((owners * CAP + 1,), jnp.int32)
     *maps, inverse = pl.pallas_call(
         functools.partial(maps_kernel, owners, per_amp, per_res),
-        out_shape=[small, pltpu.SMEM((CAP + 1,), jnp.int32), small, small, small]
+        out_shape=[small, pltpu.SMEM((CAP + 1,), jnp.int32), small, small, small, small]
         + [pltpu.VMEM((owners * CAP, TW, row_count), F32)],
         in_specs=[SMEM_SPEC] * 4 + [VMEM_SPEC] * 2,
-        out_specs=[SMEM_SPEC] * 5 + [VMEM_SPEC],
+        out_specs=[SMEM_SPEC] * 6 + [VMEM_SPEC],
         scratch_shapes=[
             pltpu.SMEM((owners * CAP + 1,), jnp.int32),
             pltpu.SMEM((owners,), jnp.int32),
@@ -343,7 +352,7 @@
         cost_estimate=cost(0, owners * CAP * TW * row_count * 4),
         name="list_maps",
     )(me_ref, lists, res_slot, window_energy, pair, virt)
-    amp_from, amp_self, res_to, res_from, res_first = (
+    amp_from, amp_self, res_to, res_from, res_first, res_last = (
         pltpu.with_memory_space_constraint(x, pltpu.SMEM) for x in maps
     )
     inverse = in_vmem(inverse)
@@ -401,17 +410,17 @@
     return pl.pallas_call(
         functools.partial(final_kernel, owners),
         out_shape=jax.ShapeDtypeStruct((per_res, TW, row_count), F32),
-        in_specs=[SMEM_SPEC] * 2 + [VMEM_SPEC] * (1 + owners) + [HBM_SPEC],
+        in_specs=[SMEM_SPEC] * 3 + [VMEM_SPEC] * (1 + owners) + [HBM_SPEC],
         out_specs=HBM_SPEC,
         scratch_shapes=[
             pltpu.VMEM((owners * CAP, TW, row_count), F32),
             pltpu.SemaphoreType.DMA((owners * CAP,)),
         ],
-        input_output_aliases={3 + owners: 0},
+        input_output_aliases={4 + owners: 0},
         compiler_params=params(),
         cost_estimate=cost(0, per_res * TW * row_count * 4),
         name="finish_tiles",
-    )(res_from, res_first, inverse, *returned, blank)
+    )(res_from, res_first, res_last, inverse, *returned, blank)
 
 
 def solution(mesh):

time: 83.4 us -> 83.8 us (level)
  waiting for transfers between devices: 36.8 us -> 38.2 us
    ppermute x14, waiting for transfers between devices: 36.8 us -> 38.2 us  [exchange(): lax.ppermute(buffer, 'tile', [(i, i ^ d) for i in range(owners)])]
  transfers between devices with their start and end apart: 14 -> 14, of which waited for: 8 -> 7; matrix products, arithmetic and copies ran while one was open for 0% -> 0% of each run, Pallas kernels for 13% -> 13%
where the time goes in v9:
time: 83.8 us; the launch traced here: 82.7 us
  waiting for transfers between devices  38.2 us (46%)
  starting transfers between devices  17.3 us (21%)
  Pallas kernels  15.5 us (18%)
  blocking collectives  10.5 us (13%)
    ppermute x14, waiting for transfers between devices, exchange(): lax.ppermute(buffer, 'tile', [(i, i ^ d) for i in range(owners)])  38.2 us
    ppermute x14, starting transfers between devices, exchange(): lax.ppermute(buffer, 'tile', [(i, i ^ d) for i in range(owners)])  17.3 us
    psum x1, blocking collectives, local(): lists = lax.psum(spread, 'tile').reshape(-1)  10.5 us
    pallas_call x1, Pallas kernels, local(): pl.pallas_call(functools.partial(sum_kernel, list_length), grid=(steps,),...  6.49 us
    pallas_call x1, Pallas kernels, local(): pl.pallas_call(functools.partial(maps_kernel, owners, per_amp, per_res),...  2.54 us
    pallas_call x2, Pallas kernels, local(): pl.pallas_call(functools.partial(pack_kernel, classes, list_length, per_a...  2.37 us
    pallas_call x1, Pallas kernels, local(): pl.pallas_call(functools.partial(product_kernel, owners), out_shape=[piec...  2.3 us
  transfers between devices with their start and end apart: 14, of which 7 were waited for; matrix products, arithmetic and copies ran while one was open for 0% of the time, Pallas kernels for 13%

profile of v9, /device:TPU:12, one launch (start us, length us, event | category | flops | bytes accessed | tf_op | source)
XLA Modules:
  0.0 82.7 jit_solution(9642506391148506880)
XLA Ops:
  0.0 0.7 spread_lists.1
  0.7 10.5 %psum.7.lists_ref = s32[128]{0:T(128)S(1)} all-reduce(s32[128]{0:T(128)S(1)} %bitcast.3), channel_id=1, replica_groups=mesh['mol'=2,'tile'=8,'rep'=2] {'tile'}, use_global_device_ids=true, to_apply=%region_0.0 | all-reduce | flops 128 | bytes 1024 | tf_op jit(solution)/shard_map/psum | solution.py:310
  11.2 0.0 copy-start.4
  11.2 0.0 copy-start.3
  11.2 0.0 copy-start.1
  11.2 0.0 copy-start.2
  11.3 0.7 pack_tiles.2
  11.9 0.0 copy-start
  12.0 1.4 %collective-permute-start = (f32[2,64,384]{2,1,0:T(8,128)S(1)}, f32[2,64,384]{2,1,0:T(8,128)S(1)}, u32[]{:S(2)}, u32[]{:S(2)}) collective-permute-start(f32[2,64,384]{2,1,0:T(8,128)S(1)} %get-tuple-element.39), channel_id=1, source_target_pairs={{0,12},{2,14},{4,8},{6,10},{8,4},{10,6},{12,0},{14,2},{1,13},{3,15... | collective-permute-start | bytes 589832 | tf_op jit(solution)/shard_map/ppermute | solution.py:315
  13.4 1.3 %collective-permute-start.1 = (f32[2,64,384]{2,1,0:T(8,128)S(1)}, f32[2,64,384]{2,1,0:T(8,128)S(1)}, u32[]{:S(2)}, u32[]{:S(2)}) collective-permute-start(f32[2,64,384]{2,1,0:T(8,128)S(1)} %get-tuple-element.40), channel_id=1, source_target_pairs={{0,4},{2,6},{4,0},{6,2},{8,12},{10,14},{12,8},{14,10},{1,5},{3,7},... | collective-permute-start | bytes 589832 | tf_op jit(solution)/shard_map/ppermute | solution.py:315
  14.7 1.7 %pack_tiles.3 = (f32[2,64,384]{2,1,0:T(8,128)S(1)}, f32[2,64,384]{2,1,0:T(8,128)S(1)}, f32[2,64,384]{2,1,0:T(8,128)S(1)}, f32[2,64,384]{2,1,0:T(8,128)S(1)}, f32[2,64,384]{2,1,0:T(8,128)S(1)}) custom-call(s32[1]{0:T(128)} %bitcast.me_ref, s32[128]{0:T(128)S(1)} %psum.7.lists_ref, f32[25,64,384]{2,1,0:T(8,128)} %amplitudes.5), custom_call_target="tpu_custom_call" | custom-call | bytes 983040 | tf_op jit(solution)/shard_map/pack_tiles/pallas_call | solution.py:322
  16.4 2.5 %collective-permute-start.2 = (f32[2,64,384]{2,1,0:T(8,128)S(1)}, f32[2,64,384]{2,1,0:T(8,128)S(1)}, u32[]{:S(2)}, u32[]{:S(2)}) collective-permute-start(f32[2,64,384]{2,1,0:T(8,128)S(1)} %get-tuple-element.41), channel_id=1, source_target_pairs={{0,8},{2,10},{4,12},{6,14},{8,0},{10,2},{12,4},{14,6},{1,9},{3,11}... | collective-permute-start | bytes 589832 | tf_op jit(solution)/shard_map/ppermute | solution.py:315
  18.9 0.9 %collective-permute-start.3 = (f32[2,64,384]{2,1,0:T(8,128)S(1)}, f32[2,64,384]{2,1,0:T(8,128)S(1)}, u32[]{:S(2)}, u32[]{:S(2)}) collective-permute-start(f32[2,64,384]{2,1,0:T(8,128)S(1)} %get-tuple-element.42), channel_id=1, source_target_pairs={{0,6},{2,4},{4,2},{6,0},{8,14},{10,12},{12,10},{14,8},{1,7},{3,5},... | collective-permute-start | bytes 589832 | tf_op jit(solution)/shard_map/ppermute | solution.py:315
  19.9 2.0 %collective-permute-start.4 = (f32[2,64,384]{2,1,0:T(8,128)S(1)}, f32[2,64,384]{2,1,0:T(8,128)S(1)}, u32[]{:S(2)}, u32[]{:S(2)}) collective-permute-start(f32[2,64,384]{2,1,0:T(8,128)S(1)} %get-tuple-element.43), channel_id=1, source_target_pairs={{0,10},{2,8},{4,14},{6,12},{8,2},{10,0},{12,6},{14,4},{1,11},{3,9}... | collective-permute-start | bytes 589832 | tf_op jit(solution)/shard_map/ppermute | solution.py:315
  21.8 3.0 %collective-permute-done.rest_0_ = f32[2,64,384]{2,1,0:T(8,128)S(1)} collective-permute-done((f32[2,64,384]{2,1,0:T(8,128)S(1)}, f32[2,64,384]{2,1,0:T(8,128)S(1)}, u32[]{:S(2)}, u32[]{:S(2)}) %collective-permute-start) | collective-permute-done | bytes 196640 | tf_op jit(solution)/shard_map/ppermute | solution.py:315
  24.9 0.6 collective-permute-start.5
  25.5 0.0 collective-permute-done.1.rest_1_
  25.5 1.0 %collective-permute-start.6 = (f32[2,64,384]{2,1,0:T(8,128)S(1)}, f32[2,64,384]{2,1,0:T(8,128)S(1)}, u32[]{:S(2)}, u32[]{:S(2)}) collective-permute-start(f32[2,64,384]{2,1,0:T(8,128)S(1)} %get-tuple-element.45), channel_id=1, source_target_pairs={{0,14},{2,12},{4,10},{6,8},{8,6},{10,4},{12,2},{14,0},{1,15},{3,13... | collective-permute-start | bytes 589832 | tf_op jit(solution)/shard_map/ppermute | solution.py:315
  27.2 0.0 copy-done.4
  27.2 0.0 copy-done.3
  27.2 0.1 broadcast_in_dim.7
  27.3 0.3 broadcast_in_dim.8.virt
  27.6 0.0 copy-done.1
  27.6 0.0 copy-done.2
  27.6 2.5 %list_maps.1 = (s32[17]{0:T(128)S(4)}, s32[3]{0:T(128)S(4)}, s32[17]{0:T(128)S(4)}, s32[17]{0:T(128)S(4)}, s32[17]{0:T(128)S(4)}, /*index=5*/s32[17]{0:T(128)S(4)}, f32[16,64,384]{2,1,0:T(8,128)S(1)}) custom-call(s32[1]{0:T(128)} %bitcast.me_ref, s32[128]{0:T(128)S(1)} %psum.7.lists_ref, s32[200]{0:T(256)S(1)} %copy-done.1, f32[8]{0:T(128)S(1)} %copy-done.2, ...), custom_call_target="tpu_custom_call" | custom-call | bytes 1572864 | tf_op jit(solution)/shard_map/list_maps/pallas_call | solution.py:340
  30.1 0.0 copy-done
  30.1 6.5 %sum_integrals.1 = (bf16[512,512]{1,0:T(8,128)(2,1)S(1)}, bf16[512,512]{1,0:T(8,128)(2,1)S(1)}, f32[1600,384]{1,0:T(8,128)}) custom-call(s32[1]{0:T(128)S(6)} %copy.14.count_ref, s32[2,512]{1,0:T(2,128)S(1)} %copy-done, f32[512,4096]{1,0:T(8,128)} %integrals_ref.1), custom_call_target="tpu_custom_call" | custom-call | flops 536870912 | bytes 9437184 | tf_op jit(solution)/shard_map/sum_integrals/pallas_call | solution.py:366
  36.6 0.0 collective-permute-done.2.rest_2_
  36.6 0.0 collective-permute-done.3.rest_3_
  36.6 4.6 %collective-permute-done.4.rest_4_ = f32[2,64,384]{2,1,0:T(8,128)S(1)} collective-permute-done((f32[2,64,384]{2,1,0:T(8,128)S(1)}, f32[2,64,384]{2,1,0:T(8,128)S(1)}, u32[]{:S(2)}, u32[]{:S(2)}) %collective-permute-start.4) | collective-permute-done | bytes 196640 | tf_op jit(solution)/shard_map/ppermute | solution.py:315
  41.2 0.0 collective-permute-done.5.rest_5_
  41.2 5.2 %collective-permute-done.6.rest_6_ = f32[2,64,384]{2,1,0:T(8,128)S(1)} collective-permute-done((f32[2,64,384]{2,1,0:T(8,128)S(1)}, f32[2,64,384]{2,1,0:T(8,128)S(1)}, u32[]{:S(2)}, u32[]{:S(2)}) %collective-permute-start.6) | collective-permute-done | bytes 196640 | tf_op jit(solution)/shard_map/ppermute | solution.py:315
  46.4 2.3 %multiply_tiles.1 = (f32[2,64,384]{2,1,0:T(8,128)S(1)}, f32[2,64,384]{2,1,0:T(8,128)S(1)}, f32[2,64,384]{2,1,0:T(8,128)S(1)}, f32[2,64,384]{2,1,0:T(8,128)S(1)},...) custom-call(s32[17]{0:T(128)S(4)} %get-tuple-element.34.amp_from, ...), custom_call_target="tpu_custom_call" | custom-call | flops 603979776 | bytes 2621440 | tf_op jit(solution)/shard_map/multiply_tiles/pallas_call | solution.py:393
  48.7 0.1 collective-permute-start.7
  48.8 0.1 collective-permute-start.8
  48.9 3.4 %collective-permute-start.9 = (f32[2,64,384]{2,1,0:T(8,128)S(1)}, f32[2,64,384]{2,1,0:T(8,128)S(1)}, u32[]{:S(2)}, u32[]{:S(2)}) collective-permute-start(f32[2,64,384]{2,1,0:T(8,128)S(1)} %get-tuple-element.49), channel_id=1, source_target_pairs={{0,8},{2,10},{4,12},{6,14},{8,0},{10,2},{12,4},{14,6},{1,9},{3,11}... | collective-permute-start | bytes 589832 | tf_op jit(solution)/shard_map/ppermute | solution.py:315
  52.3 0.5 collective-permute-start.10
  52.8 1.9 %collective-permute-start.11 = (f32[2,64,384]{2,1,0:T(8,128)S(1)}, f32[2,64,384]{2,1,0:T(8,128)S(1)}, u32[]{:S(2)}, u32[]{:S(2)}) collective-permute-start(f32[2,64,384]{2,1,0:T(8,128)S(1)} %get-tuple-element.51), channel_id=1, source_target_pairs={{0,10},{2,8},{4,14},{6,12},{8,2},{10,0},{12,6},{14,4},{1,11},{3,9}... | collective-permute-start | bytes 589832 | tf_op jit(solution)/shard_map/ppermute | solution.py:315
  54.7 6.2 %collective-permute-done.7.rest_1_ = f32[2,64,384]{2,1,0:T(8,128)S(1)} collective-permute-done((f32[2,64,384]{2,1,0:T(8,128)S(1)}, f32[2,64,384]{2,1,0:T(8,128)S(1)}, u32[]{:S(2)}, u32[]{:S(2)}) %collective-permute-start.7) | collective-permute-done | bytes 196640 | tf_op jit(solution)/shard_map/ppermute | solution.py:315
  60.9 1.1 %collective-permute-start.12 = (f32[2,64,384]{2,1,0:T(8,128)S(1)}, f32[2,64,384]{2,1,0:T(8,128)S(1)}, u32[]{:S(2)}, u32[]{:S(2)}) collective-permute-start(f32[2,64,384]{2,1,0:T(8,128)S(1)} %get-tuple-element.52), channel_id=1, source_target_pairs={{0,2},{2,0},{4,6},{6,4},{8,10},{10,8},{12,14},{14,12},{1,3},{3,1},... | collective-permute-start | bytes 589832 | tf_op jit(solution)/shard_map/ppermute | solution.py:315
  62.0 0.0 collective-permute-done.8.rest_2_
  62.0 0.4 collective-permute-start.13
  62.4 10.1 %collective-permute-done.9.rest_3_ = f32[2,64,384]{2,1,0:T(8,128)S(1)} collective-permute-done((f32[2,64,384]{2,1,0:T(8,128)S(1)}, f32[2,64,384]{2,1,0:T(8,128)S(1)}, u32[]{:S(2)}, u32[]{:S(2)}) %collective-permute-start.9) | collective-permute-done | bytes 196640 | tf_op jit(solution)/shard_map/ppermute | solution.py:315
  72.4 0.0 collective-permute-done.10.rest_4_
  72.5 4.4 %collective-permute-done.11.rest_5_ = f32[2,64,384]{2,1,0:T(8,128)S(1)} collective-permute-done((f32[2,64,384]{2,1,0:T(8,128)S(1)}, f32[2,64,384]{2,1,0:T(8,128)S(1)}, u32[]{:S(2)}, u32[]{:S(2)}) %collective-permute-start.11) | collective-permute-done | bytes 196640 | tf_op jit(solution)/shard_map/ppermute | solution.py:315
  76.8 0.0 collective-permute-done.12.rest_6_
  76.8 4.8 %collective-permute-done.13.rest_7_ = f32[2,64,384]{2,1,0:T(8,128)S(1)} collective-permute-done((f32[2,64,384]{2,1,0:T(8,128)S(1)}, f32[2,64,384]{2,1,0:T(8,128)S(1)}, u32[]{:S(2)}, u32[]{:S(2)}) %collective-permute-start.13) | collective-permute-done | bytes 196640 | tf_op jit(solution)/shard_map/ppermute | solution.py:315
  81.6 1.1 %finish_tiles.1 = f32[25,64,384]{2,1,0:T(8,128)} custom-call(s32[17]{0:T(128)S(4)} %get-tuple-element.30.res_from, s32[17]{0:T(128)S(4)} %get-tuple-element.31.res_first, s32[17]{0:T(128)S(4)} %get-tuple-element.32.res_last, f32[16,64,384]{2,1,0:T(8,128)S(1)} %get-tuple-element.33.inverse, ...), custom_call_target="tpu_custom_call", output_to_operand_aliasing={{}: (12, {})} | custom-call | bytes 2457600 | tf_op jit(solution)/shard_map/finish_tiles/pallas_call | solution.py:410
  (1 shorter events, 0.0 us)
Async XLA Ops:
  11.2 16.0 %copy-start.4 = (f32[384]{0:T(512)S(1)}, f32[384]{0:T(512)}, u32[]{:S(2)}) copy-start(f32[384]{0:T(512)} %param.19) | copy-start | bytes 4612
  11.2 16.0 %copy-start.3 = (f32[1600]{0:T(1024)S(1)}, f32[1600]{0:T(1024)}, u32[]{:S(2)}) copy-start(f32[1600]{0:T(1024)} %param.20) | copy-start | bytes 19204
  11.2 16.3 %copy-start.1 = (s32[200]{0:T(256)S(1)}, s32[200]{0:T(256)}, u32[]{:S(2)}) copy-start(s32[200]{0:T(256)} %res_slot_ref.1) | copy-start | bytes 2404
  11.2 16.3 %copy-start.2 = (f32[8]{0:T(128)S(1)}, f32[8]{0:T(128)}, u32[]{:S(2)}) copy-start(f32[8]{0:T(128)} %window.1) | copy-start | bytes 100
  11.9 18.2 %copy-start = (s32[2,512]{1,0:T(2,128)S(1)}, s32[2,512]{1,0:T(2,128)}, u32[]{:S(2)}) copy-start(s32[2,512]{1,0:T(2,128)} %tasks_ref.1) | copy-start | bytes 12292
  12.0 12.9 %collective-permute-start = (f32[2,64,384]{2,1,0:T(8,128)S(1)}, f32[2,64,384]{2,1,0:T(8,128)S(1)}, u32[]{:S(2)}, u32[]{:S(2)}) collective-permute-start(f32[2,64,384]{2,1,0:T(8,128)S(1)} %get-tuple-element.39), channel_id=1, source_target_pairs={{0,12},{2,14},{4,8},{6,10},{8,4},{10,6},{12,0},{14,2},{1,13},{3,15... | collective-permute-start | bytes 589832 | tf_op jit(solution)/shard_map/ppermute | solution.py:315
  13.4 12.1 %collective-permute-start.1 = (f32[2,64,384]{2,1,0:T(8,128)S(1)}, f32[2,64,384]{2,1,0:T(8,128)S(1)}, u32[]{:S(2)}, u32[]{:S(2)}) collective-permute-start(f32[2,64,384]{2,1,0:T(8,128)S(1)} %get-tuple-element.40), channel_id=1, source_target_pairs={{0,4},{2,6},{4,0},{6,2},{8,12},{10,14},{12,8},{14,10},{1,5},{3,7},... | collective-permute-start | bytes 589832 | tf_op jit(solution)/shard_map/ppermute | solution.py:315
  16.4 20.2 %collective-permute-start.2 = (f32[2,64,384]{2,1,0:T(8,128)S(1)}, f32[2,64,384]{2,1,0:T(8,128)S(1)}, u32[]{:S(2)}, u32[]{:S(2)}) collective-permute-start(f32[2,64,384]{2,1,0:T(8,128)S(1)} %get-tuple-element.41), channel_id=1, source_target_pairs={{0,8},{2,10},{4,12},{6,14},{8,0},{10,2},{12,4},{14,6},{1,9},{3,11}... | collective-permute-start | bytes 589832 | tf_op jit(solution)/shard_map/ppermute | solution.py:315
  18.9 17.7 %collective-permute-start.3 = (f32[2,64,384]{2,1,0:T(8,128)S(1)}, f32[2,64,384]{2,1,0:T(8,128)S(1)}, u32[]{:S(2)}, u32[]{:S(2)}) collective-permute-start(f32[2,64,384]{2,1,0:T(8,128)S(1)} %get-tuple-element.42), channel_id=1, source_target_pairs={{0,6},{2,4},{4,2},{6,0},{8,14},{10,12},{12,10},{14,8},{1,7},{3,5},... | collective-permute-start | bytes 589832 | tf_op jit(solution)/shard_map/ppermute | solution.py:315
  19.9 21.3 %collective-permute-start.4 = (f32[2,64,384]{2,1,0:T(8,128)S(1)}, f32[2,64,384]{2,1,0:T(8,128)S(1)}, u32[]{:S(2)}, u32[]{:S(2)}) collective-permute-start(f32[2,64,384]{2,1,0:T(8,128)S(1)} %get-tuple-element.43), channel_id=1, source_target_pairs={{0,10},{2,8},{4,14},{6,12},{8,2},{10,0},{12,6},{14,4},{1,11},{3,9}... | collective-permute-start | bytes 589832 | tf_op jit(solution)/shard_map/ppermute | solution.py:315
  24.9 16.3 %collective-permute-start.5 = (f32[2,64,384]{2,1,0:T(8,128)S(1)}, f32[2,64,384]{2,1,0:T(8,128)S(1)}, u32[]{:S(2)}, u32[]{:S(2)}) collective-permute-start(f32[2,64,384]{2,1,0:T(8,128)S(1)} %get-tuple-element.44), channel_id=1, source_target_pairs={{0,2},{2,0},{4,6},{6,4},{8,10},{10,8},{12,14},{14,12},{1,3},{3,1},... | collective-permute-start | bytes 589832 | tf_op jit(solution)/shard_map/ppermute | solution.py:315
  25.5 20.9 %collective-permute-start.6 = (f32[2,64,384]{2,1,0:T(8,128)S(1)}, f32[2,64,384]{2,1,0:T(8,128)S(1)}, u32[]{:S(2)}, u32[]{:S(2)}) collective-permute-start(f32[2,64,384]{2,1,0:T(8,128)S(1)} %get-tuple-element.45), channel_id=1, source_target_pairs={{0,14},{2,12},{4,10},{6,8},{8,6},{10,4},{12,2},{14,0},{1,15},{3,13... | collective-permute-start | bytes 589832 | tf_op jit(solution)/shard_map/ppermute | solution.py:315
  48.7 12.2 %collective-permute-start.7 = (f32[2,64,384]{2,1,0:T(8,128)S(1)}, f32[2,64,384]{2,1,0:T(8,128)S(1)}, u32[]{:S(2)}, u32[]{:S(2)}) collective-permute-start(f32[2,64,384]{2,1,0:T(8,128)S(1)} %get-tuple-element.47), channel_id=1, source_target_pairs={{0,12},{2,14},{4,8},{6,10},{8,4},{10,6},{12,0},{14,2},{1,13},{3,15... | collective-permute-start | bytes 589832 | tf_op jit(solution)/shard_map/ppermute | solution.py:315
  48.8 13.2 %collective-permute-start.8 = (f32[2,64,384]{2,1,0:T(8,128)S(1)}, f32[2,64,384]{2,1,0:T(8,128)S(1)}, u32[]{:S(2)}, u32[]{:S(2)}) collective-permute-start(f32[2,64,384]{2,1,0:T(8,128)S(1)} %get-tuple-element.48), channel_id=1, source_target_pairs={{0,4},{2,6},{4,0},{6,2},{8,12},{10,14},{12,8},{14,10},{1,5},{3,7},... | collective-permute-start | bytes 589832 | tf_op jit(solution)/shard_map/ppermute | solution.py:315
  48.9 23.6 %collective-permute-start.9 = (f32[2,64,384]{2,1,0:T(8,128)S(1)}, f32[2,64,384]{2,1,0:T(8,128)S(1)}, u32[]{:S(2)}, u32[]{:S(2)}) collective-permute-start(f32[2,64,384]{2,1,0:T(8,128)S(1)} %get-tuple-element.49), channel_id=1, source_target_pairs={{0,8},{2,10},{4,12},{6,14},{8,0},{10,2},{12,4},{14,6},{1,9},{3,11}... | collective-permute-start | bytes 589832 | tf_op jit(solution)/shard_map/ppermute | solution.py:315
  52.3 20.2 %collective-permute-start.10 = (f32[2,64,384]{2,1,0:T(8,128)S(1)}, f32[2,64,384]{2,1,0:T(8,128)S(1)}, u32[]{:S(2)}, u32[]{:S(2)}) collective-permute-start(f32[2,64,384]{2,1,0:T(8,128)S(1)} %get-tuple-element.50), channel_id=1, source_target_pairs={{0,6},{2,4},{4,2},{6,0},{8,14},{10,12},{12,10},{14,8},{1,7},{3,5},... | collective-permute-start | bytes 589832 | tf_op jit(solution)/shard_map/ppermute | solution.py:315
  52.8 24.0 %collective-permute-start.11 = (f32[2,64,384]{2,1,0:T(8,128)S(1)}, f32[2,64,384]{2,1,0:T(8,128)S(1)}, u32[]{:S(2)}, u32[]{:S(2)}) collective-permute-start(f32[2,64,384]{2,1,0:T(8,128)S(1)} %get-tuple-element.51), channel_id=1, source_target_pairs={{0,10},{2,8},{4,14},{6,12},{8,2},{10,0},{12,6},{14,4},{1,11},{3,9}... | collective-permute-start | bytes 589832 | tf_op jit(solution)/shard_map/ppermute | solution.py:315
  60.9 15.9 %collective-permute-start.12 = (f32[2,64,384]{2,1,0:T(8,128)S(1)}, f32[2,64,384]{2,1,0:T(8,128)S(1)}, u32[]{:S(2)}, u32[]{:S(2)}) collective-permute-start(f32[2,64,384]{2,1,0:T(8,128)S(1)} %get-tuple-element.52), channel_id=1, source_target_pairs={{0,2},{2,0},{4,6},{6,4},{8,10},{10,8},{12,14},{14,12},{1,3},{3,1},... | collective-permute-start | bytes 589832 | tf_op jit(solution)/shard_map/ppermute | solution.py:315
  62.0 19.6 %collective-permute-start.13 = (f32[2,64,384]{2,1,0:T(8,128)S(1)}, f32[2,64,384]{2,1,0:T(8,128)S(1)}, u32[]{:S(2)}, u32[]{:S(2)}) collective-permute-start(f32[2,64,384]{2,1,0:T(8,128)S(1)} %get-tuple-element.53), channel_id=1, source_target_pairs={{0,14},{2,12},{4,10},{6,8},{8,6},{10,4},{12,2},{14,0},{1,15},{3,13... | collective-permute-start | bytes 589832 | tf_op jit(solution)/shard_map/ppermute | solution.py:315
